TPU v7x, 32 devices: a whole 2x2x4 slice. The times are simulated.
32 devices in a mesh: dp: 8 (over z, y), fsdp: 4 (over x, core).
Axes of the slice: x: 2, y: 2, z: 4, core: 2. Of those that a mesh axis runs over, the one named last changes fastest.
Arguments:
- hidden_in: bfloat16 [4096, 14336], P(('dp', 'fsdp')), may hold values from -6 to 6
- out_grads: bfloat16 [4096, 4096], P(('dp', 'fsdp')), may hold values from -6 to 6
- piece_of: int32 [32, 128], P(('dp', 'fsdp')), may hold values from 0 to 7, never falling along the last dimension, each value on 1 to 32 neighbouring positions
- owner_dp: int32 [32, 8], P(('dp', 'fsdp')), may hold values from 0 to 7, as said below
- owner_slot: int32 [32, 8], P(('dp', 'fsdp')), may hold values from 0 to 3
- sketch_in: bfloat16 [14336, 64], P('fsdp'), may hold values from -0.046875 to 0.046875
- sketch_out: bfloat16 [4096, 64], P('fsdp'), may hold values from -0.09375 to 0.09375
Outputs:
- gram: float32 [192, 4096], P('dp', 'fsdp')
Inputs may be any that keep to these rules, and one draw needn't show every extreme that they name: `owner_dp`: each device sends exactly 2 pieces to each of 4 cyclically consecutive dp indices and none to the others; the first of these dp indices is the sender's dp index plus an offset that is the same for all devices that share an fsdp index, modulo 8.
All inputs are finite; a program needn't handle non-finite values.
Results may differ from a plain program's by a relative error of at most 0.0036.
Values may be sent and summed in bfloat16 or wider, within the bound.
No kernel may reach another device: no remote copies, remote signals or barrier semaphores. Data moves between devices by JAX's collectives and lax.ppermute only.
A program may use at most 64 MiB of HBM per device.

v0:
```python
import math

import jax
import jax.numpy as jnp
from jax import lax
from jax.sharding import PartitionSpec as P

CAP = 2
GR = 192


def on_device(hidden_in, out_grads, piece_of, owner_dp, owner_slot, sketch_in, sketch_out):
    count_dp = lax.axis_size("dp")
    count_fsdp = lax.axis_size("fsdp")
    full_in, full_out = (
        lax.all_gather(sketch_in, "fsdp", axis=0, tiled=True),
        lax.all_gather(sketch_out, "fsdp", axis=0, tiled=True),
    )
    inputs_low = jnp.dot(hidden_in, full_in, preferred_element_type=jnp.float32).astype(
        jnp.bfloat16
    )
    errors_low = jnp.dot(out_grads, full_out, preferred_element_type=jnp.float32).astype(
        jnp.bfloat16
    )
    rows_here = inputs_low.shape[0]
    width = inputs_low.shape[1]
    pieces = owner_dp.shape[1]
    member = piece_of[0][:, None] == jnp.arange(pieces, dtype=jnp.int32)[None, :]
    spread = (member.astype(jnp.bfloat16)[:, :, None] * inputs_low[:, None, :]).reshape(
        rows_here, pieces * width
    )
    partial_value = lax.dot_general(
        spread, errors_low, (((0,), (0,)), ((), ())), preferred_element_type=jnp.float32
    )
    partial_value = partial_value.reshape(pieces, width * width)
    target = owner_dp[0]
    earlier = jnp.arange(pieces)[None, :] < jnp.arange(pieces)[:, None]
    ranked = jnp.sum(((target[:, None] == target[None, :]) & earlier).astype(jnp.int32), axis=1)
    places = target * CAP + ranked
    slots_total = count_dp * CAP
    routing_mask = places[None, :] == jnp.arange(slots_total, dtype=jnp.int32)[:, None]
    outgoing = jnp.dot(
        routing_mask.astype(jnp.float32), partial_value, precision=lax.Precision.HIGHEST
    )
    labels = jnp.sum(routing_mask.astype(jnp.int32) * (owner_slot[0][None, :] + 1), axis=1) - 1
    incoming, arrived = (
        lax.all_to_all(outgoing, "dp", split_axis=0, concat_axis=0, tiled=True),
        lax.all_to_all(labels, "dp", split_axis=0, concat_axis=0, tiled=True),
    )
    owned = count_dp // 2
    collect = (arrived[None, :] == jnp.arange(owned, dtype=jnp.int32)[:, None]).astype(jnp.float32)
    features = jnp.dot(collect, incoming, precision=lax.Precision.HIGHEST).astype(jnp.bfloat16)
    local_gram = lax.dot_general(
        features[:, :GR], features, (((0,), (0,)), ((), ())), preferred_element_type=jnp.float32
    )
    scale_factor = 1.0 / math.sqrt(owned * count_dp * count_fsdp)
    section_one = lax.psum_scatter(local_gram, "fsdp", scatter_dimension=1, tiled=True)
    result = lax.psum_scatter(section_one, "dp", scatter_dimension=0, tiled=True)
    return result * scale_factor


def solution(mesh):
    return jax.shard_map(
        on_device,
        mesh=mesh,
        in_specs=(
            P(("dp", "fsdp"), None),
            P(("dp", "fsdp"), None),
            P(("dp", "fsdp"), None),
            P(("dp", "fsdp"), None),
            P(("dp", "fsdp"), None),
            P("fsdp", None),
            P("fsdp", None),
        ),
        out_specs=P("dp", "fsdp"),
        check_vma=False,
    )
```

profile of v0, /device:TPU:0, one launch (start us, length us, event | category | flops | bytes accessed | tf_op | source)
XLA Modules:
  0.0 169.7 jit_solution(17521904007415587335)
XLA Ops:
  6.5 0.0 copy-start
  6.5 0.0 all-gather.2.cloned.1.call-start
  6.5 0.7 all-gather.2.cloned.1.call-update
  7.3 0.9 convert_reduce_fusion
  8.2 0.7 add_bitcast_fusion
  8.8 0.7 fusion.10
  9.5 0.1 select_reduce_fusion
  9.6 0.7 sub.6
  10.3 7.3 %all-to-all-start = ((s32[8,2,1]{1,2,0:T(1,128)}), s32[8,2,1]{1,2,0:T(1,128)S(1)}, u32[]{:S(2)}, u32[]{:S(2)}) async-start(s32[8,2,1]{1,2,0:T(1,128)} %bitcast.4), calls=%async_computation | async-start | bytes 8192 | tf_op jit(solution)/shard_map/all_to_all | solution.py:48
  17.5 10.2 %all_gather.7 = bf16[4096,64]{0,1:T(8,128)(2,1)S(1)} all-gather(bf16[1024,64]{0,1:T(8,128)(2,1)} %param.13), channel_id=1, replica_groups=mesh['dp'=8,'fsdp'=4] {'fsdp'}, dimensions={0}, use_global_device_ids=true | all-gather | bytes 655360 | tf_op jit(solution)/shard_map/all_gather | solution.py:17
  27.8 0.7 fusion.6
  28.4 7.0 %all-gather.2.cloned.1.call-done = bf16[14336,64]{0,1:T(8,128)(2,1)} async-done(((bf16[3584,64]{0,1:T(8,128)(2,1)}), bf16[14336,64]{0,1:T(8,128)(2,1)}) %all-gather.2.cloned.1.call-update) | async-done | bytes 1835024 | tf_op jit(solution)/shard_map/all_gather | solution.py:16
  35.4 4.0 %convolution_convert_fusion.2 = bf16[128,64]{0,1:T(8,128)(2,1)S(1)} fusion(bf16[128,14336]{1,0:T(8,128)(2,1)} %param.7, bf16[14336,64]{0,1:T(8,128)(2,1)} %all-gather.2.cloned.1.call-done), kind=kOutput, calls=%fused_computation.2 | convolution fusion | flops 234889216 | bytes 5521408 | tf_op jit(solution)/shard_map/dot_general | solution.py:19
  39.4 0.0 copy-done
  39.4 0.7 fusion
  40.1 0.1 reshape.72
  40.3 0.3 fusion.1
  40.6 0.9 copy.16
  41.5 0.0 all-to-all-done
  41.5 5.7 %all-to-all-start.1 = ((f32[8,2,4096]{2,1,0:T(2,128)}), f32[8,2,4096]{2,1,0:T(2,128)S(1)}, u32[]{:S(2)}, u32[]{:S(2)}) async-start(f32[8,2,4096]{2,1,0:T(2,128)} %copy.16), calls=%async_computation.1 | async-start | bytes 524288 | tf_op jit(solution)/shard_map/all_to_all | solution.py:47
  47.2 0.0 reduce-scatter.3.cloned.1.call-start
  47.2 0.5 broadcast.68
  47.8 0.7 reduce.3
  48.4 0.1 eq.89
  48.5 8.0 %all-to-all-done.1 = f32[8,2,4096]{2,1,0:T(2,128)S(1)} async-done(((f32[8,2,4096]{2,1,0:T(2,128)}), f32[8,2,4096]{2,1,0:T(2,128)S(1)}, u32[]{:S(2)}, u32[]{:S(2)}) %all-to-all-start.1) | async-done | bytes 262176 | tf_op jit(solution)/shard_map/all_to_all | solution.py:47
  56.5 0.2 all_to_all.12
  56.7 0.2 convolution_convert_fusion
  56.9 2.3 %fusion.7 = f32[192,4096]{1,0:T(8,128)} fusion(bf16[4,4096]{1,0:T(4,128)(2,1)S(1)} %convolution_convert_fusion), kind=kOutput, calls=%fused_computation.17 | convolution fusion | flops 6291456 | bytes 3180544 | tf_op jit(solution)/shard_map/dot_general | solution.py:53
  59.2 0.0 reduce-scatter.3.cloned.1.call-update
  59.2 0.0 reduce-scatter.5.cloned.1.call-start
  59.3 36.1 %reduce-scatter.3.cloned.1.call-done = f32[192,1024]{1,0:T(8,128)} async-done(((f32[192,4096]{1,0:T(8,128)}), f32[192,1024]{1,0:T(8,128)}) %reduce-scatter.3.cloned.1.call-update) | async-done | bytes 786448 | tf_op jit(solution)/shard_map/reduce_scatter | solution.py:57
  95.4 0.0 reduce-scatter.5.cloned.1.call-update
  95.4 66.2 %reduce-scatter.5.cloned.1.call-done = f32[24,1024]{1,0:T(8,128)} async-done(((f32[192,1024]{1,0:T(8,128)}), f32[24,1024]{1,0:T(8,128)}) %reduce-scatter.5.cloned.1.call-update) | async-done | bytes 98320 | tf_op jit(solution)/shard_map/reduce_scatter | solution.py:58
  161.6 1.5 broadcast_multiply_fusion.1
  (3 shorter events, 0.0 us)
Async XLA Ops:
  6.5 32.9 %copy-start = (bf16[128,4096]{1,0:T(8,128)(2,1)S(1)}, bf16[128,4096]{1,0:T(8,128)(2,1)}, u32[]{:S(2)}) copy-start(bf16[128,4096]{1,0:T(8,128)(2,1)} %param.8) | copy-start | bytes 3145732
  6.5 28.9 %all-gather.2.cloned.1.call-start = ((), (), s32[]{:S(2)}) async-start(), calls=%async_computation.4 | async-start | bytes 2293760 | tf_op jit(solution)/shard_map/all_gather | solution.py:16
  10.3 31.2 %all-to-all-start = ((s32[8,2,1]{1,2,0:T(1,128)}), s32[8,2,1]{1,2,0:T(1,128)S(1)}, u32[]{:S(2)}, u32[]{:S(2)}) async-start(s32[8,2,1]{1,2,0:T(1,128)} %bitcast.4), calls=%async_computation | async-start | bytes 8192 | tf_op jit(solution)/shard_map/all_to_all | solution.py:48
  41.5 15.0 %all-to-all-start.1 = ((f32[8,2,4096]{2,1,0:T(2,128)}), f32[8,2,4096]{2,1,0:T(2,128)S(1)}, u32[]{:S(2)}, u32[]{:S(2)}) async-start(f32[8,2,4096]{2,1,0:T(2,128)} %copy.16), calls=%async_computation.1 | async-start | bytes 524288 | tf_op jit(solution)/shard_map/all_to_all | solution.py:47
  47.2 48.2 %reduce-scatter.3.cloned.1.call-start = ((), (), s32[]{:S(2)}) async-start(), calls=%async_computation.5 | async-start | bytes 3932160 | tf_op jit(solution)/shard_map/reduce_scatter | solution.py:57
  59.2 102.4 %reduce-scatter.5.cloned.1.call-start = ((), (), s32[]{:S(2)}) async-start(), calls=%async_computation.6 | async-start | bytes 884736 | tf_op jit(solution)/shard_map/reduce_scatter | solution.py:58
Sparse Core Ops, SparseCore 0:
  8.9 26.4 all-gather.1
  59.3 36.0 reduce-scatter.2
  99.1 62.5 reduce-scatter.4
where the time goes:
time: 170 us
  waiting for transfers between devices  118 us (69%)
  between operations  13.2 us (8%)
  starting transfers between devices  13.1 us (8%)
  blocking collectives  10.2 us (6%)
  matrix products  7.5 us (4%)
  other arithmetic  5.21 us (3%)
  local copies, waits for them, and re-layouts  2.47 us (1%)
    reduce_scatter x1, waiting for transfers between devices, on_device(): lax.psum_scatter(section_one, 'dp', scatter_dimension=0, tiled=True)  66.2 us
    reduce_scatter x1, waiting for transfers between devices, on_device(): lax.psum_scatter(local_gram, 'fsdp', scatter_dimension=1, tiled=True)  36.1 us
    all_gather x1, blocking collectives, on_device(): lax.all_gather(sketch_out, 'fsdp', axis=0, tiled=True)  10.2 us
    all_to_all x1, waiting for transfers between devices, on_device(): lax.all_to_all(outgoing, 'dp', split_axis=0, concat_axis=0, tiled=True)  8.01 us
    all_to_all x1, starting transfers between devices, on_device(): lax.all_to_all(labels, 'dp', split_axis=0, concat_axis=0, tiled=True)  7.28 us
    all_gather x1, waiting for transfers between devices, on_device(): lax.all_gather(sketch_in, 'fsdp', axis=0, tiled=True)  7 us
    all_to_all x1, starting transfers between devices, on_device(): lax.all_to_all(outgoing, 'dp', split_axis=0, concat_axis=0, tiled=True)  5.71 us
    dot_general x1, matrix products, on_device(): jnp.dot(hidden_in, full_in, preferred_element_type=jnp.float32)  3.99 us
  transfers between devices with their start and end apart: 5, of which 4 were waited for; matrix products, arithmetic and copies ran while one was open for 6% of the time, Pallas kernels for 0%

commit v1 on v0

v1 whole, which is shorter than its diff:
```python
import functools
import math

import jax
import jax.numpy as jnp
from jax import lax
from jax.experimental import pallas as pl
from jax.experimental.pallas import tpu as pltpu
from jax.sharding import PartitionSpec as P

CAP = 2
GR = 192
BF16 = jnp.bfloat16
F32 = jnp.float32
KEY_ROWS = 16
CONTRACT_LAST = (((1,), (1,)), ((), ()))
VMEM = pl.BlockSpec(memory_space=pltpu.VMEM)
SMEM = pl.BlockSpec(memory_space=pltpu.SMEM)


def swap(value, axis, bit):
    count = lax.axis_size(axis)
    return lax.ppermute(value, axis, [(i, i ^ bit) for i in range(count)])


def bits_of(count):
    return [1 << k for k in range(count.bit_length() - 1)]


def gather_group(rows):
    bits = bits_of(lax.axis_size("dp"))
    for bit in bits[1:] + bits[:1]:
        rows = jnp.concatenate([rows, swap(rows, "dp", bit)], axis=0)
    return rows


def gather_shards(own):
    shards = {0: own}
    for bit in reversed(bits_of(lax.axis_size("fsdp"))):
        shards.update({k ^ bit: swap(v, "fsdp", bit) for k, v in list(shards.items())})
    return [shards[k] for k in range(len(shards))]


def project_kernel(count, *refs):
    total = refs[2 * count][...] if len(refs) > 2 * count + 1 else 0.0
    for sketch, tokens in zip(refs[:count], refs[count : 2 * count]):
        total += lax.dot_general(
            sketch[...], tokens[...], CONTRACT_LAST, preferred_element_type=F32
        )
    refs[-1][...] = total.astype(refs[-1].dtype)


def project(sketches, tokens, total, dtype):
    operands = [*sketches, *tokens] + ([] if total is None else [total])
    return pl.pallas_call(
        functools.partial(project_kernel, len(sketches)),
        out_shape=jax.ShapeDtypeStruct((sketches[0].shape[0], tokens[0].shape[0]), dtype),
        in_specs=[VMEM] * len(operands),
        out_specs=VMEM,
    )(*operands)


def errors_kernel(count, owned, *refs):
    sketches, tokens = refs[:count], refs[count : 2 * count]
    piece_of, owner_dp, owner_slot, out = refs[2 * count :]
    total = 0.0
    for sketch, part in zip(sketches, tokens):
        total += lax.dot_general(
            sketch[...], part[...], CONTRACT_LAST, preferred_element_type=F32
        )
    width = total.shape[0]
    out[:width, :] = total.astype(BF16)
    piece = piece_of[...]
    key = jnp.zeros(piece.shape, jnp.int32)
    for p in range(owner_dp.shape[1]):
        key = jnp.where(piece == p, owner_dp[0, p] * owned + owner_slot[0, p], key)
    key = jnp.broadcast_to(key.astype(F32), (KEY_ROWS, key.shape[1]))
    out[width:, :] = key.astype(BF16)


def gram_kernel(count_dp, group_examples, scale, *refs):
    groups = len(refs) // 2
    errors, inputs, out = refs[:groups], refs[groups : 2 * groups], refs[-1]
    rows_here, columns_here = out.shape
    width = inputs[0].shape[0] // count_dp
    mine = columns_here // width
    high = width + KEY_ROWS
    start = pl.multiple_of(lax.axis_index("fsdp") * mine, mine)
    place = (rows_here, width)
    column = lax.axis_index("dp") * rows_here + lax.broadcasted_iota(jnp.int32, place, 0)
    at = lax.broadcasted_iota(jnp.int32, place, 1)
    pick_in = (at == column // width).astype(F32).astype(BF16)
    pick_out = (at == column % width).astype(F32).astype(BF16)
    wide, narrow = [], []
    for e_ref, i_ref in zip(errors, inputs):
        err = jnp.concatenate([e_ref[k * high : k * high + width, :] for k in range(count_dp)], axis=1)
        key = jnp.concatenate(
            [e_ref[k * high + width : (k + 1) * high, :] for k in range(count_dp)], axis=1
        )
        key = key.astype(F32)[:1, :]
        low = jnp.concatenate([i_ref[k * width : (k + 1) * width, :] for k in range(count_dp)], axis=1)
        here = jnp.concatenate(
            [i_ref[pl.ds(k * width + start, mine), :] for k in range(count_dp)], axis=1
        )
        example = lax.broadcasted_iota(jnp.int32, (group_examples, key.shape[1]), 0).astype(F32)
        member = (example == key).astype(F32).astype(BF16)
        spread = jnp.concatenate([member * here[i : i + 1, :] for i in range(mine)], axis=0)
        wide.append(
            lax.dot_general(spread, err, CONTRACT_LAST, preferred_element_type=F32).astype(BF16)
        )
        product = jnp.dot(pick_in, low, preferred_element_type=F32) * jnp.dot(
            pick_out, err, preferred_element_type=F32
        )
        upper = product.astype(BF16)
        lower = (product - upper.astype(F32)).astype(BF16)
        part = lax.dot_general(upper, member, CONTRACT_LAST, preferred_element_type=F32)
        part += lax.dot_general(lower, member, CONTRACT_LAST, preferred_element_type=F32)
        narrow.append(part.astype(BF16))
    left = jnp.concatenate(narrow, axis=1)
    blocks = []
    for i in range(mine):
        right = jnp.concatenate(
            [w[i * group_examples : (i + 1) * group_examples, :] for w in wide], axis=0
        )
        blocks.append(jnp.dot(left, right, preferred_element_type=F32))
    out[...] = jnp.concatenate(blocks, axis=1) * scale


def by_tokens(hidden_in, out_grads, piece_of, owner_dp, owner_slot, sketch_in, sketch_out):
    count_dp = lax.axis_size("dp")
    count_fsdp = lax.axis_size("fsdp")
    token_rows = hidden_in.shape[0]
    width = sketch_in.shape[1]
    owned = count_dp // 2
    me = lax.axis_index("fsdp")

    def columns(tokens, k):
        size = tokens.shape[1] // count_fsdp
        return lax.dynamic_slice_in_dim(tokens, (me ^ k) * size, size, axis=1)

    out_shards = gather_shards(sketch_out.T)
    in_shards = gather_shards(sketch_in.T)
    errors = pl.pallas_call(
        functools.partial(errors_kernel, count_fsdp, owned),
        out_shape=jax.ShapeDtypeStruct((width + KEY_ROWS, token_rows), BF16),
        in_specs=[VMEM] * (2 * count_fsdp + 1) + [SMEM] * 2,
        out_specs=VMEM,
    )(
        *out_shards,
        *[columns(out_grads, k) for k in range(count_fsdp)],
        piece_of,
        owner_dp,
        owner_slot,
    )
    near = list(range(max(1, count_fsdp // 2)))
    far = list(range(len(near), count_fsdp))
    inputs = project(
        [in_shards[k] for k in near], [columns(hidden_in, k) for k in near], None, F32
    )
    for k in far:
        inputs = project(
            [in_shards[k]], [columns(hidden_in, k)], inputs, BF16 if k == far[-1] else F32
        )
    all_errors = gather_shards(gather_group(errors))
    all_inputs = gather_shards(gather_group(inputs))
    scale = 1.0 / math.sqrt(owned * count_dp * count_fsdp)
    return pl.pallas_call(
        functools.partial(gram_kernel, count_dp, owned * count_dp, scale),
        out_shape=jax.ShapeDtypeStruct((GR // count_dp, width * width // count_fsdp), F32),
        in_specs=[VMEM] * (2 * count_fsdp),
        out_specs=VMEM,
        compiler_params=pltpu.CompilerParams(vmem_limit_bytes=24 * 1024 * 1024),
    )(*all_errors, *all_inputs)


def by_pieces(hidden_in, out_grads, piece_of, owner_dp, owner_slot, sketch_in, sketch_out):
    count_dp = lax.axis_size("dp")
    count_fsdp = lax.axis_size("fsdp")
    full_in, full_out = (
        lax.all_gather(sketch_in, "fsdp", axis=0, tiled=True),
        lax.all_gather(sketch_out, "fsdp", axis=0, tiled=True),
    )
    inputs_low = jnp.dot(hidden_in, full_in, preferred_element_type=F32).astype(BF16)
    errors_low = jnp.dot(out_grads, full_out, preferred_element_type=F32).astype(BF16)
    rows_here = inputs_low.shape[0]
    width = inputs_low.shape[1]
    pieces = owner_dp.shape[1]
    member = piece_of[0][:, None] == jnp.arange(pieces, dtype=jnp.int32)[None, :]
    spread = (member.astype(BF16)[:, :, None] * inputs_low[:, None, :]).reshape(
        rows_here, pieces * width
    )
    partial_value = lax.dot_general(
        spread, errors_low, (((0,), (0,)), ((), ())), preferred_element_type=F32
    )
    partial_value = partial_value.reshape(pieces, width * width)
    target = owner_dp[0]
    earlier = jnp.arange(pieces)[None, :] < jnp.arange(pieces)[:, None]
    ranked = jnp.sum(((target[:, None] == target[None, :]) & earlier).astype(jnp.int32), axis=1)
    places = target * CAP + ranked
    slots_total = count_dp * CAP
    routing_mask = places[None, :] == jnp.arange(slots_total, dtype=jnp.int32)[:, None]
    outgoing = jnp.dot(routing_mask.astype(F32), partial_value, precision=lax.Precision.HIGHEST)
    labels = jnp.sum(routing_mask.astype(jnp.int32) * (owner_slot[0][None, :] + 1), axis=1) - 1
    incoming, arrived = (
        lax.all_to_all(outgoing, "dp", split_axis=0, concat_axis=0, tiled=True),
        lax.all_to_all(labels, "dp", split_axis=0, concat_axis=0, tiled=True),
    )
    owned = count_dp // 2
    collect = (arrived[None, :] == jnp.arange(owned, dtype=jnp.int32)[:, None]).astype(F32)
    features = jnp.dot(collect, incoming, precision=lax.Precision.HIGHEST).astype(BF16)
    local_gram = lax.dot_general(
        features[:, :GR], features, (((0,), (0,)), ((), ())), preferred_element_type=F32
    )
    scale_factor = 1.0 / math.sqrt(owned * count_dp * count_fsdp)
    section_one = lax.psum_scatter(local_gram, "fsdp", scatter_dimension=1, tiled=True)
    result = lax.psum_scatter(section_one, "dp", scatter_dimension=0, tiled=True)
    return result * scale_factor


def on_device(hidden_in, out_grads, piece_of, owner_dp, owner_slot, sketch_in, sketch_out):
    count_dp = lax.axis_size("dp")
    count_fsdp = lax.axis_size("fsdp")
    token_rows = hidden_in.shape[0]
    width = sketch_in.shape[1]
    gathered = count_dp * count_fsdp * token_rows * 2 * width * 2
    summed = GR * width * width * 4
    doubling = all(n & (n - 1) == 0 for n in (count_dp, count_fsdp))
    whole_tiles = token_rows % 128 == 0 and width % (16 * count_fsdp) == 0
    exact_keys = count_dp * (count_dp // 2) <= 256
    form = by_tokens if gathered <= summed and doubling and whole_tiles and exact_keys else by_pieces
    return form(hidden_in, out_grads, piece_of, owner_dp, owner_slot, sketch_in, sketch_out)


def solution(mesh):
    return jax.shard_map(
        on_device,
        mesh=mesh,
        in_specs=(
            P(("dp", "fsdp"), None),
            P(("dp", "fsdp"), None),
            P(("dp", "fsdp"), None),
            P(("dp", "fsdp"), None),
            P(("dp", "fsdp"), None),
            P("fsdp", None),
            P("fsdp", None),
        ),
        out_specs=P("dp", "fsdp"),
        check_vma=False,
    )
```

time: 170 us -> 62.4 us (0.37)
  waiting for transfers between devices: 118 us -> 20.2 us
  between operations: 13.2 us -> 0.08 us
  Pallas kernels: 0 us -> 13 us
  blocking collectives: 10.2 us -> 0 us
  matrix products: 7.5 us -> 0 us
  local copies, waits for them, and re-layouts: 2.47 us -> 8.47 us
  starting transfers between devices: 13.1 us -> 18 us
  other arithmetic: 5.21 us -> 2.19 us
    reduce_scatter x2 -> x0, waiting for transfers between devices: 102 us -> none  [the longest x1 66.2 us: on_device(): lax.psum_scatter(section_one, 'dp', scatter_dimension=0, tiled=True)]
    ppermute x0 -> x18, waiting for transfers between devices: none -> 20.2 us  [swap(): return lax.ppermute(value, axis, [(i, i ^ bit) for i in range(count)])]
    ppermute x0 -> x18, starting transfers between devices: none -> 18 us  [swap(): return lax.ppermute(value, axis, [(i, i ^ bit) for i in range(count)])]
    pallas_call x0 -> x5, Pallas kernels: none -> 13 us  [the longest x3 7.77 us: project(): pl.pallas_call(functools.partial(project_kernel, len(sketches)), out_shap...]
    all_to_all x2 -> x0, starting transfers between devices: 13 us -> none  [the longest x1 7.28 us: on_device(): lax.all_to_all(labels, 'dp', split_axis=0, concat_axis=0, tiled=True)]
    all_gather x1 -> x0, blocking collectives: 10.2 us -> none  [on_device(): lax.all_gather(sketch_out, 'fsdp', axis=0, tiled=True)]
    all_to_all x2 -> x0, waiting for transfers between devices: 8.02 us -> none  [the longest x1 8.01 us: on_device(): lax.all_to_all(outgoing, 'dp', split_axis=0, concat_axis=0, tiled=True)]
    dot_general x5 -> x0, matrix products: 7.5 us -> none  [the longest x1 3.99 us: on_device(): jnp.dot(hidden_in, full_in, preferred_element_type=jnp.float32)]
  transfers between devices with their start and end apart: 5 -> 18, of which waited for: 4 -> 8; matrix products, arithmetic and copies ran while one was open for 6% -> 14% of each run, Pallas kernels for 0% -> 17%
where the time goes in v1:
time: 62.4 us; the launch traced here: 62 us
  waiting for transfers between devices  20.2 us (32%)
  starting transfers between devices  18 us (29%)
  Pallas kernels  13 us (21%)
  local copies, waits for them, and re-layouts  8.47 us (14%)
  other arithmetic  2.19 us (4%)
    ppermute x18, waiting for transfers between devices, swap(): return lax.ppermute(value, axis, [(i, i ^ bit) for i in range(count)])  20.2 us
    ppermute x18, starting transfers between devices, swap(): return lax.ppermute(value, axis, [(i, i ^ bit) for i in range(count)])  18 us
    pallas_call x3, Pallas kernels, project(): pl.pallas_call(functools.partial(project_kernel, len(sketches)), out_shap...  7.77 us
    dynamic_slice x2, local copies, waits for them, and re-layouts, columns(): return lax.dynamic_slice_in_dim(tokens, (me ^ k) * size, size, axis=1)  6.19 us
    pallas_call x1, Pallas kernels, by_tokens(): pl.pallas_call(functools.partial(gram_kernel, count_dp, owned * count_dp,...  2.73 us
    pallas_call x1, Pallas kernels, by_tokens(): pl.pallas_call(functools.partial(errors_kernel, count_fsdp, owned), out_s...  2.51 us
    unnamed x14, local copies, waits for them, and re-layouts  2.28 us
    concatenate x6, other arithmetic, gather_group(): rows = jnp.concatenate([rows, swap(rows, 'dp', bit)], axis=0)  2.19 us
  transfers between devices with their start and end apart: 18, of which 8 were waited for; matrix products, arithmetic and copies ran while one was open for 14% of the time, Pallas kernels for 17%

profile of v1, /device:TPU:0, one launch (start us, length us, event | category | flops | bytes accessed | tf_op | source)
XLA Modules:
  0.0 62.0 jit_solution(8466737351618464635)
XLA Ops:
  0.0 2.9 %collective-permute-start.9 = (bf16[64,3584]{1,0:T(8,128)(2,1)}, bf16[64,3584]{1,0:T(8,128)(2,1)S(1)}, u32[]{:S(2)}, u32[]{:S(2)}) collective-permute-start(bf16[64,3584]{1,0:T(8,128)(2,1)} %bitcast.2), channel_id=1, source_target_pairs={{0,2},{1,3},{2,0},{3,1},{4,6},{5,7},{6,4},{7,5},{8,10},{9,11},{10,... | collective-permute-start | bytes 1376264 | tf_op jit(solution)/shard_map/ppermute | solution.py:23
  2.9 0.0 collective-permute-start.1
  3.0 0.0 collective-permute-start.11
  3.0 0.5 collective-permute-start
  3.5 13.0 %collective-permute-done.1.refs_2_ = bf16[64,1024]{1,0:T(8,128)(2,1)S(1)} collective-permute-done((bf16[64,1024]{1,0:T(8,128)(2,1)}, bf16[64,1024]{1,0:T(8,128)(2,1)S(1)}, u32[]{:S(2)}, u32[]{:S(2)}) %collective-permute-start.1) | collective-permute-done | bytes 131104 | tf_op jit(solution)/shard_map/ppermute | solution.py:23
  16.5 0.0 copy-start.4
  16.5 0.0 collective-permute-start.2
  16.5 2.3 %constant_dynamic-slice_fusion.4 = (bf16[128,1024]{1,0:T(8,128)(2,1)}, bf16[128,1024]{1,0:T(8,128)(2,1)}, bf16[128,1024]{1,0:T(8,128)(2,1)}, bf16[128,1024]{1,0:T(8,128)(2,1)}) fusion(bf16[128,4096]{1,0:T(8,128)(2,1)} %param.8, s32[]{:T(128)S(6)} %select_n.27, s32[]{:T(128)S(6)} %select_n.25, s32[]{:T(128)S(6)} %select_n.24, s32[]{:T(128)S(6)} %select_n.26), kind=kLoop, calls=%fused_computation.10 | loop fusion | bytes 2097168 | tf_op jit(solution)/shard_map/dynamic_slice | solution.py:139
  18.8 0.0 collective-permute-done.refs_1_
  18.8 0.0 copy-start.5
  18.8 0.0 collective-permute-done.2.refs_3_
  18.8 0.0 copy-start.6
  18.8 0.0 copy-done.4
  18.8 0.6 copy-done.5
  19.4 0.1 copy-done.6
  19.5 2.5 %shard_map.73 = bf16[80,128]{1,0:T(8,128)(2,1)} custom-call(bf16[64,1024]{1,0:T(8,128)(2,1)} %bitcast.7, bf16[64,1024]{1,0:T(8,128)(2,1)} %copy-done.5, bf16[64,1024]{1,0:T(8,128)(2,1)} %copy-done.4, bf16[64,1024]{1,0:T(8,128)(2,1)} %copy-done.6, bf16[128,1024]{1,0:T(8,128)(2,1)} %get-tuple-element.11.refs_4_, bf16[128,1024]{1,0:T(8,128)(2,1)} %get-tuple-element.10.refs_5_, ...), custom_call_target="tpu_custom_call" | custom-call | tf_op jit(solution)/shard_map/pallas_call | solution.py:143
  22.0 1.8 %collective-permute-start.3 = (bf16[80,128]{1,0:T(8,128)(2,1)}, bf16[80,128]{1,0:T(8,128)(2,1)S(1)}, u32[]{:S(2)}, u32[]{:S(2)}) collective-permute-start(bf16[80,128]{1,0:T(8,128)(2,1)} %shard_map.73), channel_id=1, source_target_pairs={{0,8},{4,12},{8,0},{12,4},{16,24},{20,28},{24,16},{28,20},{1,9},{5... | collective-permute-start | bytes 61448 | tf_op jit(solution)/shard_map/ppermute | solution.py:23
  23.8 0.0 collective-permute-done.9.refs_0_
  23.8 0.0 copy-start
  23.8 0.2 collective-permute-start.10
  24.0 3.9 %constant_dynamic-slice_fusion = (bf16[128,3584]{1,0:T(8,128)(2,1)}, bf16[128,3584]{1,0:T(8,128)(2,1)}, bf16[128,3584]{1,0:T(8,128)(2,1)}, bf16[128,3584]{1,0:T(8,128)(2,1)}) fusion(bf16[128,14336]{1,0:T(8,128)(2,1)} %param.7, s32[]{:T(128)S(6)} %select_n.31, s32[]{:T(128)S(6)} %select_n.29, s32[]{:T(128)S(6)} %select_n.28, s32[]{:T(128)S(6)} %select_n.30), kind=kLoop, calls=%fused_computation.6 | loop fusion | bytes 7340048 | tf_op jit(solution)/shard_map/dynamic_slice | solution.py:139
  27.9 0.0 copy-done
  27.9 0.0 copy-start.3
  27.9 0.0 collective-permute-done.11.refs_1_
  27.9 0.0 copy-start.2
  27.9 0.8 %copy-done.2 = bf16[64,3584]{1,0:T(8,128)(2,1)} copy-done((bf16[64,3584]{1,0:T(8,128)(2,1)}, bf16[64,3584]{1,0:T(8,128)(2,1)S(1)}, u32[]{:S(2)}) %copy-start.2) | copy-done | bytes 458776
  28.7 3.1 %shard_map.74.refs_2_ = f32[64,128]{1,0:T(8,128)} custom-call(bf16[64,3584]{1,0:T(8,128)(2,1)} %bitcast.4, bf16[64,3584]{1,0:T(8,128)(2,1)} %copy-done.2, bf16[128,3584]{1,0:T(8,128)(2,1)} %get-tuple-element.8.refs_2_, bf16[128,3584]{1,0:T(8,128)(2,1)} %get-tuple-element.5.refs_3_), custom_call_target="tpu_custom_call" | custom-call | tf_op jit(solution)/shard_map/pallas_call | solution.py:55
  31.8 2.3 %shard_map.75.refs_2_ = f32[64,128]{1,0:T(8,128)} custom-call(bf16[64,3584]{1,0:T(8,128)(2,1)} %copy-done, bf16[128,3584]{1,0:T(8,128)(2,1)} %get-tuple-element.6.refs_1_, f32[64,128]{1,0:T(8,128)} %shard_map.74.refs_2_), custom_call_target="tpu_custom_call" | custom-call | tf_op jit(solution)/shard_map/pallas_call | solution.py:55
  34.1 0.0 collective-permute-done.10.refs_0_
  34.1 0.0 copy-start.1
  34.1 0.8 %copy-done.1 = bf16[64,3584]{1,0:T(8,128)(2,1)} copy-done((bf16[64,3584]{1,0:T(8,128)(2,1)}, bf16[64,3584]{1,0:T(8,128)(2,1)S(1)}, u32[]{:S(2)}) %copy-start.1) | copy-done | bytes 458776
  34.9 2.3 %shard_map.76 = bf16[64,128]{1,0:T(8,128)(2,1)} custom-call(bf16[64,3584]{1,0:T(8,128)(2,1)} %copy-done.1, bf16[128,3584]{1,0:T(8,128)(2,1)} %get-tuple-element.7.refs_1_, f32[64,128]{1,0:T(8,128)} %shard_map.75.refs_2_), custom_call_target="tpu_custom_call" | custom-call | tf_op jit(solution)/shard_map/pallas_call | solution.py:55
  37.3 0.4 collective-permute-start.12
  37.7 0.0 collective-permute-done.3
  37.7 0.0 copy-done.3
  37.7 2.7 %collective-permute-start.4 = (bf16[160,128]{1,0:T(8,128)(2,1)S(1)}, bf16[160,128]{1,0:T(8,128)(2,1)S(1)}, u32[]{:S(2)}, u32[]{:S(2)}) collective-permute-start(bf16[160,128]{1,0:T(8,128)(2,1)S(1)} %pad_maximum_fusion.4), channel_id=1, source_target_pairs={{0,16},{4,20},{8,24},{12,28},{16,0},{20,4},{24,8},{28,12},{1,17},{... | collective-permute-start | bytes 122888 | tf_op jit(solution)/shard_map/ppermute | solution.py:23
  40.4 0.8 %collective-permute-done.12 = bf16[64,128]{1,0:T(8,128)(2,1)S(1)} collective-permute-done((bf16[64,128]{1,0:T(8,128)(2,1)}, bf16[64,128]{1,0:T(8,128)(2,1)S(1)}, u32[]{:S(2)}, u32[]{:S(2)}) %collective-permute-start.12) | collective-permute-done | bytes 16416 | tf_op jit(solution)/shard_map/ppermute | solution.py:23
  41.2 0.7 %pad_maximum_fusion.5 = bf16[128,128]{1,0:T(8,128)(2,1)S(1)} fusion(bf16[64,128]{1,0:T(8,128)(2,1)S(1)} %collective-permute-done.12, bf16[64,128]{1,0:T(8,128)(2,1)} %shard_map.76), kind=kLoop, calls=%fused_computation.5 | loop fusion | flops 65536 | bytes 65536 | tf_op jit(solution)/shard_map/concatenate | solution.py:33
  42.0 2.6 %collective-permute-start.13 = (bf16[128,128]{1,0:T(8,128)(2,1)S(1)}, bf16[128,128]{1,0:T(8,128)(2,1)S(1)}, u32[]{:S(2)}, u32[]{:S(2)}) collective-permute-start(bf16[128,128]{1,0:T(8,128)(2,1)S(1)} %pad_maximum_fusion.5), channel_id=1, source_target_pairs={{0,16},{4,20},{8,24},{12,28},{16,0},{20,4},{24,8},{28,12},{1,17},{... | collective-permute-start | bytes 98312 | tf_op jit(solution)/shard_map/ppermute | solution.py:23
  44.6 0.0 collective-permute-done.4
  44.6 1.6 %collective-permute-start.5 = (bf16[320,128]{1,0:T(8,128)(2,1)S(1)}, bf16[320,128]{1,0:T(8,128)(2,1)S(1)}, u32[]{:S(2)}, u32[]{:S(2)}) collective-permute-start(bf16[320,128]{1,0:T(8,128)(2,1)S(1)} %pad_maximum_fusion.2), channel_id=1, source_target_pairs={{0,4},{4,0},{8,12},{12,8},{16,20},{20,16},{24,28},{28,24},{1,5},{5... | collective-permute-start | bytes 245768 | tf_op jit(solution)/shard_map/ppermute | solution.py:23
  46.1 1.0 %collective-permute-done.13 = bf16[128,128]{1,0:T(8,128)(2,1)S(1)} collective-permute-done((bf16[128,128]{1,0:T(8,128)(2,1)S(1)}, bf16[128,128]{1,0:T(8,128)(2,1)S(1)}, u32[]{:S(2)}, u32[]{:S(2)}) %collective-permute-start.13) | collective-permute-done | bytes 32800 | tf_op jit(solution)/shard_map/ppermute | solution.py:23
  47.1 0.7 %pad_maximum_fusion.3 = bf16[256,128]{1,0:T(8,128)(2,1)S(1)} fusion(bf16[128,128]{1,0:T(8,128)(2,1)S(1)} %collective-permute-done.13, bf16[64,128]{1,0:T(8,128)(2,1)S(1)} %collective-permute-done.12, bf16[64,128]{1,0:T(8,128)(2,1)} %shard_map.76), kind=kLoop, calls=%fused_computation.3 | loop fusion | flops 196608 | bytes 131072 | tf_op jit(solution)/shard_map/concatenate | solution.py:33
  47.8 1.5 %collective-permute-start.14 = (bf16[256,128]{1,0:T(8,128)(2,1)S(1)}, bf16[256,128]{1,0:T(8,128)(2,1)S(1)}, u32[]{:S(2)}, u32[]{:S(2)}) collective-permute-start(bf16[256,128]{1,0:T(8,128)(2,1)S(1)} %pad_maximum_fusion.3), channel_id=1, source_target_pairs={{0,4},{4,0},{8,12},{12,8},{16,20},{20,16},{24,28},{28,24},{1,5},{5... | collective-permute-start | bytes 196616 | tf_op jit(solution)/shard_map/ppermute | solution.py:23
  49.4 0.3 collective-permute-done.5
  49.7 1.6 %collective-permute-start.7 = (bf16[640,128]{1,0:T(8,128)(2,1)S(1)}, bf16[640,128]{1,0:T(8,128)(2,1)S(1)}, u32[]{:S(2)}, u32[]{:S(2)}) collective-permute-start(bf16[640,128]{1,0:T(8,128)(2,1)S(1)} %pad_maximum_fusion.refs_0_), channel_id=1, source_target_pairs={{0,2},{1,3},{2,0},{3,1},{4,6},{5,7},{6,4},{7,5},{8,10},{9,11},{10,... | collective-permute-start | bytes 491528 | tf_op jit(solution)/shard_map/ppermute | solution.py:23
  51.3 0.8 %collective-permute-done.14 = bf16[256,128]{1,0:T(8,128)(2,1)S(1)} collective-permute-done((bf16[256,128]{1,0:T(8,128)(2,1)S(1)}, bf16[256,128]{1,0:T(8,128)(2,1)S(1)}, u32[]{:S(2)}, u32[]{:S(2)}) %collective-permute-start.14) | collective-permute-done | bytes 65568 | tf_op jit(solution)/shard_map/ppermute | solution.py:23
  52.1 0.7 %pad_maximum_fusion.1.refs_4_ = bf16[512,128]{1,0:T(8,128)(2,1)S(1)} fusion(bf16[256,128]{1,0:T(8,128)(2,1)S(1)} %collective-permute-done.14, bf16[128,128]{1,0:T(8,128)(2,1)S(1)} %collective-permute-done.13, bf16[64,128]{1,0:T(8,128)(2,1)S(1)} %collective-permute-done.12, bf16[64,128]{1,0:T(8,128)(2,1)} %shard_map.76), kind=kLoop, calls=%fused_computation.1 | loop fusion | flops 524288 | bytes 262144 | tf_op jit(solution)/shard_map/concatenate | solution.py:33
  52.8 1.6 %collective-permute-start.16 = (bf16[512,128]{1,0:T(8,128)(2,1)S(1)}, bf16[512,128]{1,0:T(8,128)(2,1)S(1)}, u32[]{:S(2)}, u32[]{:S(2)}) collective-permute-start(bf16[512,128]{1,0:T(8,128)(2,1)S(1)} %pad_maximum_fusion.1.refs_4_), channel_id=1, source_target_pairs={{0,2},{1,3},{2,0},{3,1},{4,6},{5,7},{6,4},{7,5},{8,10},{9,11},{10,... | collective-permute-start | bytes 393224 | tf_op jit(solution)/shard_map/ppermute | solution.py:23
  54.4 0.0 collective-permute-start.6
  54.4 1.7 %collective-permute-done.7.refs_2_ = bf16[640,128]{1,0:T(8,128)(2,1)S(1)} collective-permute-done((bf16[640,128]{1,0:T(8,128)(2,1)S(1)}, bf16[640,128]{1,0:T(8,128)(2,1)S(1)}, u32[]{:S(2)}, u32[]{:S(2)}) %collective-permute-start.7) | collective-permute-done | bytes 163872 | tf_op jit(solution)/shard_map/ppermute | solution.py:23
  56.1 0.0 collective-permute-start.8
  56.1 0.5 collective-permute-start.15
  56.6 1.3 %collective-permute-done.16.refs_6_ = bf16[512,128]{1,0:T(8,128)(2,1)S(1)} collective-permute-done((bf16[512,128]{1,0:T(8,128)(2,1)S(1)}, bf16[512,128]{1,0:T(8,128)(2,1)S(1)}, u32[]{:S(2)}, u32[]{:S(2)}) %collective-permute-start.16) | collective-permute-done | bytes 131104 | tf_op jit(solution)/shard_map/ppermute | solution.py:23
  57.9 0.0 collective-permute-start.17
  57.9 0.0 collective-permute-done.6.refs_1_
  57.9 0.0 collective-permute-done.8.refs_3_
  57.9 0.0 collective-permute-done.15.refs_5_
  57.9 1.3 %collective-permute-done.17.refs_7_ = bf16[512,128]{1,0:T(8,128)(2,1)S(1)} collective-permute-done((bf16[512,128]{1,0:T(8,128)(2,1)S(1)}, bf16[512,128]{1,0:T(8,128)(2,1)S(1)}, u32[]{:S(2)}, u32[]{:S(2)}) %collective-permute-start.17) | collective-permute-done | bytes 131104 | tf_op jit(solution)/shard_map/ppermute | solution.py:23
  59.2 2.7 %shard_map.77 = f32[24,1024]{1,0:T(8,128)} custom-call(bf16[640,128]{1,0:T(8,128)(2,1)S(1)} %pad_maximum_fusion.refs_0_, bf16[640,128]{1,0:T(8,128)(2,1)S(1)} %collective-permute-done.6.refs_1_, bf16[640,128]{1,0:T(8,128)(2,1)S(1)} %collective-permute-done.7.refs_2_, bf16[640,128]{1,0:T(8,128)(2,1)S(1)} %collective-permute-done.8.refs_3_, ...), custom_call_target="tpu_custom_call" | custom-call | tf_op jit(solution)/shard_map/pallas_call | solution.py:167
  (3 shorter events, 0.0 us)
Async XLA Ops:
  0.0 23.8 %collective-permute-start.9 = (bf16[64,3584]{1,0:T(8,128)(2,1)}, bf16[64,3584]{1,0:T(8,128)(2,1)S(1)}, u32[]{:S(2)}, u32[]{:S(2)}) collective-permute-start(bf16[64,3584]{1,0:T(8,128)(2,1)} %bitcast.2), channel_id=1, source_target_pairs={{0,2},{1,3},{2,0},{3,1},{4,6},{5,7},{6,4},{7,5},{8,10},{9,11},{10,... | collective-permute-start | bytes 1376264 | tf_op jit(solution)/shard_map/ppermute | solution.py:23
  2.9 13.5 %collective-permute-start.1 = (bf16[64,1024]{1,0:T(8,128)(2,1)}, bf16[64,1024]{1,0:T(8,128)(2,1)S(1)}, u32[]{:S(2)}, u32[]{:S(2)}) collective-permute-start(bf16[64,1024]{1,0:T(8,128)(2,1)} %bitcast.5), channel_id=1, source_target_pairs={{0,2},{1,3},{2,0},{3,1},{4,6},{5,7},{6,4},{7,5},{8,10},{9,11},{10,... | collective-permute-start | bytes 393224 | tf_op jit(solution)/shard_map/ppermute | solution.py:23
  3.0 24.9 %collective-permute-start.11 = (bf16[64,3584]{1,0:T(8,128)(2,1)}, bf16[64,3584]{1,0:T(8,128)(2,1)S(1)}, u32[]{:S(2)}, u32[]{:S(2)}) collective-permute-start(bf16[64,3584]{1,0:T(8,128)(2,1)} %bitcast.3), channel_id=1, source_target_pairs={{0,1},{1,0},{2,3},{3,2},{4,5},{5,4},{6,7},{7,6},{8,9},{9,8},{10,11... | collective-permute-start | bytes 1376264 | tf_op jit(solution)/shard_map/ppermute | solution.py:23
  3.0 15.8 %collective-permute-start = (bf16[64,1024]{1,0:T(8,128)(2,1)}, bf16[64,1024]{1,0:T(8,128)(2,1)S(1)}, u32[]{:S(2)}, u32[]{:S(2)}) collective-permute-start(bf16[64,1024]{1,0:T(8,128)(2,1)} %bitcast.6), channel_id=1, source_target_pairs={{0,1},{1,0},{2,3},{3,2},{4,5},{5,4},{6,7},{7,6},{8,9},{9,8},{10,11... | collective-permute-start | bytes 393224 | tf_op jit(solution)/shard_map/ppermute | solution.py:23
  16.5 2.3 %copy-start.4 = (bf16[64,1024]{1,0:T(8,128)(2,1)}, bf16[64,1024]{1,0:T(8,128)(2,1)S(1)}, u32[]{:S(2)}) copy-start(bf16[64,1024]{1,0:T(8,128)(2,1)S(1)} %collective-permute-done.1.refs_2_) | copy-start | bytes 393220
  16.5 2.3 %collective-permute-start.2 = (bf16[64,1024]{1,0:T(8,128)(2,1)S(1)}, bf16[64,1024]{1,0:T(8,128)(2,1)S(1)}, u32[]{:S(2)}, u32[]{:S(2)}) collective-permute-start(bf16[64,1024]{1,0:T(8,128)(2,1)S(1)} %collective-permute-done.1.refs_2_), channel_id=1, source_target_pairs={{0,1},{1,0},{2,3},{3,2},{4,5},{5,4},{6,7},{7,6},{8,9},{9,8},{10,11... | collective-permute-start | bytes 393224 | tf_op jit(solution)/shard_map/ppermute | solution.py:23
  18.8 0.6 %copy-start.5 = (bf16[64,1024]{1,0:T(8,128)(2,1)}, bf16[64,1024]{1,0:T(8,128)(2,1)S(1)}, u32[]{:S(2)}) copy-start(bf16[64,1024]{1,0:T(8,128)(2,1)S(1)} %collective-permute-done.refs_1_) | copy-start | bytes 393220
  18.8 0.7 %copy-start.6 = (bf16[64,1024]{1,0:T(8,128)(2,1)}, bf16[64,1024]{1,0:T(8,128)(2,1)S(1)}, u32[]{:S(2)}) copy-start(bf16[64,1024]{1,0:T(8,128)(2,1)S(1)} %collective-permute-done.2.refs_3_) | copy-start | bytes 393220
  22.0 15.7 %collective-permute-start.3 = (bf16[80,128]{1,0:T(8,128)(2,1)}, bf16[80,128]{1,0:T(8,128)(2,1)S(1)}, u32[]{:S(2)}, u32[]{:S(2)}) collective-permute-start(bf16[80,128]{1,0:T(8,128)(2,1)} %shard_map.73), channel_id=1, source_target_pairs={{0,8},{4,12},{8,0},{12,4},{16,24},{20,28},{24,16},{28,20},{1,9},{5... | collective-permute-start | bytes 61448 | tf_op jit(solution)/shard_map/ppermute | solution.py:23
  23.8 4.1 %copy-start = (bf16[64,3584]{1,0:T(8,128)(2,1)}, bf16[64,3584]{1,0:T(8,128)(2,1)S(1)}, u32[]{:S(2)}) copy-start(bf16[64,3584]{1,0:T(8,128)(2,1)S(1)} %collective-permute-done.9.refs_0_) | copy-start | bytes 1376260
  23.8 10.3 %collective-permute-start.10 = (bf16[64,3584]{1,0:T(8,128)(2,1)S(1)}, bf16[64,3584]{1,0:T(8,128)(2,1)S(1)}, u32[]{:S(2)}, u32[]{:S(2)}) collective-permute-start(bf16[64,3584]{1,0:T(8,128)(2,1)S(1)} %collective-permute-done.9.refs_0_), channel_id=1, source_target_pairs={{0,1},{1,0},{2,3},{3,2},{4,5},{5,4},{6,7},{7,6},{8,9},{9,8},{10,11... | collective-permute-start | bytes 1376264 | tf_op jit(solution)/shard_map/ppermute | solution.py:23
  27.9 9.8 %copy-start.3 = (bf16[80,128]{1,0:T(8,128)(2,1)S(1)}, bf16[80,128]{1,0:T(8,128)(2,1)}, u32[]{:S(2)}) copy-start(bf16[80,128]{1,0:T(8,128)(2,1)} %shard_map.73) | copy-start | bytes 61444
  27.9 0.8 %copy-start.2 = (bf16[64,3584]{1,0:T(8,128)(2,1)}, bf16[64,3584]{1,0:T(8,128)(2,1)S(1)}, u32[]{:S(2)}) copy-start(bf16[64,3584]{1,0:T(8,128)(2,1)S(1)} %collective-permute-done.11.refs_1_) | copy-start | bytes 1376260
  34.1 0.8 %copy-start.1 = (bf16[64,3584]{1,0:T(8,128)(2,1)}, bf16[64,3584]{1,0:T(8,128)(2,1)S(1)}, u32[]{:S(2)}) copy-start(bf16[64,3584]{1,0:T(8,128)(2,1)S(1)} %collective-permute-done.10.refs_0_) | copy-start | bytes 1376260
  37.3 3.9 %collective-permute-start.12 = (bf16[64,128]{1,0:T(8,128)(2,1)}, bf16[64,128]{1,0:T(8,128)(2,1)S(1)}, u32[]{:S(2)}, u32[]{:S(2)}) collective-permute-start(bf16[64,128]{1,0:T(8,128)(2,1)} %shard_map.76), channel_id=1, source_target_pairs={{0,8},{4,12},{8,0},{12,4},{16,24},{20,28},{24,16},{28,20},{1,9},{5... | collective-permute-start | bytes 49160 | tf_op jit(solution)/shard_map/ppermute | solution.py:23
  37.7 6.9 %collective-permute-start.4 = (bf16[160,128]{1,0:T(8,128)(2,1)S(1)}, bf16[160,128]{1,0:T(8,128)(2,1)S(1)}, u32[]{:S(2)}, u32[]{:S(2)}) collective-permute-start(bf16[160,128]{1,0:T(8,128)(2,1)S(1)} %pad_maximum_fusion.4), channel_id=1, source_target_pairs={{0,16},{4,20},{8,24},{12,28},{16,0},{20,4},{24,8},{28,12},{1,17},{... | collective-permute-start | bytes 122888 | tf_op jit(solution)/shard_map/ppermute | solution.py:23
  42.0 5.2 %collective-permute-start.13 = (bf16[128,128]{1,0:T(8,128)(2,1)S(1)}, bf16[128,128]{1,0:T(8,128)(2,1)S(1)}, u32[]{:S(2)}, u32[]{:S(2)}) collective-permute-start(bf16[128,128]{1,0:T(8,128)(2,1)S(1)} %pad_maximum_fusion.5), channel_id=1, source_target_pairs={{0,16},{4,20},{8,24},{12,28},{16,0},{20,4},{24,8},{28,12},{1,17},{... | collective-permute-start | bytes 98312 | tf_op jit(solution)/shard_map/ppermute | solution.py:23
  44.6 5.1 %collective-permute-start.5 = (bf16[320,128]{1,0:T(8,128)(2,1)S(1)}, bf16[320,128]{1,0:T(8,128)(2,1)S(1)}, u32[]{:S(2)}, u32[]{:S(2)}) collective-permute-start(bf16[320,128]{1,0:T(8,128)(2,1)S(1)} %pad_maximum_fusion.2), channel_id=1, source_target_pairs={{0,4},{4,0},{8,12},{12,8},{16,20},{20,16},{24,28},{28,24},{1,5},{5... | collective-permute-start | bytes 245768 | tf_op jit(solution)/shard_map/ppermute | solution.py:23
  47.8 4.3 %collective-permute-start.14 = (bf16[256,128]{1,0:T(8,128)(2,1)S(1)}, bf16[256,128]{1,0:T(8,128)(2,1)S(1)}, u32[]{:S(2)}, u32[]{:S(2)}) collective-permute-start(bf16[256,128]{1,0:T(8,128)(2,1)S(1)} %pad_maximum_fusion.3), channel_id=1, source_target_pairs={{0,4},{4,0},{8,12},{12,8},{16,20},{20,16},{24,28},{28,24},{1,5},{5... | collective-permute-start | bytes 196616 | tf_op jit(solution)/shard_map/ppermute | solution.py:23
  49.7 6.4 %collective-permute-start.7 = (bf16[640,128]{1,0:T(8,128)(2,1)S(1)}, bf16[640,128]{1,0:T(8,128)(2,1)S(1)}, u32[]{:S(2)}, u32[]{:S(2)}) collective-permute-start(bf16[640,128]{1,0:T(8,128)(2,1)S(1)} %pad_maximum_fusion.refs_0_), channel_id=1, source_target_pairs={{0,2},{1,3},{2,0},{3,1},{4,6},{5,7},{6,4},{7,5},{8,10},{9,11},{10,... | collective-permute-start | bytes 491528 | tf_op jit(solution)/shard_map/ppermute | solution.py:23
  52.8 5.0 %collective-permute-start.16 = (bf16[512,128]{1,0:T(8,128)(2,1)S(1)}, bf16[512,128]{1,0:T(8,128)(2,1)S(1)}, u32[]{:S(2)}, u32[]{:S(2)}) collective-permute-start(bf16[512,128]{1,0:T(8,128)(2,1)S(1)} %pad_maximum_fusion.1.refs_4_), channel_id=1, source_target_pairs={{0,2},{1,3},{2,0},{3,1},{4,6},{5,7},{6,4},{7,5},{8,10},{9,11},{10,... | collective-permute-start | bytes 393224 | tf_op jit(solution)/shard_map/ppermute | solution.py:23
  54.4 3.5 %collective-permute-start.6 = (bf16[640,128]{1,0:T(8,128)(2,1)S(1)}, bf16[640,128]{1,0:T(8,128)(2,1)S(1)}, u32[]{:S(2)}, u32[]{:S(2)}) collective-permute-start(bf16[640,128]{1,0:T(8,128)(2,1)S(1)} %pad_maximum_fusion.refs_0_), channel_id=1, source_target_pairs={{0,1},{1,0},{2,3},{3,2},{4,5},{5,4},{6,7},{7,6},{8,9},{9,8},{10,11... | collective-permute-start | bytes 491528 | tf_op jit(solution)/shard_map/ppermute | solution.py:23
  56.1 1.8 %collective-permute-start.8 = (bf16[640,128]{1,0:T(8,128)(2,1)S(1)}, bf16[640,128]{1,0:T(8,128)(2,1)S(1)}, u32[]{:S(2)}, u32[]{:S(2)}) collective-permute-start(bf16[640,128]{1,0:T(8,128)(2,1)S(1)} %collective-permute-done.7.refs_2_), channel_id=1, source_target_pairs={{0,1},{1,0},{2,3},{3,2},{4,5},{5,4},{6,7},{7,6},{8,9},{9,8},{10,11... | collective-permute-start | bytes 491528 | tf_op jit(solution)/shard_map/ppermute | solution.py:23
  56.1 1.8 %collective-permute-start.15 = (bf16[512,128]{1,0:T(8,128)(2,1)S(1)}, bf16[512,128]{1,0:T(8,128)(2,1)S(1)}, u32[]{:S(2)}, u32[]{:S(2)}) collective-permute-start(bf16[512,128]{1,0:T(8,128)(2,1)S(1)} %pad_maximum_fusion.1.refs_4_), channel_id=1, source_target_pairs={{0,1},{1,0},{2,3},{3,2},{4,5},{5,4},{6,7},{7,6},{8,9},{9,8},{10,11... | collective-permute-start | bytes 393224 | tf_op jit(solution)/shard_map/ppermute | solution.py:23
  57.9 1.3 %collective-permute-start.17 = (bf16[512,128]{1,0:T(8,128)(2,1)S(1)}, bf16[512,128]{1,0:T(8,128)(2,1)S(1)}, u32[]{:S(2)}, u32[]{:S(2)}) collective-permute-start(bf16[512,128]{1,0:T(8,128)(2,1)S(1)} %collective-permute-done.16.refs_6_), channel_id=1, source_target_pairs={{0,1},{1,0},{2,3},{3,2},{4,5},{5,4},{6,7},{7,6},{8,9},{9,8},{10,11... | collective-permute-start | bytes 393224 | tf_op jit(solution)/shard_map/ppermute | solution.py:23

commit v2 on v1

--- a/solution.py
+++ b/solution.py
@@ -16,6 +16,8 @@
 CONTRACT_LAST = (((1,), (1,)), ((), ()))
 VMEM = pl.BlockSpec(memory_space=pltpu.VMEM)
 SMEM = pl.BlockSpec(memory_space=pltpu.SMEM)
+ANY = pl.BlockSpec(memory_space=pl.ANY)
+ROOM = pltpu.CompilerParams(vmem_limit_bytes=16 * 1024 * 1024)
 
 
 def swap(value, axis, bit):
@@ -27,47 +29,61 @@
     return [1 << k for k in range(count.bit_length() - 1)]
 
 
+def after(value, *others):
+    return lax.optimization_barrier((value, *others))[0]
+
+
 def gather_group(rows):
     bits = bits_of(lax.axis_size("dp"))
+    stages = [rows]
     for bit in bits[1:] + bits[:1]:
         rows = jnp.concatenate([rows, swap(rows, "dp", bit)], axis=0)
-    return rows
-
-
-def gather_shards(own):
-    shards = {0: own}
-    for bit in reversed(bits_of(lax.axis_size("fsdp"))):
-        shards.update({k ^ bit: swap(v, "fsdp", bit) for k, v in list(shards.items())})
-    return [shards[k] for k in range(len(shards))]
-
-
-def project_kernel(count, *refs):
-    total = refs[2 * count][...] if len(refs) > 2 * count + 1 else 0.0
-    for sketch, tokens in zip(refs[:count], refs[count : 2 * count]):
+        stages.append(rows)
+    return rows, stages[-2]
+
+
+def spread(value, bits):
+    held = {0: value}
+    for bit in reversed(bits):
+        held.update({k ^ bit: swap(v, "fsdp", bit) for k, v in list(held.items())})
+    return [held[k] for k in range(len(held))]
+
+
+def low_rank(sketches, which, tokens):
+    me = lax.axis_index("fsdp")
+    total = 0.0
+    for sketch, k in zip(sketches, which):
+        size = sketch.shape[1]
+        start = pl.multiple_of((me ^ k) * size, size)
         total += lax.dot_general(
-            sketch[...], tokens[...], CONTRACT_LAST, preferred_element_type=F32
-        )
+            sketch[...], tokens[:, pl.ds(start, size)], CONTRACT_LAST, preferred_element_type=F32
+        )
+    return total
+
+
+def project_kernel(which, *refs):
+    count = len(which)
+    total = low_rank(refs[:count], which, refs[count])
+    if len(refs) > count + 2:
+        total += refs[count + 1][...]
     refs[-1][...] = total.astype(refs[-1].dtype)
 
 
-def project(sketches, tokens, total, dtype):
-    operands = [*sketches, *tokens] + ([] if total is None else [total])
+def project(sketches, which, tokens, total, dtype):
+    operands = [*sketches, tokens] + ([] if total is None else [total])
     return pl.pallas_call(
-        functools.partial(project_kernel, len(sketches)),
-        out_shape=jax.ShapeDtypeStruct((sketches[0].shape[0], tokens[0].shape[0]), dtype),
+        functools.partial(project_kernel, which),
+        out_shape=jax.ShapeDtypeStruct((sketches[0].shape[0], tokens.shape[0]), dtype),
         in_specs=[VMEM] * len(operands),
         out_specs=VMEM,
+        compiler_params=ROOM,
     )(*operands)
 
 
-def errors_kernel(count, owned, *refs):
-    sketches, tokens = refs[:count], refs[count : 2 * count]
-    piece_of, owner_dp, owner_slot, out = refs[2 * count :]
-    total = 0.0
-    for sketch, part in zip(sketches, tokens):
-        total += lax.dot_general(
-            sketch[...], part[...], CONTRACT_LAST, preferred_element_type=F32
-        )
+def errors_kernel(which, owned, *refs):
+    count = len(which)
+    tokens, piece_of, owner_dp, owner_slot, _, out = refs[count:]
+    total = low_rank(refs[:count], which, tokens)
     width = total.shape[0]
     out[:width, :] = total.astype(BF16)
     piece = piece_of[...]
@@ -132,44 +148,39 @@
     token_rows = hidden_in.shape[0]
     width = sketch_in.shape[1]
     owned = count_dp // 2
-    me = lax.axis_index("fsdp")
-
-    def columns(tokens, k):
-        size = tokens.shape[1] // count_fsdp
-        return lax.dynamic_slice_in_dim(tokens, (me ^ k) * size, size, axis=1)
-
-    out_shards = gather_shards(sketch_out.T)
-    in_shards = gather_shards(sketch_in.T)
+    bits = bits_of(count_fsdp)
+    low, top = bits[:-1], bits[-1]
+    own_out, own_in = sketch_out.T, sketch_in.T
+    near_out = spread(own_out, low)
+    far_out = swap(own_out, "fsdp", top)
+    near_in = spread(own_in, low)
+    near = list(range(top))
+    inputs = project(near_in, near, hidden_in, None, F32)
+    far_in = swap(own_in, "fsdp", top)
+    out_shards = near_out + spread(after(far_out, inputs), low)
     errors = pl.pallas_call(
-        functools.partial(errors_kernel, count_fsdp, owned),
+        functools.partial(errors_kernel, list(range(count_fsdp)), owned),
         out_shape=jax.ShapeDtypeStruct((width + KEY_ROWS, token_rows), BF16),
-        in_specs=[VMEM] * (2 * count_fsdp + 1) + [SMEM] * 2,
+        in_specs=[VMEM] * (count_fsdp + 2) + [SMEM] * 2 + [ANY],
         out_specs=VMEM,
-    )(
-        *out_shards,
-        *[columns(out_grads, k) for k in range(count_fsdp)],
-        piece_of,
-        owner_dp,
-        owner_slot,
-    )
-    near = list(range(max(1, count_fsdp // 2)))
-    far = list(range(len(near), count_fsdp))
-    inputs = project(
-        [in_shards[k] for k in near], [columns(hidden_in, k) for k in near], None, F32
-    )
-    for k in far:
-        inputs = project(
-            [in_shards[k]], [columns(hidden_in, k)], inputs, BF16 if k == far[-1] else F32
-        )
-    all_errors = gather_shards(gather_group(errors))
-    all_inputs = gather_shards(gather_group(inputs))
+        compiler_params=ROOM,
+        cost_estimate=pl.CostEstimate(flops=30_000_000_000, bytes_accessed=60_000_000, transcendentals=0),
+    )(*out_shards, out_grads, piece_of, owner_dp, owner_slot, inputs)
+    group_errors, halfway = gather_group(errors)
+    far_in = spread(after(far_in, halfway), low)
+    for k, shard in enumerate(far_in):
+        last = k == len(far_in) - 1
+        inputs = project([shard], [top + k], hidden_in, inputs, BF16 if last else F32)
+    group_inputs, _ = gather_group(inputs)
+    all_errors = spread(group_errors, bits)
+    all_inputs = spread(group_inputs, bits)
     scale = 1.0 / math.sqrt(owned * count_dp * count_fsdp)
     return pl.pallas_call(
         functools.partial(gram_kernel, count_dp, owned * count_dp, scale),
         out_shape=jax.ShapeDtypeStruct((GR // count_dp, width * width // count_fsdp), F32),
         in_specs=[VMEM] * (2 * count_fsdp),
         out_specs=VMEM,
-        compiler_params=pltpu.CompilerParams(vmem_limit_bytes=24 * 1024 * 1024),
+        compiler_params=ROOM,
     )(*all_errors, *all_inputs)
 
 

time: 62.4 us -> 45 us (0.72)
  Pallas kernels: 13 us -> 6.47 us
  local copies, waits for them, and re-layouts: 8.47 us -> 2.06 us
  waiting for transfers between devices: 20.2 us -> 15 us
  starting transfers between devices: 18 us -> 21.2 us
  other arithmetic: 2.19 us -> 0.04 us
    pallas_call x4, Pallas kernels: 10.3 us -> 3.74 us  [the longest x3 2.71 us: project(): pl.pallas_call(functools.partial(project_kernel, which), out_shape=jax.Sh...]
    dynamic_slice x2 -> x0, local copies, waits for them, and re-layouts: 6.19 us -> none  [columns(): return lax.dynamic_slice_in_dim(tokens, (me ^ k) * size, size, axis=1)]
    ppermute x18, waiting for transfers between devices: 20.2 us -> 15 us  [swap(): return lax.ppermute(value, axis, [(i, i ^ bit) for i in range(count)])]
    ppermute x18, starting transfers between devices: 18 us -> 21.2 us  [swap(): return lax.ppermute(value, axis, [(i, i ^ bit) for i in range(count)])]
    concatenate x6, other arithmetic: 2.19 us -> 0.04 us  [gather_group(): rows = jnp.concatenate([rows, swap(rows, 'dp', bit)], axis=0)]
  transfers between devices with their start and end apart: 18 -> 18, of which waited for: 8 -> 13; matrix products, arithmetic and copies ran while one was open for 14% -> 0% of each run, Pallas kernels for 17% -> 7%
where the time goes in v2:
time: 45 us; the launch traced here: 44.8 us
  starting transfers between devices  21.2 us (47%)
  waiting for transfers between devices  15 us (33%)
  Pallas kernels  6.47 us (14%)
  local copies, waits for them, and re-layouts  2.06 us (5%)
    ppermute x18, starting transfers between devices, swap(): return lax.ppermute(value, axis, [(i, i ^ bit) for i in range(count)])  21.2 us
    ppermute x18, waiting for transfers between devices, swap(): return lax.ppermute(value, axis, [(i, i ^ bit) for i in range(count)])  15 us
    pallas_call x1, Pallas kernels, by_tokens(): pl.pallas_call(functools.partial(gram_kernel, count_dp, owned * count_dp,...  2.73 us
    pallas_call x3, Pallas kernels, project(): pl.pallas_call(functools.partial(project_kernel, which), out_shape=jax.Sh...  2.71 us
    unnamed x14, local copies, waits for them, and re-layouts  2.06 us
    pallas_call x1, Pallas kernels, by_tokens(): pl.pallas_call(functools.partial(errors_kernel, list(range(count_fsdp)),...  1.03 us
  transfers between devices with their start and end apart: 18, of which 13 were waited for; matrix products, arithmetic and copies ran while one was open for 0% of the time, Pallas kernels for 7%

profile of v2, /device:TPU:0, one launch (start us, length us, event | category | flops | bytes accessed | tf_op | source)
XLA Modules:
  0.0 44.8 jit_solution(1832823745257970712)
XLA Ops:
  0.0 0.0 copy-start.5
  0.0 0.0 copy-start.6
  0.0 0.0 copy-start.4
  0.0 0.5 %collective-permute-start.2 = (bf16[64,3584]{1,0:T(8,128)(2,1)}, bf16[64,3584]{1,0:T(8,128)(2,1)S(1)}, u32[]{:S(2)}, u32[]{:S(2)}) collective-permute-start(bf16[64,3584]{1,0:T(8,128)(2,1)} %bitcast.1.refs_0_), channel_id=1, source_target_pairs={{0,1},{1,0},{2,3},{3,2},{4,5},{5,4},{6,7},{7,6},{8,9},{9,8},{10,11... | collective-permute-start | bytes 1376264 | tf_op jit(solution)/shard_map/ppermute | solution.py:25
  0.5 2.6 %collective-permute-start.1 = (bf16[64,1024]{1,0:T(8,128)(2,1)}, bf16[64,1024]{1,0:T(8,128)(2,1)S(1)}, u32[]{:S(2)}, u32[]{:S(2)}) collective-permute-start(bf16[64,1024]{1,0:T(8,128)(2,1)} %bitcast.2), channel_id=1, source_target_pairs={{0,2},{1,3},{2,0},{3,1},{4,6},{5,7},{6,4},{7,5},{8,10},{9,11},{10,... | collective-permute-start | bytes 393224 | tf_op jit(solution)/shard_map/ppermute | solution.py:25
  3.1 0.2 collective-permute-start
  3.3 0.0 collective-permute-done.2.refs_1_
  3.3 0.0 copy-start
  3.3 2.0 %copy-done = bf16[128,14336]{1,0:T(8,128)(2,1)S(1)} copy-done((bf16[128,14336]{1,0:T(8,128)(2,1)S(1)}, bf16[128,14336]{1,0:T(8,128)(2,1)}, u32[]{:S(2)}) %copy-start) | copy-done | bytes 3670040
  5.3 0.0 copy-start.2
  5.3 0.0 copy-start.3
  5.3 1.9 %shard_map.73.refs_8_.refs_2_ = f32[64,128]{1,0:T(8,128)S(1)} custom-call(bf16[64,3584]{1,0:T(8,128)(2,1)} %bitcast.1.refs_0_, bf16[64,3584]{1,0:T(8,128)(2,1)S(1)} %collective-permute-done.2.refs_1_, bf16[128,14336]{1,0:T(8,128)(2,1)S(1)} %copy-done), custom_call_target="tpu_custom_call" | custom-call | tf_op jit(solution)/shard_map/pallas_call | solution.py:74
  7.2 0.0 copy-start.1
  7.2 0.2 collective-permute-done.1.refs_2_
  7.4 0.2 collective-permute-start.3
  7.6 1.6 %collective-permute-start.10 = (bf16[64,3584]{1,0:T(8,128)(2,1)}, bf16[64,3584]{1,0:T(8,128)(2,1)S(1)}, u32[]{:S(2)}, u32[]{:S(2)}) collective-permute-start(bf16[64,3584]{1,0:T(8,128)(2,1)} %bitcast.1.refs_0_), channel_id=1, source_target_pairs={{0,2},{1,3},{2,0},{3,1},{4,6},{5,7},{6,4},{7,5},{8,10},{9,11},{10,... | collective-permute-start | bytes 1376264 | tf_op jit(solution)/shard_map/ppermute | solution.py:25
  9.2 0.0 collective-permute-done.refs_1_
  9.2 0.0 collective-permute-done.3.refs_3_
  9.2 0.0 copy-done.5
  9.2 0.0 copy-done.6
  9.2 0.0 copy-done.4
  9.2 0.0 copy-done.2
  9.2 0.0 copy-done.3
  9.2 1.0 %shard_map.74 = bf16[80,128]{1,0:T(8,128)(2,1)S(1)} custom-call(bf16[64,1024]{1,0:T(8,128)(2,1)S(1)} %bitcast.4, bf16[64,1024]{1,0:T(8,128)(2,1)S(1)} %collective-permute-done.refs_1_, bf16[64,1024]{1,0:T(8,128)(2,1)S(1)} %collective-permute-done.1.refs_2_, bf16[64,1024]{1,0:T(8,128)(2,1)S(1)} %collective-permute-done.3.refs_3_, ...), custom_call_target="tpu_custom_call" | custom-call | flops 30000001024 | bytes 60000000 | tf_op jit(solution)/shard_map/pallas_call | solution.py:161
  10.3 1.6 %collective-permute-start.4 = (bf16[80,128]{1,0:T(8,128)(2,1)S(1)}, bf16[80,128]{1,0:T(8,128)(2,1)S(1)}, u32[]{:S(2)}, u32[]{:S(2)}) collective-permute-start(bf16[80,128]{1,0:T(8,128)(2,1)S(1)} %shard_map.74), channel_id=1, source_target_pairs={{0,8},{4,12},{8,0},{12,4},{16,24},{20,28},{24,16},{28,20},{1,9},{5... | collective-permute-start | bytes 61448 | tf_op jit(solution)/shard_map/ppermute | solution.py:25
  11.9 2.2 %collective-permute-done.4 = bf16[80,128]{1,0:T(8,128)(2,1)S(1)} collective-permute-done((bf16[80,128]{1,0:T(8,128)(2,1)S(1)}, bf16[80,128]{1,0:T(8,128)(2,1)S(1)}, u32[]{:S(2)}, u32[]{:S(2)}) %collective-permute-start.4) | collective-permute-done | bytes 20512 | tf_op jit(solution)/shard_map/ppermute | solution.py:25
  14.1 2.6 %collective-permute-start.5 = (bf16[160,128]{1,0:T(8,128)(2,1)S(1)}, bf16[160,128]{1,0:T(8,128)(2,1)S(1)}, u32[]{:S(2)}, u32[]{:S(2)}) collective-permute-start(bf16[160,128]{1,0:T(8,128)(2,1)S(1)} %pad_maximum_fusion.4), channel_id=1, source_target_pairs={{0,16},{4,20},{8,24},{12,28},{16,0},{20,4},{24,8},{28,12},{1,17},{... | collective-permute-start | bytes 122888 | tf_op jit(solution)/shard_map/ppermute | solution.py:25
  16.7 2.3 %collective-permute-done.5 = bf16[160,128]{1,0:T(8,128)(2,1)S(1)} collective-permute-done((bf16[160,128]{1,0:T(8,128)(2,1)S(1)}, bf16[160,128]{1,0:T(8,128)(2,1)S(1)}, u32[]{:S(2)}, u32[]{:S(2)}) %collective-permute-start.5) | collective-permute-done | bytes 40992 | tf_op jit(solution)/shard_map/ppermute | solution.py:25
  19.0 1.5 %collective-permute-done.10.refs_0_ = bf16[64,3584]{1,0:T(8,128)(2,1)S(1)} collective-permute-done((bf16[64,3584]{1,0:T(8,128)(2,1)}, bf16[64,3584]{1,0:T(8,128)(2,1)S(1)}, u32[]{:S(2)}, u32[]{:S(2)}) %collective-permute-start.10) | collective-permute-done | bytes 458784 | tf_op jit(solution)/shard_map/ppermute | solution.py:25
  20.6 0.0 collective-permute-start.11
  20.6 0.0 copy-done.1
  20.6 0.4 shard_map.75.refs_2_
  21.0 1.4 %collective-permute-done.11.refs_0_ = bf16[64,3584]{1,0:T(8,128)(2,1)S(1)} collective-permute-done((bf16[64,3584]{1,0:T(8,128)(2,1)S(1)}, bf16[64,3584]{1,0:T(8,128)(2,1)S(1)}, u32[]{:S(2)}, u32[]{:S(2)}) %collective-permute-start.11) | collective-permute-done | bytes 458784 | tf_op jit(solution)/shard_map/ppermute | solution.py:25
  22.4 0.4 shard_map.76
  22.8 1.9 %collective-permute-start.12 = (bf16[64,128]{1,0:T(8,128)(2,1)S(1)}, bf16[64,128]{1,0:T(8,128)(2,1)S(1)}, u32[]{:S(2)}, u32[]{:S(2)}) collective-permute-start(bf16[64,128]{1,0:T(8,128)(2,1)S(1)} %shard_map.76), channel_id=1, source_target_pairs={{0,8},{4,12},{8,0},{12,4},{16,24},{20,28},{24,16},{28,20},{1,9},{5... | collective-permute-start | bytes 49160 | tf_op jit(solution)/shard_map/ppermute | solution.py:25
  24.7 1.9 %collective-permute-done.12 = bf16[64,128]{1,0:T(8,128)(2,1)S(1)} collective-permute-done((bf16[64,128]{1,0:T(8,128)(2,1)S(1)}, bf16[64,128]{1,0:T(8,128)(2,1)S(1)}, u32[]{:S(2)}, u32[]{:S(2)}) %collective-permute-start.12) | collective-permute-done | bytes 16416 | tf_op jit(solution)/shard_map/ppermute | solution.py:25
  26.6 2.8 %collective-permute-start.13 = (bf16[128,128]{1,0:T(8,128)(2,1)S(1)}, bf16[128,128]{1,0:T(8,128)(2,1)S(1)}, u32[]{:S(2)}, u32[]{:S(2)}) collective-permute-start(bf16[128,128]{1,0:T(8,128)(2,1)S(1)} %pad_maximum_fusion.5), channel_id=1, source_target_pairs={{0,16},{4,20},{8,24},{12,28},{16,0},{20,4},{24,8},{28,12},{1,17},{... | collective-permute-start | bytes 98312 | tf_op jit(solution)/shard_map/ppermute | solution.py:25
  29.4 1.5 %collective-permute-start.6 = (bf16[320,128]{1,0:T(8,128)(2,1)S(1)}, bf16[320,128]{1,0:T(8,128)(2,1)S(1)}, u32[]{:S(2)}, u32[]{:S(2)}) collective-permute-start(bf16[320,128]{1,0:T(8,128)(2,1)S(1)} %pad_maximum_fusion.2), channel_id=1, source_target_pairs={{0,4},{4,0},{8,12},{12,8},{16,20},{20,16},{24,28},{28,24},{1,5},{5... | collective-permute-start | bytes 245768 | tf_op jit(solution)/shard_map/ppermute | solution.py:25
  31.0 0.5 %collective-permute-done.13 = bf16[128,128]{1,0:T(8,128)(2,1)S(1)} collective-permute-done((bf16[128,128]{1,0:T(8,128)(2,1)S(1)}, bf16[128,128]{1,0:T(8,128)(2,1)S(1)}, u32[]{:S(2)}, u32[]{:S(2)}) %collective-permute-start.13) | collective-permute-done | bytes 32800 | tf_op jit(solution)/shard_map/ppermute | solution.py:25
  31.4 1.8 %collective-permute-start.14 = (bf16[256,128]{1,0:T(8,128)(2,1)S(1)}, bf16[256,128]{1,0:T(8,128)(2,1)S(1)}, u32[]{:S(2)}, u32[]{:S(2)}) collective-permute-start(bf16[256,128]{1,0:T(8,128)(2,1)S(1)} %pad_maximum_fusion.3), channel_id=1, source_target_pairs={{0,4},{4,0},{8,12},{12,8},{16,20},{20,16},{24,28},{28,24},{1,5},{5... | collective-permute-start | bytes 196616 | tf_op jit(solution)/shard_map/ppermute | solution.py:25
  33.2 0.7 %collective-permute-done.6 = bf16[320,128]{1,0:T(8,128)(2,1)S(1)} collective-permute-done((bf16[320,128]{1,0:T(8,128)(2,1)S(1)}, bf16[320,128]{1,0:T(8,128)(2,1)S(1)}, u32[]{:S(2)}, u32[]{:S(2)}) %collective-permute-start.6) | collective-permute-done | bytes 81952 | tf_op jit(solution)/shard_map/ppermute | solution.py:25
  33.9 1.6 %collective-permute-start.8 = (bf16[640,128]{1,0:T(8,128)(2,1)S(1)}, bf16[640,128]{1,0:T(8,128)(2,1)S(1)}, u32[]{:S(2)}, u32[]{:S(2)}) collective-permute-start(bf16[640,128]{1,0:T(8,128)(2,1)S(1)} %pad_maximum_fusion.refs_0_), channel_id=1, source_target_pairs={{0,2},{1,3},{2,0},{3,1},{4,6},{5,7},{6,4},{7,5},{8,10},{9,11},{10,... | collective-permute-start | bytes 491528 | tf_op jit(solution)/shard_map/ppermute | solution.py:25
  35.5 0.2 collective-permute-done.14
  35.7 1.8 %collective-permute-start.16 = (bf16[512,128]{1,0:T(8,128)(2,1)S(1)}, bf16[512,128]{1,0:T(8,128)(2,1)S(1)}, u32[]{:S(2)}, u32[]{:S(2)}) collective-permute-start(bf16[512,128]{1,0:T(8,128)(2,1)S(1)} %pad_maximum_fusion.1.refs_4_), channel_id=1, source_target_pairs={{0,2},{1,3},{2,0},{3,1},{4,6},{5,7},{6,4},{7,5},{8,10},{9,11},{10,... | collective-permute-start | bytes 393224 | tf_op jit(solution)/shard_map/ppermute | solution.py:25
  37.5 0.0 collective-permute-start.7
  37.5 1.8 %collective-permute-done.8.refs_2_ = bf16[640,128]{1,0:T(8,128)(2,1)S(1)} collective-permute-done((bf16[640,128]{1,0:T(8,128)(2,1)S(1)}, bf16[640,128]{1,0:T(8,128)(2,1)S(1)}, u32[]{:S(2)}, u32[]{:S(2)}) %collective-permute-start.8) | collective-permute-done | bytes 163872 | tf_op jit(solution)/shard_map/ppermute | solution.py:25
  39.3 0.0 collective-permute-start.9
  39.3 0.5 %collective-permute-start.15 = (bf16[512,128]{1,0:T(8,128)(2,1)S(1)}, bf16[512,128]{1,0:T(8,128)(2,1)S(1)}, u32[]{:S(2)}, u32[]{:S(2)}) collective-permute-start(bf16[512,128]{1,0:T(8,128)(2,1)S(1)} %pad_maximum_fusion.1.refs_4_), channel_id=1, source_target_pairs={{0,1},{1,0},{2,3},{3,2},{4,5},{5,4},{6,7},{7,6},{8,9},{9,8},{10,11... | collective-permute-start | bytes 393224 | tf_op jit(solution)/shard_map/ppermute | solution.py:25
  39.8 0.9 %collective-permute-done.16.refs_6_ = bf16[512,128]{1,0:T(8,128)(2,1)S(1)} collective-permute-done((bf16[512,128]{1,0:T(8,128)(2,1)S(1)}, bf16[512,128]{1,0:T(8,128)(2,1)S(1)}, u32[]{:S(2)}, u32[]{:S(2)}) %collective-permute-start.16) | collective-permute-done | bytes 131104 | tf_op jit(solution)/shard_map/ppermute | solution.py:25
  40.7 0.0 collective-permute-start.17
  40.7 0.0 collective-permute-done.7.refs_1_
  40.7 0.0 collective-permute-done.9.refs_3_
  40.8 0.1 collective-permute-done.15.refs_5_
  40.9 1.2 %collective-permute-done.17.refs_7_ = bf16[512,128]{1,0:T(8,128)(2,1)S(1)} collective-permute-done((bf16[512,128]{1,0:T(8,128)(2,1)S(1)}, bf16[512,128]{1,0:T(8,128)(2,1)S(1)}, u32[]{:S(2)}, u32[]{:S(2)}) %collective-permute-start.17) | collective-permute-done | bytes 131104 | tf_op jit(solution)/shard_map/ppermute | solution.py:25
  42.1 2.7 %shard_map.77 = f32[24,1024]{1,0:T(8,128)} custom-call(bf16[640,128]{1,0:T(8,128)(2,1)S(1)} %pad_maximum_fusion.refs_0_, bf16[640,128]{1,0:T(8,128)(2,1)S(1)} %collective-permute-done.7.refs_1_, bf16[640,128]{1,0:T(8,128)(2,1)S(1)} %collective-permute-done.8.refs_2_, bf16[640,128]{1,0:T(8,128)(2,1)S(1)} %collective-permute-done.9.refs_3_, ...), custom_call_target="tpu_custom_call" | custom-call | tf_op jit(solution)/shard_map/pallas_call | solution.py:178
  (6 shorter events, 0.0 us)
Async XLA Ops:
  0.0 9.2 %copy-start.5 = (s32[1,8]{1,0:T(1,128)S(1)}, s32[1,8]{1,0:T(1,128)}, u32[]{:S(2)}) copy-start(s32[1,8]{1,0:T(1,128)} %refs_6_.1) | copy-start | bytes 100
  0.0 9.2 %copy-start.6 = (s32[1,8]{1,0:T(1,128)S(1)}, s32[1,8]{1,0:T(1,128)}, u32[]{:S(2)}) copy-start(s32[1,8]{1,0:T(1,128)} %refs_7_.1) | copy-start | bytes 100
  0.0 9.2 %copy-start.4 = (s32[1,128]{1,0:T(1,128)S(1)}, s32[1,128]{1,0:T(1,128)}, u32[]{:S(2)}) copy-start(s32[1,128]{1,0:T(1,128)} %refs_5_.1) | copy-start | bytes 1540
  0.0 3.3 %collective-permute-start.2 = (bf16[64,3584]{1,0:T(8,128)(2,1)}, bf16[64,3584]{1,0:T(8,128)(2,1)S(1)}, u32[]{:S(2)}, u32[]{:S(2)}) collective-permute-start(bf16[64,3584]{1,0:T(8,128)(2,1)} %bitcast.1.refs_0_), channel_id=1, source_target_pairs={{0,1},{1,0},{2,3},{3,2},{4,5},{5,4},{6,7},{7,6},{8,9},{9,8},{10,11... | collective-permute-start | bytes 1376264 | tf_op jit(solution)/shard_map/ppermute | solution.py:25
  0.5 6.9 %collective-permute-start.1 = (bf16[64,1024]{1,0:T(8,128)(2,1)}, bf16[64,1024]{1,0:T(8,128)(2,1)S(1)}, u32[]{:S(2)}, u32[]{:S(2)}) collective-permute-start(bf16[64,1024]{1,0:T(8,128)(2,1)} %bitcast.2), channel_id=1, source_target_pairs={{0,2},{1,3},{2,0},{3,1},{4,6},{5,7},{6,4},{7,5},{8,10},{9,11},{10,... | collective-permute-start | bytes 393224 | tf_op jit(solution)/shard_map/ppermute | solution.py:25
  3.1 6.1 %collective-permute-start = (bf16[64,1024]{1,0:T(8,128)(2,1)}, bf16[64,1024]{1,0:T(8,128)(2,1)S(1)}, u32[]{:S(2)}, u32[]{:S(2)}) collective-permute-start(bf16[64,1024]{1,0:T(8,128)(2,1)} %bitcast.3), channel_id=1, source_target_pairs={{0,1},{1,0},{2,3},{3,2},{4,5},{5,4},{6,7},{7,6},{8,9},{9,8},{10,11... | collective-permute-start | bytes 393224 | tf_op jit(solution)/shard_map/ppermute | solution.py:25
  3.3 2.0 %copy-start = (bf16[128,14336]{1,0:T(8,128)(2,1)S(1)}, bf16[128,14336]{1,0:T(8,128)(2,1)}, u32[]{:S(2)}) copy-start(bf16[128,14336]{1,0:T(8,128)(2,1)} %refs_1_.3) | copy-start | bytes 11010052
  5.3 3.9 %copy-start.2 = (bf16[128,4096]{1,0:T(8,128)(2,1)S(1)}, bf16[128,4096]{1,0:T(8,128)(2,1)}, u32[]{:S(2)}) copy-start(bf16[128,4096]{1,0:T(8,128)(2,1)} %refs_4_.1) | copy-start | bytes 3145732
  5.3 3.9 %copy-start.3 = (bf16[1024,64]{0,1:T(8,128)(2,1)S(1)}, bf16[1024,64]{0,1:T(8,128)(2,1)}, u32[]{:S(2)}) copy-start(bf16[1024,64]{0,1:T(8,128)(2,1)} %param.13) | copy-start | bytes 393220
  7.2 13.4 %copy-start.1 = (bf16[128,14336]{1,0:T(8,128)(2,1)S(1)}, bf16[128,14336]{1,0:T(8,128)(2,1)}, u32[]{:S(2)}) copy-start(bf16[128,14336]{1,0:T(8,128)(2,1)} %refs_1_.3) | copy-start | bytes 11010052
  7.4 1.8 %collective-permute-start.3 = (bf16[64,1024]{1,0:T(8,128)(2,1)S(1)}, bf16[64,1024]{1,0:T(8,128)(2,1)S(1)}, u32[]{:S(2)}, u32[]{:S(2)}) collective-permute-start(bf16[64,1024]{1,0:T(8,128)(2,1)S(1)} %collective-permute-done.1.refs_2_), channel_id=1, source_target_pairs={{0,1},{1,0},{2,3},{3,2},{4,5},{5,4},{6,7},{7,6},{8,9},{9,8},{10,11... | collective-permute-start | bytes 393224 | tf_op jit(solution)/shard_map/ppermute | solution.py:25
  7.6 12.9 %collective-permute-start.10 = (bf16[64,3584]{1,0:T(8,128)(2,1)}, bf16[64,3584]{1,0:T(8,128)(2,1)S(1)}, u32[]{:S(2)}, u32[]{:S(2)}) collective-permute-start(bf16[64,3584]{1,0:T(8,128)(2,1)} %bitcast.1.refs_0_), channel_id=1, source_target_pairs={{0,2},{1,3},{2,0},{3,1},{4,6},{5,7},{6,4},{7,5},{8,10},{9,11},{10,... | collective-permute-start | bytes 1376264 | tf_op jit(solution)/shard_map/ppermute | solution.py:25
  10.3 3.8 %collective-permute-start.4 = (bf16[80,128]{1,0:T(8,128)(2,1)S(1)}, bf16[80,128]{1,0:T(8,128)(2,1)S(1)}, u32[]{:S(2)}, u32[]{:S(2)}) collective-permute-start(bf16[80,128]{1,0:T(8,128)(2,1)S(1)} %shard_map.74), channel_id=1, source_target_pairs={{0,8},{4,12},{8,0},{12,4},{16,24},{20,28},{24,16},{28,20},{1,9},{5... | collective-permute-start | bytes 61448 | tf_op jit(solution)/shard_map/ppermute | solution.py:25
  14.1 4.9 %collective-permute-start.5 = (bf16[160,128]{1,0:T(8,128)(2,1)S(1)}, bf16[160,128]{1,0:T(8,128)(2,1)S(1)}, u32[]{:S(2)}, u32[]{:S(2)}) collective-permute-start(bf16[160,128]{1,0:T(8,128)(2,1)S(1)} %pad_maximum_fusion.4), channel_id=1, source_target_pairs={{0,16},{4,20},{8,24},{12,28},{16,0},{20,4},{24,8},{28,12},{1,17},{... | collective-permute-start | bytes 122888 | tf_op jit(solution)/shard_map/ppermute | solution.py:25
  20.6 1.8 %collective-permute-start.11 = (bf16[64,3584]{1,0:T(8,128)(2,1)S(1)}, bf16[64,3584]{1,0:T(8,128)(2,1)S(1)}, u32[]{:S(2)}, u32[]{:S(2)}) collective-permute-start(bf16[64,3584]{1,0:T(8,128)(2,1)S(1)} %collective-permute-done.10.refs_0_), channel_id=1, source_target_pairs={{0,1},{1,0},{2,3},{3,2},{4,5},{5,4},{6,7},{7,6},{8,9},{9,8},{10,11... | collective-permute-start | bytes 1376264 | tf_op jit(solution)/shard_map/ppermute | solution.py:25
  22.8 3.8 %collective-permute-start.12 = (bf16[64,128]{1,0:T(8,128)(2,1)S(1)}, bf16[64,128]{1,0:T(8,128)(2,1)S(1)}, u32[]{:S(2)}, u32[]{:S(2)}) collective-permute-start(bf16[64,128]{1,0:T(8,128)(2,1)S(1)} %shard_map.76), channel_id=1, source_target_pairs={{0,8},{4,12},{8,0},{12,4},{16,24},{20,28},{24,16},{28,20},{1,9},{5... | collective-permute-start | bytes 49160 | tf_op jit(solution)/shard_map/ppermute | solution.py:25
  26.6 4.8 %collective-permute-start.13 = (bf16[128,128]{1,0:T(8,128)(2,1)S(1)}, bf16[128,128]{1,0:T(8,128)(2,1)S(1)}, u32[]{:S(2)}, u32[]{:S(2)}) collective-permute-start(bf16[128,128]{1,0:T(8,128)(2,1)S(1)} %pad_maximum_fusion.5), channel_id=1, source_target_pairs={{0,16},{4,20},{8,24},{12,28},{16,0},{20,4},{24,8},{28,12},{1,17},{... | collective-permute-start | bytes 98312 | tf_op jit(solution)/shard_map/ppermute | solution.py:25
  29.4 4.4 %collective-permute-start.6 = (bf16[320,128]{1,0:T(8,128)(2,1)S(1)}, bf16[320,128]{1,0:T(8,128)(2,1)S(1)}, u32[]{:S(2)}, u32[]{:S(2)}) collective-permute-start(bf16[320,128]{1,0:T(8,128)(2,1)S(1)} %pad_maximum_fusion.2), channel_id=1, source_target_pairs={{0,4},{4,0},{8,12},{12,8},{16,20},{20,16},{24,28},{28,24},{1,5},{5... | collective-permute-start | bytes 245768 | tf_op jit(solution)/shard_map/ppermute | solution.py:25
  31.4 4.3 %collective-permute-start.14 = (bf16[256,128]{1,0:T(8,128)(2,1)S(1)}, bf16[256,128]{1,0:T(8,128)(2,1)S(1)}, u32[]{:S(2)}, u32[]{:S(2)}) collective-permute-start(bf16[256,128]{1,0:T(8,128)(2,1)S(1)} %pad_maximum_fusion.3), channel_id=1, source_target_pairs={{0,4},{4,0},{8,12},{12,8},{16,20},{20,16},{24,28},{28,24},{1,5},{5... | collective-permute-start | bytes 196616 | tf_op jit(solution)/shard_map/ppermute | solution.py:25
  33.9 5.4 %collective-permute-start.8 = (bf16[640,128]{1,0:T(8,128)(2,1)S(1)}, bf16[640,128]{1,0:T(8,128)(2,1)S(1)}, u32[]{:S(2)}, u32[]{:S(2)}) collective-permute-start(bf16[640,128]{1,0:T(8,128)(2,1)S(1)} %pad_maximum_fusion.refs_0_), channel_id=1, source_target_pairs={{0,2},{1,3},{2,0},{3,1},{4,6},{5,7},{6,4},{7,5},{8,10},{9,11},{10,... | collective-permute-start | bytes 491528 | tf_op jit(solution)/shard_map/ppermute | solution.py:25
  35.7 5.0 %collective-permute-start.16 = (bf16[512,128]{1,0:T(8,128)(2,1)S(1)}, bf16[512,128]{1,0:T(8,128)(2,1)S(1)}, u32[]{:S(2)}, u32[]{:S(2)}) collective-permute-start(bf16[512,128]{1,0:T(8,128)(2,1)S(1)} %pad_maximum_fusion.1.refs_4_), channel_id=1, source_target_pairs={{0,2},{1,3},{2,0},{3,1},{4,6},{5,7},{6,4},{7,5},{8,10},{9,11},{10,... | collective-permute-start | bytes 393224 | tf_op jit(solution)/shard_map/ppermute | solution.py:25
  37.5 3.2 %collective-permute-start.7 = (bf16[640,128]{1,0:T(8,128)(2,1)S(1)}, bf16[640,128]{1,0:T(8,128)(2,1)S(1)}, u32[]{:S(2)}, u32[]{:S(2)}) collective-permute-start(bf16[640,128]{1,0:T(8,128)(2,1)S(1)} %pad_maximum_fusion.refs_0_), channel_id=1, source_target_pairs={{0,1},{1,0},{2,3},{3,2},{4,5},{5,4},{6,7},{7,6},{8,9},{9,8},{10,11... | collective-permute-start | bytes 491528 | tf_op jit(solution)/shard_map/ppermute | solution.py:25
  39.3 1.5 %collective-permute-start.9 = (bf16[640,128]{1,0:T(8,128)(2,1)S(1)}, bf16[640,128]{1,0:T(8,128)(2,1)S(1)}, u32[]{:S(2)}, u32[]{:S(2)}) collective-permute-start(bf16[640,128]{1,0:T(8,128)(2,1)S(1)} %collective-permute-done.8.refs_2_), channel_id=1, source_target_pairs={{0,1},{1,0},{2,3},{3,2},{4,5},{5,4},{6,7},{7,6},{8,9},{9,8},{10,11... | collective-permute-start | bytes 491528 | tf_op jit(solution)/shard_map/ppermute | solution.py:25
  39.3 1.6 %collective-permute-start.15 = (bf16[512,128]{1,0:T(8,128)(2,1)S(1)}, bf16[512,128]{1,0:T(8,128)(2,1)S(1)}, u32[]{:S(2)}, u32[]{:S(2)}) collective-permute-start(bf16[512,128]{1,0:T(8,128)(2,1)S(1)} %pad_maximum_fusion.1.refs_4_), channel_id=1, source_target_pairs={{0,1},{1,0},{2,3},{3,2},{4,5},{5,4},{6,7},{7,6},{8,9},{9,8},{10,11... | collective-permute-start | bytes 393224 | tf_op jit(solution)/shard_map/ppermute | solution.py:25
  40.7 1.3 %collective-permute-start.17 = (bf16[512,128]{1,0:T(8,128)(2,1)S(1)}, bf16[512,128]{1,0:T(8,128)(2,1)S(1)}, u32[]{:S(2)}, u32[]{:S(2)}) collective-permute-start(bf16[512,128]{1,0:T(8,128)(2,1)S(1)} %collective-permute-done.16.refs_6_), channel_id=1, source_target_pairs={{0,1},{1,0},{2,3},{3,2},{4,5},{5,4},{6,7},{7,6},{8,9},{9,8},{10,11... | collective-permute-start | bytes 393224 | tf_op jit(solution)/shard_map/ppermute | solution.py:25

commit v3 on v2

--- a/solution.py
+++ b/solution.py
@@ -12,11 +12,17 @@
 GR = 192
 BF16 = jnp.bfloat16
 F32 = jnp.float32
-KEY_ROWS = 16
+BOTH = ("dp", "fsdp")
 CONTRACT_LAST = (((1,), (1,)), ((), ()))
 VMEM = pl.BlockSpec(memory_space=pltpu.VMEM)
 SMEM = pl.BlockSpec(memory_space=pltpu.SMEM)
 ANY = pl.BlockSpec(memory_space=pl.ANY)
+ERRORS_COST = pl.CostEstimate(
+    flops=1_500_000_000, bytes_accessed=1_000_000, transcendentals=0
+)
+PICKED_COST = pl.CostEstimate(
+    flops=2_000_000_000, bytes_accessed=1_000_000, transcendentals=0
+)
 ROOM = pltpu.CompilerParams(vmem_limit_bytes=16 * 1024 * 1024)
 
 
@@ -33,13 +39,8 @@
     return lax.optimization_barrier((value, *others))[0]
 
 
-def gather_group(rows):
-    bits = bits_of(lax.axis_size("dp"))
-    stages = [rows]
-    for bit in bits[1:] + bits[:1]:
-        rows = jnp.concatenate([rows, swap(rows, "dp", bit)], axis=0)
-        stages.append(rows)
-    return rows, stages[-2]
+def widen(rows, axis, bit):
+    return jnp.concatenate([rows, swap(rows, axis, bit)], axis=0)
 
 
 def spread(value, bits):
@@ -61,72 +62,92 @@
     return total
 
 
+def near_kernel(which, *refs):
+    refs[-1][...] = low_rank(refs[: len(which)], which, refs[-2])
+
+
 def project_kernel(which, *refs):
     count = len(which)
-    total = low_rank(refs[:count], which, refs[count])
-    if len(refs) > count + 2:
-        total += refs[count + 1][...]
-    refs[-1][...] = total.astype(refs[-1].dtype)
-
-
-def project(sketches, which, tokens, total, dtype):
-    operands = [*sketches, tokens] + ([] if total is None else [total])
-    return pl.pallas_call(
-        functools.partial(project_kernel, which),
-        out_shape=jax.ShapeDtypeStruct((sketches[0].shape[0], tokens.shape[0]), dtype),
-        in_specs=[VMEM] * len(operands),
-        out_specs=VMEM,
-        compiler_params=ROOM,
-    )(*operands)
-
-
-def errors_kernel(which, owned, *refs):
-    count = len(which)
-    tokens, piece_of, owner_dp, owner_slot, _, out = refs[count:]
-    total = low_rank(refs[:count], which, tokens)
-    width = total.shape[0]
-    out[:width, :] = total.astype(BF16)
+    tokens, total, out = refs[count:]
+    out[...] = low_rank(refs[:count], which, tokens) + total[...]
+
+
+def keys_kernel(owned, piece_of, owner_dp, owner_slot, _, out):
     piece = piece_of[...]
     key = jnp.zeros(piece.shape, jnp.int32)
     for p in range(owner_dp.shape[1]):
         key = jnp.where(piece == p, owner_dp[0, p] * owned + owner_slot[0, p], key)
-    key = jnp.broadcast_to(key.astype(F32), (KEY_ROWS, key.shape[1]))
-    out[width:, :] = key.astype(BF16)
-
-
-def gram_kernel(count_dp, group_examples, scale, *refs):
-    groups = len(refs) // 2
-    errors, inputs, out = refs[:groups], refs[groups : 2 * groups], refs[-1]
+    out[...] = jnp.broadcast_to(key.astype(F32), out.shape).astype(BF16)
+
+
+def message_kernel(which, mine, lead, *refs):
+    count = len(which)
+    tokens, total, keys, out = refs[count:]
+    rows = (low_rank(refs[:count], which, tokens) + total[...]).astype(BF16)
+    shared = jnp.concatenate([rows[:lead, :], keys[lead:, :]], axis=0)
+    parts = rows.shape[0] // mine
+    for k in range(out.shape[0]):
+        f = k % parts
+        out[k, :mine, :] = rows[f * mine : (f + 1) * mine, :]
+        out[k, mine:, :] = shared
+
+
+def call(kernel, operands, outputs, specs=None, cost=None):
+    return pl.pallas_call(
+        kernel,
+        out_shape=outputs,
+        in_specs=specs or [VMEM] * len(operands),
+        out_specs=VMEM,
+        compiler_params=ROOM,
+        cost_estimate=cost,
+    )(*operands)
+
+
+def errors_kernel(which, *refs):
+    count = len(which)
+    refs[-1][...] = low_rank(refs[:count], which, refs[count]).astype(BF16)
+
+
+def picked_kernel(*refs):
+    out = refs[-1]
+    rows, count = out.shape[0], out.shape[1] // refs[0].shape[1]
+    width = len(refs[:-1]) * refs[0].shape[0] // count
+    column = lax.axis_index("dp") * rows + lax.broadcasted_iota(jnp.int32, (rows, width), 0)
+    at = lax.broadcasted_iota(jnp.int32, (rows, width), 1)
+    pick = (at == column % width).astype(F32).astype(BF16)
+    err = jnp.concatenate(
+        [ref[k : k + width, :] for ref in refs[:-1] for k in range(0, ref.shape[0], width)], axis=1
+    )
+    out[...] = jnp.dot(pick, err, preferred_element_type=F32)
+
+
+def gram_kernel(order, lead, group_examples, scale, *refs):
+    errors, picked, messages, out = refs[:-3], refs[-3], refs[-2], refs[-1]
+    count_fsdp, count_dp = len(errors), len(order)
     rows_here, columns_here = out.shape
-    width = inputs[0].shape[0] // count_dp
+    width = errors[0].shape[0] // count_dp
     mine = columns_here // width
-    high = width + KEY_ROWS
-    start = pl.multiple_of(lax.axis_index("fsdp") * mine, mine)
-    place = (rows_here, width)
-    column = lax.axis_index("dp") * rows_here + lax.broadcasted_iota(jnp.int32, place, 0)
-    at = lax.broadcasted_iota(jnp.int32, place, 1)
-    pick_in = (at == column // width).astype(F32).astype(BF16)
-    pick_out = (at == column % width).astype(F32).astype(BF16)
+    size = messages.shape[1]
+    d, f = lax.axis_index("dp"), lax.axis_index("fsdp")
+    place = (rows_here, size - mine)
+    column = d * rows_here + lax.broadcasted_iota(jnp.int32, place, 0)
+    pick_in = (lax.broadcasted_iota(jnp.int32, place, 1) == column // width).astype(F32).astype(BF16)
     wide, narrow = [], []
-    for e_ref, i_ref in zip(errors, inputs):
-        err = jnp.concatenate([e_ref[k * high : k * high + width, :] for k in range(count_dp)], axis=1)
-        key = jnp.concatenate(
-            [e_ref[k * high + width : (k + 1) * high, :] for k in range(count_dp)], axis=1
+    for g, e_ref in enumerate(errors):
+        places = [(d ^ k) * count_fsdp + (f ^ g) for k in order]
+        err = jnp.concatenate([e_ref[k * width : (k + 1) * width, :] for k in range(count_dp)], axis=1)
+        here = jnp.concatenate([messages[k, :mine, :] for k in places], axis=1)
+        shared = jnp.concatenate([messages[k, mine:, :] for k in places], axis=1)
+        key = shared.astype(F32)[lead : lead + 1, :]
+        tokens = key.shape[1]
+        example = lax.broadcasted_iota(jnp.int32, (group_examples, tokens), 0).astype(F32)
+        member = (example == key).astype(F32).astype(BF16)
+        spread_rows = jnp.concatenate([member * here[i : i + 1, :] for i in range(mine)], axis=0)
+        wide.append(
+            lax.dot_general(spread_rows, err, CONTRACT_LAST, preferred_element_type=F32).astype(BF16)
         )
-        key = key.astype(F32)[:1, :]
-        low = jnp.concatenate([i_ref[k * width : (k + 1) * width, :] for k in range(count_dp)], axis=1)
-        here = jnp.concatenate(
-            [i_ref[pl.ds(k * width + start, mine), :] for k in range(count_dp)], axis=1
-        )
-        example = lax.broadcasted_iota(jnp.int32, (group_examples, key.shape[1]), 0).astype(F32)
-        member = (example == key).astype(F32).astype(BF16)
-        spread = jnp.concatenate([member * here[i : i + 1, :] for i in range(mine)], axis=0)
-        wide.append(
-            lax.dot_general(spread, err, CONTRACT_LAST, preferred_element_type=F32).astype(BF16)
-        )
-        product = jnp.dot(pick_in, low, preferred_element_type=F32) * jnp.dot(
-            pick_out, err, preferred_element_type=F32
-        )
+        product = jnp.dot(pick_in, shared, preferred_element_type=F32)
+        product = product * picked[:, g * tokens : (g + 1) * tokens]
         upper = product.astype(BF16)
         lower = (product - upper.astype(F32)).astype(BF16)
         part = lax.dot_general(upper, member, CONTRACT_LAST, preferred_element_type=F32)
@@ -150,38 +171,65 @@
     owned = count_dp // 2
     bits = bits_of(count_fsdp)
     low, top = bits[:-1], bits[-1]
+    mine = width // count_fsdp
+    lead = -(-GR // width)
+    tile = (lead + 16) // 16 * 16
+    rows_here = GR // count_dp
+    square = jax.ShapeDtypeStruct((width, token_rows), F32)
     own_out, own_in = sketch_out.T, sketch_in.T
+
     near_out = spread(own_out, low)
     far_out = swap(own_out, "fsdp", top)
     near_in = spread(own_in, low)
-    near = list(range(top))
-    inputs = project(near_in, near, hidden_in, None, F32)
     far_in = swap(own_in, "fsdp", top)
+    inputs = call(functools.partial(near_kernel, list(range(top))), [*near_in, hidden_in], square)
     out_shards = near_out + spread(after(far_out, inputs), low)
-    errors = pl.pallas_call(
-        functools.partial(errors_kernel, list(range(count_fsdp)), owned),
-        out_shape=jax.ShapeDtypeStruct((width + KEY_ROWS, token_rows), BF16),
-        in_specs=[VMEM] * (count_fsdp + 2) + [SMEM] * 2 + [ANY],
-        out_specs=VMEM,
-        compiler_params=ROOM,
-        cost_estimate=pl.CostEstimate(flops=30_000_000_000, bytes_accessed=60_000_000, transcendentals=0),
-    )(*out_shards, out_grads, piece_of, owner_dp, owner_slot, inputs)
-    group_errors, halfway = gather_group(errors)
-    far_in = spread(after(far_in, halfway), low)
-    for k, shard in enumerate(far_in):
-        last = k == len(far_in) - 1
-        inputs = project([shard], [top + k], hidden_in, inputs, BF16 if last else F32)
-    group_inputs, _ = gather_group(inputs)
-    all_errors = spread(group_errors, bits)
-    all_inputs = spread(group_inputs, bits)
+    errors = call(
+        functools.partial(errors_kernel, list(range(count_fsdp))),
+        [*out_shards, out_grads, inputs],
+        jax.ShapeDtypeStruct(square.shape, BF16),
+        [VMEM] * (count_fsdp + 1) + [ANY],
+        ERRORS_COST,
+    )
+    first, *later = bits_of(count_dp)
+    order = [0]
+    for bit in [*later, first]:
+        order += [k ^ bit for k in order]
+    keys = None
+    for bit in later:
+        errors = widen(errors, "dp", bit)
+        far_in = after(far_in, errors)
+        if keys is None:
+            keys = call(
+                functools.partial(keys_kernel, owned),
+                [piece_of, owner_dp, owner_slot, errors],
+                jax.ShapeDtypeStruct((tile, token_rows), BF16),
+                [VMEM, SMEM, SMEM, ANY],
+            )
+    far_in = spread(far_in, low)
+    for k in range(top - 1):
+        inputs = call(
+            functools.partial(project_kernel, [top + k]), [far_in[k], hidden_in, inputs], square
+        )
+    messages = call(
+        functools.partial(message_kernel, [2 * top - 1], mine, lead),
+        [far_in[-1], hidden_in, inputs, keys],
+        jax.ShapeDtypeStruct((count_dp * count_fsdp, mine + tile, token_rows), BF16),
+    )
+    messages = lax.all_to_all(messages, BOTH, split_axis=0, concat_axis=0, tiled=True)
+    all_errors = spread(widen(errors, "dp", first), bits)
+    picked = call(
+        picked_kernel,
+        all_errors,
+        jax.ShapeDtypeStruct((rows_here, count_dp * count_fsdp * token_rows), F32),
+        cost=PICKED_COST,
+    )
     scale = 1.0 / math.sqrt(owned * count_dp * count_fsdp)
-    return pl.pallas_call(
-        functools.partial(gram_kernel, count_dp, owned * count_dp, scale),
-        out_shape=jax.ShapeDtypeStruct((GR // count_dp, width * width // count_fsdp), F32),
-        in_specs=[VMEM] * (2 * count_fsdp),
-        out_specs=VMEM,
-        compiler_params=ROOM,
-    )(*all_errors, *all_inputs)
+    return call(
+        functools.partial(gram_kernel, order, lead, owned * count_dp, scale),
+        [*all_errors, picked, messages],
+        jax.ShapeDtypeStruct((rows_here, width * width // count_fsdp), F32),
+    )
 
 
 def by_pieces(hidden_in, out_grads, piece_of, owner_dp, owner_slot, sketch_in, sketch_out):
@@ -235,7 +283,7 @@
     width = sketch_in.shape[1]
     gathered = count_dp * count_fsdp * token_rows * 2 * width * 2
     summed = GR * width * width * 4
-    doubling = all(n & (n - 1) == 0 for n in (count_dp, count_fsdp))
+    doubling = all(n > 1 and n & (n - 1) == 0 for n in (count_dp, count_fsdp))
     whole_tiles = token_rows % 128 == 0 and width % (16 * count_fsdp) == 0
     exact_keys = count_dp * (count_dp // 2) <= 256
     form = by_tokens if gathered <= summed and doubling and whole_tiles and exact_keys else by_pieces

time: 45 us -> 41.4 us (0.920)
  starting transfers between devices: 21.2 us -> 17.3 us
  waiting for transfers between devices: 15 us -> 13.9 us
  local copies, waits for them, and re-layouts: 2.06 us -> 3.09 us
    ppermute x18 -> x12, starting transfers between devices: 21.2 us -> 12.1 us  [swap(): return lax.ppermute(value, axis, [(i, i ^ bit) for i in range(count)])]
    all_to_all x0 -> x1, starting transfers between devices: none -> 5.28 us  [by_tokens(): lax.all_to_all(messages, BOTH, split_axis=0, concat_axis=0, tiled=True)]
    ppermute x18 -> x12, waiting for transfers between devices: 15 us -> 12.9 us  [swap(): return lax.ppermute(value, axis, [(i, i ^ bit) for i in range(count)])]
    unnamed x14 -> x16, local copies, waits for them, and re-layouts: 2.06 us -> 3.09 us
    all_to_all x0 -> x1, waiting for transfers between devices: none -> 1.01 us  [by_tokens(): lax.all_to_all(messages, BOTH, split_axis=0, concat_axis=0, tiled=True)]
    pallas_call x5 -> x7, Pallas kernels: 6.47 us -> 6.62 us  [call(): pl.pallas_call(kernel, out_shape=outputs, in_specs=specs or [VMEM] * len(...]
  transfers between devices with their start and end apart: 18 -> 13, of which waited for: 13 -> 8; matrix products, arithmetic and copies ran while one was open for 0% -> 0% of each run, Pallas kernels for 7% -> 9%
where the time goes in v3:
time: 41.4 us; the launch traced here: 41.1 us
  starting transfers between devices  17.3 us (42%)
  waiting for transfers between devices  13.9 us (34%)
  Pallas kernels  6.62 us (16%)
  local copies, waits for them, and re-layouts  3.09 us (7%)
    ppermute x12, waiting for transfers between devices, swap(): return lax.ppermute(value, axis, [(i, i ^ bit) for i in range(count)])  12.9 us
    ppermute x12, starting transfers between devices, swap(): return lax.ppermute(value, axis, [(i, i ^ bit) for i in range(count)])  12.1 us
    pallas_call x7, Pallas kernels, call(): pl.pallas_call(kernel, out_shape=outputs, in_specs=specs or [VMEM] * len(...  6.62 us
    all_to_all x1, starting transfers between devices, by_tokens(): lax.all_to_all(messages, BOTH, split_axis=0, concat_axis=0, tiled=True)  5.28 us
    unnamed x16, local copies, waits for them, and re-layouts  3.09 us
    all_to_all x1, waiting for transfers between devices, by_tokens(): lax.all_to_all(messages, BOTH, split_axis=0, concat_axis=0, tiled=True)  1.01 us
  transfers between devices with their start and end apart: 13, of which 8 were waited for; matrix products, arithmetic and copies ran while one was open for 0% of the time, Pallas kernels for 9%

profile of v3, /device:TPU:0, one launch (start us, length us, event | category | flops | bytes accessed | tf_op | source)
XLA Modules:
  0.0 41.1 jit_solution(10243352512917392007)
XLA Ops:
  0.0 0.5 %collective-permute-start.2 = (bf16[64,3584]{1,0:T(8,128)(2,1)}, bf16[64,3584]{1,0:T(8,128)(2,1)S(1)}, u32[]{:S(2)}, u32[]{:S(2)}) collective-permute-start(bf16[64,3584]{1,0:T(8,128)(2,1)} %bitcast.2), channel_id=1, source_target_pairs={{0,1},{1,0},{2,3},{3,2},{4,5},{5,4},{6,7},{7,6},{8,9},{9,8},{10,11... | collective-permute-start | bytes 1376264 | tf_op jit(solution)/shard_map/ppermute | solution.py:31
  0.5 2.5 %collective-permute-start.1 = (bf16[64,1024]{1,0:T(8,128)(2,1)}, bf16[64,1024]{1,0:T(8,128)(2,1)S(1)}, u32[]{:S(2)}, u32[]{:S(2)}) collective-permute-start(bf16[64,1024]{1,0:T(8,128)(2,1)} %bitcast.5), channel_id=1, source_target_pairs={{0,2},{1,3},{2,0},{3,1},{4,6},{5,7},{6,4},{7,5},{8,10},{9,11},{10,... | collective-permute-start | bytes 393224 | tf_op jit(solution)/shard_map/ppermute | solution.py:31
  2.9 0.1 collective-permute-start.10
  3.0 0.2 collective-permute-start
  3.2 0.0 collective-permute-done.2.refs_1_
  3.2 0.0 copy-start
  3.2 2.0 %copy-done = bf16[128,14336]{1,0:T(8,128)(2,1)S(1)} copy-done((bf16[128,14336]{1,0:T(8,128)(2,1)S(1)}, bf16[128,14336]{1,0:T(8,128)(2,1)}, u32[]{:S(2)}) %copy-start) | copy-done | bytes 3670040
  5.2 0.0 copy-start.2
  5.2 1.0 %copy-done.2 = bf16[3584,64]{0,1:T(8,128)(2,1)S(1)} copy-done((bf16[3584,64]{0,1:T(8,128)(2,1)S(1)}, bf16[3584,64]{0,1:T(8,128)(2,1)}, u32[]{:S(2)}) %copy-start.2) | copy-done | bytes 458776
  6.3 0.0 copy-start.6
  6.3 0.0 copy-start.7
  6.3 0.7 %shard_map.73.refs_5_.refs_2_ = f32[64,128]{1,0:T(8,128)S(1)} custom-call(bf16[64,3584]{1,0:T(8,128)(2,1)S(1)} %bitcast.4, bf16[64,3584]{1,0:T(8,128)(2,1)S(1)} %collective-permute-done.2.refs_1_, bf16[128,14336]{1,0:T(8,128)(2,1)S(1)} %copy-done), custom_call_target="tpu_custom_call" | custom-call | tf_op jit(solution)/shard_map/pallas_call | solution.py:96
  7.0 0.0 copy-start.3
  7.0 0.0 copy-start.4
  7.1 0.0 copy-start.5
  7.1 0.0 copy-start.1
  7.1 0.4 %collective-permute-done.1.refs_2_ = bf16[64,1024]{1,0:T(8,128)(2,1)S(1)} collective-permute-done((bf16[64,1024]{1,0:T(8,128)(2,1)}, bf16[64,1024]{1,0:T(8,128)(2,1)S(1)}, u32[]{:S(2)}, u32[]{:S(2)}) %collective-permute-start.1) | collective-permute-done | bytes 131104 | tf_op jit(solution)/shard_map/ppermute | solution.py:31
  7.5 0.0 collective-permute-start.3
  7.5 0.0 collective-permute-done.refs_1_
  7.5 1.3 %collective-permute-done.3.refs_3_ = bf16[64,1024]{1,0:T(8,128)(2,1)S(1)} collective-permute-done((bf16[64,1024]{1,0:T(8,128)(2,1)S(1)}, bf16[64,1024]{1,0:T(8,128)(2,1)S(1)}, u32[]{:S(2)}, u32[]{:S(2)}) %collective-permute-start.3) | collective-permute-done | bytes 131104 | tf_op jit(solution)/shard_map/ppermute | solution.py:31
  8.8 0.0 copy-done.6
  8.9 0.0 copy-done.7
  8.9 0.5 %shard_map.74 = bf16[64,128]{1,0:T(8,128)(2,1)S(1)} custom-call(bf16[64,1024]{1,0:T(8,128)(2,1)S(1)} %bitcast.7, bf16[64,1024]{1,0:T(8,128)(2,1)S(1)} %collective-permute-done.refs_1_, bf16[64,1024]{1,0:T(8,128)(2,1)S(1)} %collective-permute-done.1.refs_2_, bf16[64,1024]{1,0:T(8,128)(2,1)S(1)} %collective-permute-done.3.refs_3_, ...), custom_call_target="tpu_custom_call" | custom-call | flops 1500000000 | bytes 1000000 | tf_op jit(solution)/shard_map/pallas_call | solution.py:96
  9.3 2.1 %collective-permute-start.4 = (bf16[64,128]{1,0:T(8,128)(2,1)S(1)}, bf16[64,128]{1,0:T(8,128)(2,1)S(1)}, u32[]{:S(2)}, u32[]{:S(2)}) collective-permute-start(bf16[64,128]{1,0:T(8,128)(2,1)S(1)} %shard_map.74), channel_id=1, source_target_pairs={{0,8},{4,12},{8,0},{12,4},{16,24},{20,28},{24,16},{28,20},{1,9},{5... | collective-permute-start | bytes 49160 | tf_op jit(solution)/shard_map/ppermute | solution.py:31
  11.4 1.7 %collective-permute-done.4 = bf16[64,128]{1,0:T(8,128)(2,1)S(1)} collective-permute-done((bf16[64,128]{1,0:T(8,128)(2,1)S(1)}, bf16[64,128]{1,0:T(8,128)(2,1)S(1)}, u32[]{:S(2)}, u32[]{:S(2)}) %collective-permute-start.4) | collective-permute-done | bytes 16416 | tf_op jit(solution)/shard_map/ppermute | solution.py:31
  13.2 3.0 %collective-permute-start.5 = (bf16[128,128]{1,0:T(8,128)(2,1)S(1)}, bf16[128,128]{1,0:T(8,128)(2,1)S(1)}, u32[]{:S(2)}, u32[]{:S(2)}) collective-permute-start(bf16[128,128]{1,0:T(8,128)(2,1)S(1)} %pad_maximum_fusion.2._), channel_id=1, source_target_pairs={{0,16},{4,20},{8,24},{12,28},{16,0},{20,4},{24,8},{28,12},{1,17},{... | collective-permute-start | bytes 98312 | tf_op jit(solution)/shard_map/ppermute | solution.py:31
  16.2 1.0 %collective-permute-done.10.refs_0_ = bf16[64,3584]{1,0:T(8,128)(2,1)S(1)} collective-permute-done((bf16[64,3584]{1,0:T(8,128)(2,1)}, bf16[64,3584]{1,0:T(8,128)(2,1)S(1)}, u32[]{:S(2)}, u32[]{:S(2)}) %collective-permute-start.10) | collective-permute-done | bytes 458784 | tf_op jit(solution)/shard_map/ppermute | solution.py:31
  17.2 1.0 %collective-permute-done.5 = bf16[128,128]{1,0:T(8,128)(2,1)S(1)} collective-permute-done((bf16[128,128]{1,0:T(8,128)(2,1)S(1)}, bf16[128,128]{1,0:T(8,128)(2,1)S(1)}, u32[]{:S(2)}, u32[]{:S(2)}) %collective-permute-start.5) | collective-permute-done | bytes 32800 | tf_op jit(solution)/shard_map/ppermute | solution.py:31
  18.1 0.0 collective-permute-start.11
  18.1 1.9 %collective-permute-start.6 = (bf16[256,128]{1,0:T(8,128)(2,1)S(1)}, bf16[256,128]{1,0:T(8,128)(2,1)S(1)}, u32[]{:S(2)}, u32[]{:S(2)}) collective-permute-start(bf16[256,128]{1,0:T(8,128)(2,1)S(1)} %pad_maximum_fusion.1), channel_id=1, source_target_pairs={{0,4},{4,0},{8,12},{12,8},{16,20},{20,16},{24,28},{28,24},{1,5},{5... | collective-permute-start | bytes 196616 | tf_op jit(solution)/shard_map/ppermute | solution.py:31
  20.0 0.0 copy-done.3
  20.0 0.0 copy-done.4
  20.0 0.0 copy-done.5
  20.0 0.6 %shard_map.77.refs_3_ = bf16[16,128]{1,0:T(8,128)(2,1)S(1)} custom-call(s32[1,128]{1,0:T(1,128)S(1)} %copy-done.3, s32[1,8]{1,0:T(1,128)S(1)} %copy-done.4, s32[1,8]{1,0:T(1,128)S(1)} %copy-done.5, bf16[128,128]{1,0:T(8,128)(2,1)S(1)} %pad_maximum_fusion.2._), custom_call_target="tpu_custom_call" | custom-call | tf_op jit(solution)/shard_map/pallas_call | solution.py:96
  20.6 0.0 copy-done.1
  20.6 0.4 %shard_map.76.refs_2_ = f32[64,128]{1,0:T(8,128)S(1)} custom-call(bf16[64,3584]{1,0:T(8,128)(2,1)S(1)} %collective-permute-done.10.refs_0_, bf16[128,14336]{1,0:T(8,128)(2,1)S(1)} %copy-done.1, f32[64,128]{1,0:T(8,128)S(1)} %shard_map.73.refs_5_.refs_2_), custom_call_target="tpu_custom_call" | custom-call | tf_op jit(solution)/shard_map/pallas_call | solution.py:96
  21.0 0.0 collective-permute-done.11.refs_0_
  21.0 1.2 %shard_map.78 = bf16[32,32,128]{2,1,0:T(8,128)(2,1)} custom-call(bf16[64,3584]{1,0:T(8,128)(2,1)S(1)} %collective-permute-done.11.refs_0_, bf16[128,14336]{1,0:T(8,128)(2,1)S(1)} %copy-done.1, f32[64,128]{1,0:T(8,128)S(1)} %shard_map.76.refs_2_, bf16[16,128]{1,0:T(8,128)(2,1)S(1)} %shard_map.77.refs_3_), custom_call_target="tpu_custom_call" | custom-call | tf_op jit(solution)/shard_map/pallas_call | solution.py:96
  22.2 5.3 %all-to-all-start = ((bf16[32,32,128]{2,1,0:T(8,128)(2,1)}), bf16[32,32,128]{2,1,0:T(8,128)(2,1)S(1)}, u32[]{:S(2)}, u32[]{:S(2)}) async-start(bf16[32,32,128]{2,1,0:T(8,128)(2,1)} %shard_map.78), calls=%async_computation | async-start | bytes 524288 | tf_op jit(solution)/shard_map/all_to_all | solution.py:219
  27.5 0.0 collective-permute-done.6
  27.5 1.8 %collective-permute-start.8 = (bf16[512,128]{1,0:T(8,128)(2,1)S(1)}, bf16[512,128]{1,0:T(8,128)(2,1)S(1)}, u32[]{:S(2)}, u32[]{:S(2)}) collective-permute-start(bf16[512,128]{1,0:T(8,128)(2,1)S(1)} %pad_maximum_fusion.refs_0_), channel_id=1, source_target_pairs={{0,2},{1,3},{2,0},{3,1},{4,6},{5,7},{6,4},{7,5},{8,10},{9,11},{10,... | collective-permute-start | bytes 393224 | tf_op jit(solution)/shard_map/ppermute | solution.py:31
  29.3 0.0 collective-permute-start.7
  29.4 6.2 %collective-permute-done.8.refs_2_ = bf16[512,128]{1,0:T(8,128)(2,1)S(1)} collective-permute-done((bf16[512,128]{1,0:T(8,128)(2,1)S(1)}, bf16[512,128]{1,0:T(8,128)(2,1)S(1)}, u32[]{:S(2)}, u32[]{:S(2)}) %collective-permute-start.8) | collective-permute-done | bytes 131104 | tf_op jit(solution)/shard_map/ppermute | solution.py:31
  35.5 0.0 collective-permute-start.9
  35.5 0.0 collective-permute-done.7.refs_1_
  35.5 1.3 %collective-permute-done.9.refs_3_ = bf16[512,128]{1,0:T(8,128)(2,1)S(1)} collective-permute-done((bf16[512,128]{1,0:T(8,128)(2,1)S(1)}, bf16[512,128]{1,0:T(8,128)(2,1)S(1)}, u32[]{:S(2)}, u32[]{:S(2)}) %collective-permute-start.9) | collective-permute-done | bytes 131104 | tf_op jit(solution)/shard_map/ppermute | solution.py:31
  36.9 0.2 shard_map.75.refs_4_
  37.1 1.0 %all-to-all-done.refs_5_ = bf16[32,32,128]{2,1,0:T(8,128)(2,1)S(1)} async-done(((bf16[32,32,128]{2,1,0:T(8,128)(2,1)}), bf16[32,32,128]{2,1,0:T(8,128)(2,1)S(1)}, u32[]{:S(2)}, u32[]{:S(2)}) %all-to-all-start) | async-done | bytes 262176 | tf_op jit(solution)/shard_map/all_to_all | solution.py:219
  38.1 3.0 %shard_map.79 = f32[24,1024]{1,0:T(8,128)} custom-call(bf16[512,128]{1,0:T(8,128)(2,1)S(1)} %pad_maximum_fusion.refs_0_, bf16[512,128]{1,0:T(8,128)(2,1)S(1)} %collective-permute-done.7.refs_1_, bf16[512,128]{1,0:T(8,128)(2,1)S(1)} %collective-permute-done.8.refs_2_, bf16[512,128]{1,0:T(8,128)(2,1)S(1)} %collective-permute-done.9.refs_3_, ...), custom_call_target="tpu_custom_call" | custom-call | tf_op jit(solution)/shard_map/pallas_call | solution.py:96
  (3 shorter events, 0.0 us)
Async XLA Ops:
  0.0 3.2 %collective-permute-start.2 = (bf16[64,3584]{1,0:T(8,128)(2,1)}, bf16[64,3584]{1,0:T(8,128)(2,1)S(1)}, u32[]{:S(2)}, u32[]{:S(2)}) collective-permute-start(bf16[64,3584]{1,0:T(8,128)(2,1)} %bitcast.2), channel_id=1, source_target_pairs={{0,1},{1,0},{2,3},{3,2},{4,5},{5,4},{6,7},{7,6},{8,9},{9,8},{10,11... | collective-permute-start | bytes 1376264 | tf_op jit(solution)/shard_map/ppermute | solution.py:31
  0.5 7.0 %collective-permute-start.1 = (bf16[64,1024]{1,0:T(8,128)(2,1)}, bf16[64,1024]{1,0:T(8,128)(2,1)S(1)}, u32[]{:S(2)}, u32[]{:S(2)}) collective-permute-start(bf16[64,1024]{1,0:T(8,128)(2,1)} %bitcast.5), channel_id=1, source_target_pairs={{0,2},{1,3},{2,0},{3,1},{4,6},{5,7},{6,4},{7,5},{8,10},{9,11},{10,... | collective-permute-start | bytes 393224 | tf_op jit(solution)/shard_map/ppermute | solution.py:31
  2.9 14.2 %collective-permute-start.10 = (bf16[64,3584]{1,0:T(8,128)(2,1)}, bf16[64,3584]{1,0:T(8,128)(2,1)S(1)}, u32[]{:S(2)}, u32[]{:S(2)}) collective-permute-start(bf16[64,3584]{1,0:T(8,128)(2,1)} %bitcast.3), channel_id=1, source_target_pairs={{0,2},{1,3},{2,0},{3,1},{4,6},{5,7},{6,4},{7,5},{8,10},{9,11},{10,... | collective-permute-start | bytes 1376264 | tf_op jit(solution)/shard_map/ppermute | solution.py:31
  3.0 4.5 %collective-permute-start = (bf16[64,1024]{1,0:T(8,128)(2,1)}, bf16[64,1024]{1,0:T(8,128)(2,1)S(1)}, u32[]{:S(2)}, u32[]{:S(2)}) collective-permute-start(bf16[64,1024]{1,0:T(8,128)(2,1)} %bitcast.6), channel_id=1, source_target_pairs={{0,1},{1,0},{2,3},{3,2},{4,5},{5,4},{6,7},{7,6},{8,9},{9,8},{10,11... | collective-permute-start | bytes 393224 | tf_op jit(solution)/shard_map/ppermute | solution.py:31
  3.2 2.0 %copy-start = (bf16[128,14336]{1,0:T(8,128)(2,1)S(1)}, bf16[128,14336]{1,0:T(8,128)(2,1)}, u32[]{:S(2)}) copy-start(bf16[128,14336]{1,0:T(8,128)(2,1)} %refs_1_.3) | copy-start | bytes 11010052
  5.2 1.0 %copy-start.2 = (bf16[3584,64]{0,1:T(8,128)(2,1)S(1)}, bf16[3584,64]{0,1:T(8,128)(2,1)}, u32[]{:S(2)}) copy-start(bf16[3584,64]{0,1:T(8,128)(2,1)} %param.12) | copy-start | bytes 1376260
  6.3 2.6 %copy-start.6 = (bf16[128,4096]{1,0:T(8,128)(2,1)S(1)}, bf16[128,4096]{1,0:T(8,128)(2,1)}, u32[]{:S(2)}) copy-start(bf16[128,4096]{1,0:T(8,128)(2,1)} %refs_4_.1) | copy-start | bytes 3145732
  6.3 2.6 %copy-start.7 = (bf16[1024,64]{0,1:T(8,128)(2,1)S(1)}, bf16[1024,64]{0,1:T(8,128)(2,1)}, u32[]{:S(2)}) copy-start(bf16[1024,64]{0,1:T(8,128)(2,1)} %param.13) | copy-start | bytes 393220
  7.0 13.0 %copy-start.3 = (s32[1,128]{1,0:T(1,128)S(1)}, s32[1,128]{1,0:T(1,128)}, u32[]{:S(2)}) copy-start(s32[1,128]{1,0:T(1,128)} %piece_of.1) | copy-start | bytes 1540
  7.0 13.0 %copy-start.4 = (s32[1,8]{1,0:T(1,128)S(1)}, s32[1,8]{1,0:T(1,128)}, u32[]{:S(2)}) copy-start(s32[1,8]{1,0:T(1,128)} %owner_dp.1) | copy-start | bytes 100
  7.1 13.0 %copy-start.5 = (s32[1,8]{1,0:T(1,128)S(1)}, s32[1,8]{1,0:T(1,128)}, u32[]{:S(2)}) copy-start(s32[1,8]{1,0:T(1,128)} %owner_slot.1) | copy-start | bytes 100
  7.1 13.5 %copy-start.1 = (bf16[128,14336]{1,0:T(8,128)(2,1)S(1)}, bf16[128,14336]{1,0:T(8,128)(2,1)}, u32[]{:S(2)}) copy-start(bf16[128,14336]{1,0:T(8,128)(2,1)} %refs_1_.3) | copy-start | bytes 11010052
  7.5 1.3 %collective-permute-start.3 = (bf16[64,1024]{1,0:T(8,128)(2,1)S(1)}, bf16[64,1024]{1,0:T(8,128)(2,1)S(1)}, u32[]{:S(2)}, u32[]{:S(2)}) collective-permute-start(bf16[64,1024]{1,0:T(8,128)(2,1)S(1)} %collective-permute-done.1.refs_2_), channel_id=1, source_target_pairs={{0,1},{1,0},{2,3},{3,2},{4,5},{5,4},{6,7},{7,6},{8,9},{9,8},{10,11... | collective-permute-start | bytes 393224 | tf_op jit(solution)/shard_map/ppermute | solution.py:31
  9.3 3.8 %collective-permute-start.4 = (bf16[64,128]{1,0:T(8,128)(2,1)S(1)}, bf16[64,128]{1,0:T(8,128)(2,1)S(1)}, u32[]{:S(2)}, u32[]{:S(2)}) collective-permute-start(bf16[64,128]{1,0:T(8,128)(2,1)S(1)} %shard_map.74), channel_id=1, source_target_pairs={{0,8},{4,12},{8,0},{12,4},{16,24},{20,28},{24,16},{28,20},{1,9},{5... | collective-permute-start | bytes 49160 | tf_op jit(solution)/shard_map/ppermute | solution.py:31
  13.2 4.9 %collective-permute-start.5 = (bf16[128,128]{1,0:T(8,128)(2,1)S(1)}, bf16[128,128]{1,0:T(8,128)(2,1)S(1)}, u32[]{:S(2)}, u32[]{:S(2)}) collective-permute-start(bf16[128,128]{1,0:T(8,128)(2,1)S(1)} %pad_maximum_fusion.2._), channel_id=1, source_target_pairs={{0,16},{4,20},{8,24},{12,28},{16,0},{20,4},{24,8},{28,12},{1,17},{... | collective-permute-start | bytes 98312 | tf_op jit(solution)/shard_map/ppermute | solution.py:31
  18.1 2.9 %collective-permute-start.11 = (bf16[64,3584]{1,0:T(8,128)(2,1)S(1)}, bf16[64,3584]{1,0:T(8,128)(2,1)S(1)}, u32[]{:S(2)}, u32[]{:S(2)}) collective-permute-start(bf16[64,3584]{1,0:T(8,128)(2,1)S(1)} %collective-permute-done.10.refs_0_), channel_id=1, source_target_pairs={{0,1},{1,0},{2,3},{3,2},{4,5},{5,4},{6,7},{7,6},{8,9},{9,8},{10,11... | collective-permute-start | bytes 1376264 | tf_op jit(solution)/shard_map/ppermute | solution.py:31
  18.1 9.4 %collective-permute-start.6 = (bf16[256,128]{1,0:T(8,128)(2,1)S(1)}, bf16[256,128]{1,0:T(8,128)(2,1)S(1)}, u32[]{:S(2)}, u32[]{:S(2)}) collective-permute-start(bf16[256,128]{1,0:T(8,128)(2,1)S(1)} %pad_maximum_fusion.1), channel_id=1, source_target_pairs={{0,4},{4,0},{8,12},{12,8},{16,20},{20,16},{24,28},{28,24},{1,5},{5... | collective-permute-start | bytes 196616 | tf_op jit(solution)/shard_map/ppermute | solution.py:31
  22.2 15.9 %all-to-all-start = ((bf16[32,32,128]{2,1,0:T(8,128)(2,1)}), bf16[32,32,128]{2,1,0:T(8,128)(2,1)S(1)}, u32[]{:S(2)}, u32[]{:S(2)}) async-start(bf16[32,32,128]{2,1,0:T(8,128)(2,1)} %shard_map.78), calls=%async_computation | async-start | bytes 524288 | tf_op jit(solution)/shard_map/all_to_all | solution.py:219
  27.5 8.0 %collective-permute-start.8 = (bf16[512,128]{1,0:T(8,128)(2,1)S(1)}, bf16[512,128]{1,0:T(8,128)(2,1)S(1)}, u32[]{:S(2)}, u32[]{:S(2)}) collective-permute-start(bf16[512,128]{1,0:T(8,128)(2,1)S(1)} %pad_maximum_fusion.refs_0_), channel_id=1, source_target_pairs={{0,2},{1,3},{2,0},{3,1},{4,6},{5,7},{6,4},{7,5},{8,10},{9,11},{10,... | collective-permute-start | bytes 393224 | tf_op jit(solution)/shard_map/ppermute | solution.py:31
  29.3 6.2 %collective-permute-start.7 = (bf16[512,128]{1,0:T(8,128)(2,1)S(1)}, bf16[512,128]{1,0:T(8,128)(2,1)S(1)}, u32[]{:S(2)}, u32[]{:S(2)}) collective-permute-start(bf16[512,128]{1,0:T(8,128)(2,1)S(1)} %pad_maximum_fusion.refs_0_), channel_id=1, source_target_pairs={{0,1},{1,0},{2,3},{3,2},{4,5},{5,4},{6,7},{7,6},{8,9},{9,8},{10,11... | collective-permute-start | bytes 393224 | tf_op jit(solution)/shard_map/ppermute | solution.py:31
  35.5 1.3 %collective-permute-start.9 = (bf16[512,128]{1,0:T(8,128)(2,1)S(1)}, bf16[512,128]{1,0:T(8,128)(2,1)S(1)}, u32[]{:S(2)}, u32[]{:S(2)}) collective-permute-start(bf16[512,128]{1,0:T(8,128)(2,1)S(1)} %collective-permute-done.8.refs_2_), channel_id=1, source_target_pairs={{0,1},{1,0},{2,3},{3,2},{4,5},{5,4},{6,7},{7,6},{8,9},{9,8},{10,11... | collective-permute-start | bytes 393224 | tf_op jit(solution)/shard_map/ppermute | solution.py:31

commit v4 on v3

--- a/solution.py
+++ b/solution.py
@@ -21,7 +21,7 @@
     flops=1_500_000_000, bytes_accessed=1_000_000, transcendentals=0
 )
 PICKED_COST = pl.CostEstimate(
-    flops=2_000_000_000, bytes_accessed=1_000_000, transcendentals=0
+    flops=600_000_000, bytes_accessed=1_000_000, transcendentals=0
 )
 ROOM = pltpu.CompilerParams(vmem_limit_bytes=16 * 1024 * 1024)
 
@@ -84,12 +84,11 @@
     count = len(which)
     tokens, total, keys, out = refs[count:]
     rows = (low_rank(refs[:count], which, tokens) + total[...]).astype(BF16)
-    shared = jnp.concatenate([rows[:lead, :], keys[lead:, :]], axis=0)
+    shared = jnp.concatenate([rows[:lead, :], keys[: out.shape[1] - mine - lead, :]], axis=0)
     parts = rows.shape[0] // mine
     for k in range(out.shape[0]):
         f = k % parts
-        out[k, :mine, :] = rows[f * mine : (f + 1) * mine, :]
-        out[k, mine:, :] = shared
+        out[k] = jnp.concatenate([rows[f * mine : (f + 1) * mine, :], shared], axis=0)
 
 
 def call(kernel, operands, outputs, specs=None, cost=None):
@@ -127,27 +126,34 @@
     rows_here, columns_here = out.shape
     width = errors[0].shape[0] // count_dp
     mine = columns_here // width
-    size = messages.shape[1]
     d, f = lax.axis_index("dp"), lax.axis_index("fsdp")
-    place = (rows_here, size - mine)
-    column = d * rows_here + lax.broadcasted_iota(jnp.int32, place, 0)
-    pick_in = (lax.broadcasted_iota(jnp.int32, place, 1) == column // width).astype(F32).astype(BF16)
     wide, narrow = [], []
     for g, e_ref in enumerate(errors):
         places = [(d ^ k) * count_fsdp + (f ^ g) for k in order]
         err = jnp.concatenate([e_ref[k * width : (k + 1) * width, :] for k in range(count_dp)], axis=1)
-        here = jnp.concatenate([messages[k, :mine, :] for k in places], axis=1)
-        shared = jnp.concatenate([messages[k, mine:, :] for k in places], axis=1)
+        held = jnp.concatenate([messages[k] for k in places], axis=1)
+        here, shared = held[:mine, :], held[mine:, :]
         key = shared.astype(F32)[lead : lead + 1, :]
         tokens = key.shape[1]
         example = lax.broadcasted_iota(jnp.int32, (group_examples, tokens), 0).astype(F32)
         member = (example == key).astype(F32).astype(BF16)
-        spread_rows = jnp.concatenate([member * here[i : i + 1, :] for i in range(mine)], axis=0)
+        spread_rows = [member * here[i : i + 1, :] for i in range(mine)]
+        spread_rows = jnp.concatenate(
+            [jnp.concatenate(spread_rows[i : i + 2], axis=1) for i in range(0, mine, 2)], axis=0
+        )
+        blank = jnp.zeros_like(err)
+        twice = jnp.concatenate(
+            [jnp.concatenate([err, blank], axis=1), jnp.concatenate([blank, err], axis=1)], axis=0
+        )
         wide.append(
-            lax.dot_general(spread_rows, err, CONTRACT_LAST, preferred_element_type=F32).astype(BF16)
-        )
-        product = jnp.dot(pick_in, shared, preferred_element_type=F32)
-        product = product * picked[:, g * tokens : (g + 1) * tokens]
+            lax.dot_general(spread_rows, twice, CONTRACT_LAST, preferred_element_type=F32).astype(BF16)
+        )
+        column = d * rows_here + lax.broadcasted_iota(jnp.int32, (rows_here, tokens), 0)
+        shared = shared.astype(F32)
+        chosen = shared[:1, :]
+        for i in range(1, lead):
+            chosen = jnp.where(column >= i * width, shared[i : i + 1, :], chosen)
+        product = chosen * picked[:, g * tokens : (g + 1) * tokens]
         upper = product.astype(BF16)
         lower = (product - upper.astype(F32)).astype(BF16)
         part = lax.dot_general(upper, member, CONTRACT_LAST, preferred_element_type=F32)
@@ -155,7 +161,7 @@
         narrow.append(part.astype(BF16))
     left = jnp.concatenate(narrow, axis=1)
     blocks = []
-    for i in range(mine):
+    for i in range(mine // 2):
         right = jnp.concatenate(
             [w[i * group_examples : (i + 1) * group_examples, :] for w in wide], axis=0
         )
@@ -173,7 +179,7 @@
     low, top = bits[:-1], bits[-1]
     mine = width // count_fsdp
     lead = -(-GR // width)
-    tile = (lead + 16) // 16 * 16
+    tile = (lead + 8) // 8 * 8
     rows_here = GR // count_dp
     square = jax.ShapeDtypeStruct((width, token_rows), F32)
     own_out, own_in = sketch_out.T, sketch_in.T
@@ -184,28 +190,26 @@
     far_in = swap(own_in, "fsdp", top)
     inputs = call(functools.partial(near_kernel, list(range(top))), [*near_in, hidden_in], square)
     out_shards = near_out + spread(after(far_out, inputs), low)
+    keys = call(
+        functools.partial(keys_kernel, owned),
+        [piece_of, owner_dp, owner_slot, inputs],
+        jax.ShapeDtypeStruct((16, token_rows), BF16),
+        [VMEM, SMEM, SMEM, ANY],
+    )
     errors = call(
         functools.partial(errors_kernel, list(range(count_fsdp))),
-        [*out_shards, out_grads, inputs],
+        [*out_shards, out_grads, inputs, keys],
         jax.ShapeDtypeStruct(square.shape, BF16),
-        [VMEM] * (count_fsdp + 1) + [ANY],
+        [VMEM] * (count_fsdp + 1) + [ANY] * 2,
         ERRORS_COST,
     )
     first, *later = bits_of(count_dp)
     order = [0]
     for bit in [*later, first]:
         order += [k ^ bit for k in order]
-    keys = None
     for bit in later:
         errors = widen(errors, "dp", bit)
         far_in = after(far_in, errors)
-        if keys is None:
-            keys = call(
-                functools.partial(keys_kernel, owned),
-                [piece_of, owner_dp, owner_slot, errors],
-                jax.ShapeDtypeStruct((tile, token_rows), BF16),
-                [VMEM, SMEM, SMEM, ANY],
-            )
     far_in = spread(far_in, low)
     for k in range(top - 1):
         inputs = call(

time: 41.4 us -> 39.2 us (0.947)
  waiting for transfers between devices: 13.9 us -> 11.9 us
  Pallas kernels: 6.62 us -> 5.82 us
  starting transfers between devices: 17.3 us -> 18 us
    ppermute x12, waiting for transfers between devices: 12.9 us -> 11.9 us  [swap(): return lax.ppermute(value, axis, [(i, i ^ bit) for i in range(count)])]
    all_to_all x1, waiting for transfers between devices: 1.01 us -> 0.01 us  [by_tokens(): lax.all_to_all(messages, BOTH, split_axis=0, concat_axis=0, tiled=True)]
    pallas_call x7, Pallas kernels: 6.62 us -> 5.82 us  [call(): pl.pallas_call(kernel, out_shape=outputs, in_specs=specs or [VMEM] * len(...]
    all_to_all x1, starting transfers between devices: 5.28 us -> 5.87 us  [by_tokens(): lax.all_to_all(messages, BOTH, split_axis=0, concat_axis=0, tiled=True)]
  transfers between devices with their start and end apart: 13 -> 13, of which waited for: 8 -> 7; matrix products, arithmetic and copies ran while one was open for 0% -> 0% of each run, Pallas kernels for 9% -> 9%
where the time goes in v4:
time: 39.2 us; the launch traced here: 39 us
  starting transfers between devices  18 us (46%)
  waiting for transfers between devices  11.9 us (30%)
  Pallas kernels  5.82 us (15%)
  local copies, waits for them, and re-layouts  3.08 us (8%)
    ppermute x12, starting transfers between devices, swap(): return lax.ppermute(value, axis, [(i, i ^ bit) for i in range(count)])  12.1 us
    ppermute x12, waiting for transfers between devices, swap(): return lax.ppermute(value, axis, [(i, i ^ bit) for i in range(count)])  11.9 us
    all_to_all x1, starting transfers between devices, by_tokens(): lax.all_to_all(messages, BOTH, split_axis=0, concat_axis=0, tiled=True)  5.87 us
    pallas_call x7, Pallas kernels, call(): pl.pallas_call(kernel, out_shape=outputs, in_specs=specs or [VMEM] * len(...  5.82 us
    unnamed x16, local copies, waits for them, and re-layouts  3.08 us
  transfers between devices with their start and end apart: 13, of which 7 were waited for; matrix products, arithmetic and copies ran while one was open for 0% of the time, Pallas kernels for 9%

profile of v4, /device:TPU:0, one launch (start us, length us, event | category | flops | bytes accessed | tf_op | source)
XLA Modules:
  0.0 39.0 jit_solution(14832861501391645529)
XLA Ops:
  0.0 0.0 copy-start.4
  0.0 0.0 copy-start.5
  0.0 0.0 copy-start.3
  0.0 0.5 %collective-permute-start.2 = (bf16[64,3584]{1,0:T(8,128)(2,1)}, bf16[64,3584]{1,0:T(8,128)(2,1)S(1)}, u32[]{:S(2)}, u32[]{:S(2)}) collective-permute-start(bf16[64,3584]{1,0:T(8,128)(2,1)} %bitcast.2), channel_id=1, source_target_pairs={{0,1},{1,0},{2,3},{3,2},{4,5},{5,4},{6,7},{7,6},{8,9},{9,8},{10,11... | collective-permute-start | bytes 1376264 | tf_op jit(solution)/shard_map/ppermute | solution.py:31
  0.5 2.6 %collective-permute-start.1 = (bf16[64,1024]{1,0:T(8,128)(2,1)}, bf16[64,1024]{1,0:T(8,128)(2,1)S(1)}, u32[]{:S(2)}, u32[]{:S(2)}) collective-permute-start(bf16[64,1024]{1,0:T(8,128)(2,1)} %bitcast.5), channel_id=1, source_target_pairs={{0,2},{1,3},{2,0},{3,1},{4,6},{5,7},{6,4},{7,5},{8,10},{9,11},{10,... | collective-permute-start | bytes 393224 | tf_op jit(solution)/shard_map/ppermute | solution.py:31
  3.1 0.1 collective-permute-start.10
  3.2 0.1 collective-permute-start
  3.3 0.0 collective-permute-done.2.refs_1_
  3.3 0.0 copy-start
  3.3 2.0 %copy-done = bf16[128,14336]{1,0:T(8,128)(2,1)S(1)} copy-done((bf16[128,14336]{1,0:T(8,128)(2,1)S(1)}, bf16[128,14336]{1,0:T(8,128)(2,1)}, u32[]{:S(2)}) %copy-start) | copy-done | bytes 3670040
  5.3 0.0 copy-start.2
  5.3 1.0 %copy-done.2 = bf16[3584,64]{0,1:T(8,128)(2,1)S(1)} copy-done((bf16[3584,64]{0,1:T(8,128)(2,1)S(1)}, bf16[3584,64]{0,1:T(8,128)(2,1)}, u32[]{:S(2)}) %copy-start.2) | copy-done | bytes 458776
  6.3 0.0 copy-start.6
  6.3 0.0 copy-start.7
  6.3 0.7 %shard_map.73._.refs_5_.refs_2_ = f32[64,128]{1,0:T(8,128)S(1)} custom-call(bf16[64,3584]{1,0:T(8,128)(2,1)S(1)} %bitcast.4, bf16[64,3584]{1,0:T(8,128)(2,1)S(1)} %collective-permute-done.2.refs_1_, bf16[128,14336]{1,0:T(8,128)(2,1)S(1)} %copy-done), custom_call_target="tpu_custom_call" | custom-call | tf_op jit(solution)/shard_map/pallas_call | solution.py:95
  7.1 0.0 copy-start.1
  7.1 0.5 %collective-permute-done.1.refs_2_ = bf16[64,1024]{1,0:T(8,128)(2,1)S(1)} collective-permute-done((bf16[64,1024]{1,0:T(8,128)(2,1)}, bf16[64,1024]{1,0:T(8,128)(2,1)S(1)}, u32[]{:S(2)}, u32[]{:S(2)}) %collective-permute-start.1) | collective-permute-done | bytes 131104 | tf_op jit(solution)/shard_map/ppermute | solution.py:31
  7.7 0.0 collective-permute-start.3
  7.7 0.0 copy-done.4
  7.7 0.0 copy-done.5
  7.7 0.0 copy-done.3
  7.7 0.6 %shard_map.74.refs_6_.refs_3_ = bf16[16,128]{1,0:T(8,128)(2,1)S(1)} custom-call(s32[1,128]{1,0:T(1,128)S(1)} %copy-done.3, s32[1,8]{1,0:T(1,128)S(1)} %copy-done.4, s32[1,8]{1,0:T(1,128)S(1)} %copy-done.5, f32[64,128]{1,0:T(8,128)S(1)} %shard_map.73._.refs_5_.refs_2_), custom_call_target="tpu_custom_call" | custom-call | tf_op jit(solution)/shard_map/pallas_call | solution.py:95
  8.2 0.0 collective-permute-done.refs_1_
  8.2 0.8 %collective-permute-done.3.refs_3_ = bf16[64,1024]{1,0:T(8,128)(2,1)S(1)} collective-permute-done((bf16[64,1024]{1,0:T(8,128)(2,1)S(1)}, bf16[64,1024]{1,0:T(8,128)(2,1)S(1)}, u32[]{:S(2)}, u32[]{:S(2)}) %collective-permute-start.3) | collective-permute-done | bytes 131104 | tf_op jit(solution)/shard_map/ppermute | solution.py:31
  9.0 0.0 copy-done.6
  9.0 0.0 copy-done.7
  9.0 0.5 %shard_map.75 = bf16[64,128]{1,0:T(8,128)(2,1)S(1)} custom-call(bf16[64,1024]{1,0:T(8,128)(2,1)S(1)} %bitcast.7, bf16[64,1024]{1,0:T(8,128)(2,1)S(1)} %collective-permute-done.refs_1_, bf16[64,1024]{1,0:T(8,128)(2,1)S(1)} %collective-permute-done.1.refs_2_, bf16[64,1024]{1,0:T(8,128)(2,1)S(1)} %collective-permute-done.3.refs_3_, ...), custom_call_target="tpu_custom_call" | custom-call | flops 1500000000 | bytes 1000000 | tf_op jit(solution)/shard_map/pallas_call | solution.py:95
  9.5 2.1 %collective-permute-start.4 = (bf16[64,128]{1,0:T(8,128)(2,1)S(1)}, bf16[64,128]{1,0:T(8,128)(2,1)S(1)}, u32[]{:S(2)}, u32[]{:S(2)}) collective-permute-start(bf16[64,128]{1,0:T(8,128)(2,1)S(1)} %shard_map.75), channel_id=1, source_target_pairs={{0,8},{4,12},{8,0},{12,4},{16,24},{20,28},{24,16},{28,20},{1,9},{5... | collective-permute-start | bytes 49160 | tf_op jit(solution)/shard_map/ppermute | solution.py:31
  11.6 1.7 %collective-permute-done.4 = bf16[64,128]{1,0:T(8,128)(2,1)S(1)} collective-permute-done((bf16[64,128]{1,0:T(8,128)(2,1)S(1)}, bf16[64,128]{1,0:T(8,128)(2,1)S(1)}, u32[]{:S(2)}, u32[]{:S(2)}) %collective-permute-start.4) | collective-permute-done | bytes 16416 | tf_op jit(solution)/shard_map/ppermute | solution.py:31
  13.3 3.0 %collective-permute-start.5 = (bf16[128,128]{1,0:T(8,128)(2,1)S(1)}, bf16[128,128]{1,0:T(8,128)(2,1)S(1)}, u32[]{:S(2)}, u32[]{:S(2)}) collective-permute-start(bf16[128,128]{1,0:T(8,128)(2,1)S(1)} %pad_maximum_fusion.2), channel_id=1, source_target_pairs={{0,16},{4,20},{8,24},{12,28},{16,0},{20,4},{24,8},{28,12},{1,17},{... | collective-permute-start | bytes 98312 | tf_op jit(solution)/shard_map/ppermute | solution.py:31
  16.4 0.9 %collective-permute-done.10.refs_0_ = bf16[64,3584]{1,0:T(8,128)(2,1)S(1)} collective-permute-done((bf16[64,3584]{1,0:T(8,128)(2,1)}, bf16[64,3584]{1,0:T(8,128)(2,1)S(1)}, u32[]{:S(2)}, u32[]{:S(2)}) %collective-permute-start.10) | collective-permute-done | bytes 458784 | tf_op jit(solution)/shard_map/ppermute | solution.py:31
  17.2 1.0 %collective-permute-done.5 = bf16[128,128]{1,0:T(8,128)(2,1)S(1)} collective-permute-done((bf16[128,128]{1,0:T(8,128)(2,1)S(1)}, bf16[128,128]{1,0:T(8,128)(2,1)S(1)}, u32[]{:S(2)}, u32[]{:S(2)}) %collective-permute-start.5) | collective-permute-done | bytes 32800 | tf_op jit(solution)/shard_map/ppermute | solution.py:31
  18.3 0.0 collective-permute-start.11
  18.3 1.9 %collective-permute-start.6 = (bf16[256,128]{1,0:T(8,128)(2,1)S(1)}, bf16[256,128]{1,0:T(8,128)(2,1)S(1)}, u32[]{:S(2)}, u32[]{:S(2)}) collective-permute-start(bf16[256,128]{1,0:T(8,128)(2,1)S(1)} %pad_maximum_fusion.1), channel_id=1, source_target_pairs={{0,4},{4,0},{8,12},{12,8},{16,20},{20,16},{24,28},{28,24},{1,5},{5... | collective-permute-start | bytes 196616 | tf_op jit(solution)/shard_map/ppermute | solution.py:31
  20.2 0.0 copy-done.1
  20.2 0.4 %shard_map.77.refs_2_ = f32[64,128]{1,0:T(8,128)S(1)} custom-call(bf16[64,3584]{1,0:T(8,128)(2,1)S(1)} %collective-permute-done.10.refs_0_, bf16[128,14336]{1,0:T(8,128)(2,1)S(1)} %copy-done.1, f32[64,128]{1,0:T(8,128)S(1)} %shard_map.73._.refs_5_.refs_2_), custom_call_target="tpu_custom_call" | custom-call | tf_op jit(solution)/shard_map/pallas_call | solution.py:95
  20.6 0.0 collective-permute-done.11.refs_0_
  20.6 1.1 %shard_map.78 = bf16[32,24,128]{2,1,0:T(8,128)(2,1)} custom-call(bf16[64,3584]{1,0:T(8,128)(2,1)S(1)} %collective-permute-done.11.refs_0_, bf16[128,14336]{1,0:T(8,128)(2,1)S(1)} %copy-done.1, f32[64,128]{1,0:T(8,128)S(1)} %shard_map.77.refs_2_, bf16[16,128]{1,0:T(8,128)(2,1)S(1)} %shard_map.74.refs_6_.refs_3_), custom_call_target="tpu_custom_call" | custom-call | tf_op jit(solution)/shard_map/pallas_call | solution.py:95
  21.7 5.9 %all-to-all-start = ((bf16[32,24,128]{2,1,0:T(8,128)(2,1)}), bf16[32,24,128]{2,1,0:T(8,128)(2,1)S(1)}, u32[]{:S(2)}, u32[]{:S(2)}) async-start(bf16[32,24,128]{2,1,0:T(8,128)(2,1)} %shard_map.78), calls=%async_computation | async-start | bytes 393216 | tf_op jit(solution)/shard_map/all_to_all | solution.py:223
  27.6 0.0 collective-permute-done.6
  27.6 1.8 %collective-permute-start.8 = (bf16[512,128]{1,0:T(8,128)(2,1)S(1)}, bf16[512,128]{1,0:T(8,128)(2,1)S(1)}, u32[]{:S(2)}, u32[]{:S(2)}) collective-permute-start(bf16[512,128]{1,0:T(8,128)(2,1)S(1)} %pad_maximum_fusion.refs_0_), channel_id=1, source_target_pairs={{0,2},{1,3},{2,0},{3,1},{4,6},{5,7},{6,4},{7,5},{8,10},{9,11},{10,... | collective-permute-start | bytes 393224 | tf_op jit(solution)/shard_map/ppermute | solution.py:31
  29.5 0.0 collective-permute-start.7
  29.5 5.6 %collective-permute-done.8.refs_2_ = bf16[512,128]{1,0:T(8,128)(2,1)S(1)} collective-permute-done((bf16[512,128]{1,0:T(8,128)(2,1)S(1)}, bf16[512,128]{1,0:T(8,128)(2,1)S(1)}, u32[]{:S(2)}, u32[]{:S(2)}) %collective-permute-start.8) | collective-permute-done | bytes 131104 | tf_op jit(solution)/shard_map/ppermute | solution.py:31
  35.1 0.0 collective-permute-start.9
  35.1 0.0 collective-permute-done.7.refs_1_
  35.1 1.3 %collective-permute-done.9.refs_3_ = bf16[512,128]{1,0:T(8,128)(2,1)S(1)} collective-permute-done((bf16[512,128]{1,0:T(8,128)(2,1)S(1)}, bf16[512,128]{1,0:T(8,128)(2,1)S(1)}, u32[]{:S(2)}, u32[]{:S(2)}) %collective-permute-start.9) | collective-permute-done | bytes 131104 | tf_op jit(solution)/shard_map/ppermute | solution.py:31
  36.4 0.2 shard_map.76.refs_4_
  36.7 0.0 all-to-all-done.refs_5_
  36.7 2.3 %shard_map.79 = f32[24,1024]{1,0:T(8,128)} custom-call(bf16[512,128]{1,0:T(8,128)(2,1)S(1)} %pad_maximum_fusion.refs_0_, bf16[512,128]{1,0:T(8,128)(2,1)S(1)} %collective-permute-done.7.refs_1_, bf16[512,128]{1,0:T(8,128)(2,1)S(1)} %collective-permute-done.8.refs_2_, bf16[512,128]{1,0:T(8,128)(2,1)S(1)} %collective-permute-done.9.refs_3_, ...), custom_call_target="tpu_custom_call" | custom-call | tf_op jit(solution)/shard_map/pallas_call | solution.py:95
  (3 shorter events, 0.0 us)
Async XLA Ops:
  0.0 7.7 %copy-start.4 = (s32[1,8]{1,0:T(1,128)S(1)}, s32[1,8]{1,0:T(1,128)}, u32[]{:S(2)}) copy-start(s32[1,8]{1,0:T(1,128)} %owner_dp.1) | copy-start | bytes 100
  0.0 7.7 %copy-start.5 = (s32[1,8]{1,0:T(1,128)S(1)}, s32[1,8]{1,0:T(1,128)}, u32[]{:S(2)}) copy-start(s32[1,8]{1,0:T(1,128)} %owner_slot.1) | copy-start | bytes 100
  0.0 7.7 %copy-start.3 = (s32[1,128]{1,0:T(1,128)S(1)}, s32[1,128]{1,0:T(1,128)}, u32[]{:S(2)}) copy-start(s32[1,128]{1,0:T(1,128)} %piece_of.1) | copy-start | bytes 1540
  0.0 3.3 %collective-permute-start.2 = (bf16[64,3584]{1,0:T(8,128)(2,1)}, bf16[64,3584]{1,0:T(8,128)(2,1)S(1)}, u32[]{:S(2)}, u32[]{:S(2)}) collective-permute-start(bf16[64,3584]{1,0:T(8,128)(2,1)} %bitcast.2), channel_id=1, source_target_pairs={{0,1},{1,0},{2,3},{3,2},{4,5},{5,4},{6,7},{7,6},{8,9},{9,8},{10,11... | collective-permute-start | bytes 1376264 | tf_op jit(solution)/shard_map/ppermute | solution.py:31
  0.5 7.1 %collective-permute-start.1 = (bf16[64,1024]{1,0:T(8,128)(2,1)}, bf16[64,1024]{1,0:T(8,128)(2,1)S(1)}, u32[]{:S(2)}, u32[]{:S(2)}) collective-permute-start(bf16[64,1024]{1,0:T(8,128)(2,1)} %bitcast.5), channel_id=1, source_target_pairs={{0,2},{1,3},{2,0},{3,1},{4,6},{5,7},{6,4},{7,5},{8,10},{9,11},{10,... | collective-permute-start | bytes 393224 | tf_op jit(solution)/shard_map/ppermute | solution.py:31
  3.1 14.1 %collective-permute-start.10 = (bf16[64,3584]{1,0:T(8,128)(2,1)}, bf16[64,3584]{1,0:T(8,128)(2,1)S(1)}, u32[]{:S(2)}, u32[]{:S(2)}) collective-permute-start(bf16[64,3584]{1,0:T(8,128)(2,1)} %bitcast.3), channel_id=1, source_target_pairs={{0,2},{1,3},{2,0},{3,1},{4,6},{5,7},{6,4},{7,5},{8,10},{9,11},{10,... | collective-permute-start | bytes 1376264 | tf_op jit(solution)/shard_map/ppermute | solution.py:31
  3.2 5.1 %collective-permute-start = (bf16[64,1024]{1,0:T(8,128)(2,1)}, bf16[64,1024]{1,0:T(8,128)(2,1)S(1)}, u32[]{:S(2)}, u32[]{:S(2)}) collective-permute-start(bf16[64,1024]{1,0:T(8,128)(2,1)} %bitcast.6), channel_id=1, source_target_pairs={{0,1},{1,0},{2,3},{3,2},{4,5},{5,4},{6,7},{7,6},{8,9},{9,8},{10,11... | collective-permute-start | bytes 393224 | tf_op jit(solution)/shard_map/ppermute | solution.py:31
  3.3 2.0 %copy-start = (bf16[128,14336]{1,0:T(8,128)(2,1)S(1)}, bf16[128,14336]{1,0:T(8,128)(2,1)}, u32[]{:S(2)}) copy-start(bf16[128,14336]{1,0:T(8,128)(2,1)} %refs_1_.3) | copy-start | bytes 11010052
  5.3 1.0 %copy-start.2 = (bf16[3584,64]{0,1:T(8,128)(2,1)S(1)}, bf16[3584,64]{0,1:T(8,128)(2,1)}, u32[]{:S(2)}) copy-start(bf16[3584,64]{0,1:T(8,128)(2,1)} %param.12) | copy-start | bytes 1376260
  6.3 2.7 %copy-start.6 = (bf16[128,4096]{1,0:T(8,128)(2,1)S(1)}, bf16[128,4096]{1,0:T(8,128)(2,1)}, u32[]{:S(2)}) copy-start(bf16[128,4096]{1,0:T(8,128)(2,1)} %refs_4_.1) | copy-start | bytes 3145732
  6.3 2.7 %copy-start.7 = (bf16[1024,64]{0,1:T(8,128)(2,1)S(1)}, bf16[1024,64]{0,1:T(8,128)(2,1)}, u32[]{:S(2)}) copy-start(bf16[1024,64]{0,1:T(8,128)(2,1)} %param.13) | copy-start | bytes 393220
  7.1 13.1 %copy-start.1 = (bf16[128,14336]{1,0:T(8,128)(2,1)S(1)}, bf16[128,14336]{1,0:T(8,128)(2,1)}, u32[]{:S(2)}) copy-start(bf16[128,14336]{1,0:T(8,128)(2,1)} %refs_1_.3) | copy-start | bytes 11010052
  7.7 1.3 %collective-permute-start.3 = (bf16[64,1024]{1,0:T(8,128)(2,1)S(1)}, bf16[64,1024]{1,0:T(8,128)(2,1)S(1)}, u32[]{:S(2)}, u32[]{:S(2)}) collective-permute-start(bf16[64,1024]{1,0:T(8,128)(2,1)S(1)} %collective-permute-done.1.refs_2_), channel_id=1, source_target_pairs={{0,1},{1,0},{2,3},{3,2},{4,5},{5,4},{6,7},{7,6},{8,9},{9,8},{10,11... | collective-permute-start | bytes 393224 | tf_op jit(solution)/shard_map/ppermute | solution.py:31
  9.5 3.8 %collective-permute-start.4 = (bf16[64,128]{1,0:T(8,128)(2,1)S(1)}, bf16[64,128]{1,0:T(8,128)(2,1)S(1)}, u32[]{:S(2)}, u32[]{:S(2)}) collective-permute-start(bf16[64,128]{1,0:T(8,128)(2,1)S(1)} %shard_map.75), channel_id=1, source_target_pairs={{0,8},{4,12},{8,0},{12,4},{16,24},{20,28},{24,16},{28,20},{1,9},{5... | collective-permute-start | bytes 49160 | tf_op jit(solution)/shard_map/ppermute | solution.py:31
  13.3 4.9 %collective-permute-start.5 = (bf16[128,128]{1,0:T(8,128)(2,1)S(1)}, bf16[128,128]{1,0:T(8,128)(2,1)S(1)}, u32[]{:S(2)}, u32[]{:S(2)}) collective-permute-start(bf16[128,128]{1,0:T(8,128)(2,1)S(1)} %pad_maximum_fusion.2), channel_id=1, source_target_pairs={{0,16},{4,20},{8,24},{12,28},{16,0},{20,4},{24,8},{28,12},{1,17},{... | collective-permute-start | bytes 98312 | tf_op jit(solution)/shard_map/ppermute | solution.py:31
  18.3 2.3 %collective-permute-start.11 = (bf16[64,3584]{1,0:T(8,128)(2,1)S(1)}, bf16[64,3584]{1,0:T(8,128)(2,1)S(1)}, u32[]{:S(2)}, u32[]{:S(2)}) collective-permute-start(bf16[64,3584]{1,0:T(8,128)(2,1)S(1)} %collective-permute-done.10.refs_0_), channel_id=1, source_target_pairs={{0,1},{1,0},{2,3},{3,2},{4,5},{5,4},{6,7},{7,6},{8,9},{9,8},{10,11... | collective-permute-start | bytes 1376264 | tf_op jit(solution)/shard_map/ppermute | solution.py:31
  18.3 9.3 %collective-permute-start.6 = (bf16[256,128]{1,0:T(8,128)(2,1)S(1)}, bf16[256,128]{1,0:T(8,128)(2,1)S(1)}, u32[]{:S(2)}, u32[]{:S(2)}) collective-permute-start(bf16[256,128]{1,0:T(8,128)(2,1)S(1)} %pad_maximum_fusion.1), channel_id=1, source_target_pairs={{0,4},{4,0},{8,12},{12,8},{16,20},{20,16},{24,28},{28,24},{1,5},{5... | collective-permute-start | bytes 196616 | tf_op jit(solution)/shard_map/ppermute | solution.py:31
  21.7 14.9 %all-to-all-start = ((bf16[32,24,128]{2,1,0:T(8,128)(2,1)}), bf16[32,24,128]{2,1,0:T(8,128)(2,1)S(1)}, u32[]{:S(2)}, u32[]{:S(2)}) async-start(bf16[32,24,128]{2,1,0:T(8,128)(2,1)} %shard_map.78), calls=%async_computation | async-start | bytes 393216 | tf_op jit(solution)/shard_map/all_to_all | solution.py:223
  27.6 7.5 %collective-permute-start.8 = (bf16[512,128]{1,0:T(8,128)(2,1)S(1)}, bf16[512,128]{1,0:T(8,128)(2,1)S(1)}, u32[]{:S(2)}, u32[]{:S(2)}) collective-permute-start(bf16[512,128]{1,0:T(8,128)(2,1)S(1)} %pad_maximum_fusion.refs_0_), channel_id=1, source_target_pairs={{0,2},{1,3},{2,0},{3,1},{4,6},{5,7},{6,4},{7,5},{8,10},{9,11},{10,... | collective-permute-start | bytes 393224 | tf_op jit(solution)/shard_map/ppermute | solution.py:31
  29.5 5.6 %collective-permute-start.7 = (bf16[512,128]{1,0:T(8,128)(2,1)S(1)}, bf16[512,128]{1,0:T(8,128)(2,1)S(1)}, u32[]{:S(2)}, u32[]{:S(2)}) collective-permute-start(bf16[512,128]{1,0:T(8,128)(2,1)S(1)} %pad_maximum_fusion.refs_0_), channel_id=1, source_target_pairs={{0,1},{1,0},{2,3},{3,2},{4,5},{5,4},{6,7},{7,6},{8,9},{9,8},{10,11... | collective-permute-start | bytes 393224 | tf_op jit(solution)/shard_map/ppermute | solution.py:31
  35.1 1.3 %collective-permute-start.9 = (bf16[512,128]{1,0:T(8,128)(2,1)S(1)}, bf16[512,128]{1,0:T(8,128)(2,1)S(1)}, u32[]{:S(2)}, u32[]{:S(2)}) collective-permute-start(bf16[512,128]{1,0:T(8,128)(2,1)S(1)} %collective-permute-done.8.refs_2_), channel_id=1, source_target_pairs={{0,1},{1,0},{2,3},{3,2},{4,5},{5,4},{6,7},{7,6},{8,9},{9,8},{10,11... | collective-permute-start | bytes 393224 | tf_op jit(solution)/shard_map/ppermute | solution.py:31

commit v5 on v4

--- a/solution.py
+++ b/solution.py
@@ -207,10 +207,9 @@
     order = [0]
     for bit in [*later, first]:
         order += [k ^ bit for k in order]
-    for bit in later:
-        errors = widen(errors, "dp", bit)
-        far_in = after(far_in, errors)
-    far_in = spread(far_in, low)
+    half = order[: len(order) // 2]
+    errors = jnp.concatenate([errors] + [swap(errors, "dp", k) for k in half[1:]], axis=0)
+    far_in = spread(after(far_in, errors), low)
     for k in range(top - 1):
         inputs = call(
             functools.partial(project_kernel, [top + k]), [far_in[k], hidden_in, inputs], square

time: 39.2 us -> 37.9 us (0.967)
  starting transfers between devices: 18 us -> 14.7 us
  waiting for transfers between devices: 11.9 us -> 13.8 us
    all_to_all x1, starting transfers between devices: 5.87 us -> 3.26 us  [by_tokens(): lax.all_to_all(messages, BOTH, split_axis=0, concat_axis=0, tiled=True)]
    ppermute x12 -> x13, waiting for transfers between devices: 11.9 us -> 13.8 us  [swap(): return lax.ppermute(value, axis, [(i, i ^ bit) for i in range(count)])]
    ppermute x12 -> x13, starting transfers between devices: 12.1 us -> 11.5 us  [swap(): return lax.ppermute(value, axis, [(i, i ^ bit) for i in range(count)])]
    unnamed x16 -> x20, local copies, waits for them, and re-layouts: 3.08 us -> 3.11 us
  transfers between devices with their start and end apart: 13 -> 14, of which waited for: 7 -> 6; matrix products, arithmetic and copies ran while one was open for 0% -> 0% of each run, Pallas kernels for 9% -> 9%
where the time goes in v5:
time: 37.9 us; the launch traced here: 37.6 us
  starting transfers between devices  14.7 us (39%)
  waiting for transfers between devices  13.8 us (36%)
  Pallas kernels  5.84 us (15%)
  local copies, waits for them, and re-layouts  3.12 us (8%)
    ppermute x13, waiting for transfers between devices, swap(): return lax.ppermute(value, axis, [(i, i ^ bit) for i in range(count)])  13.8 us
    ppermute x13, starting transfers between devices, swap(): return lax.ppermute(value, axis, [(i, i ^ bit) for i in range(count)])  11.5 us
    pallas_call x7, Pallas kernels, call(): pl.pallas_call(kernel, out_shape=outputs, in_specs=specs or [VMEM] * len(...  5.84 us
    all_to_all x1, starting transfers between devices, by_tokens(): lax.all_to_all(messages, BOTH, split_axis=0, concat_axis=0, tiled=True)  3.26 us
    unnamed x20, local copies, waits for them, and re-layouts  3.11 us
  transfers between devices with their start and end apart: 14, of which 6 were waited for; matrix products, arithmetic and copies ran while one was open for 0% of the time, Pallas kernels for 9%

profile of v5, /device:TPU:0, one launch (start us, length us, event | category | flops | bytes accessed | tf_op | source)
XLA Modules:
  0.0 37.6 jit_solution(7123436188351089079)
XLA Ops:
  0.0 0.0 copy-start.4
  0.0 0.0 copy-start.5
  0.0 0.0 copy-start.3
  0.0 0.5 %collective-permute-start.2 = (bf16[64,3584]{1,0:T(8,128)(2,1)}, bf16[64,3584]{1,0:T(8,128)(2,1)S(1)}, u32[]{:S(2)}, u32[]{:S(2)}) collective-permute-start(bf16[64,3584]{1,0:T(8,128)(2,1)} %bitcast.2), channel_id=1, source_target_pairs={{0,1},{1,0},{2,3},{3,2},{4,5},{5,4},{6,7},{7,6},{8,9},{9,8},{10,11... | collective-permute-start | bytes 1376264 | tf_op jit(solution)/shard_map/ppermute | solution.py:31
  0.5 2.6 %collective-permute-start.1 = (bf16[64,1024]{1,0:T(8,128)(2,1)}, bf16[64,1024]{1,0:T(8,128)(2,1)S(1)}, u32[]{:S(2)}, u32[]{:S(2)}) collective-permute-start(bf16[64,1024]{1,0:T(8,128)(2,1)} %bitcast.5), channel_id=1, source_target_pairs={{0,2},{1,3},{2,0},{3,1},{4,6},{5,7},{6,4},{7,5},{8,10},{9,11},{10,... | collective-permute-start | bytes 393224 | tf_op jit(solution)/shard_map/ppermute | solution.py:31
  3.1 0.1 collective-permute-start.11
  3.2 0.1 collective-permute-start
  3.3 0.0 collective-permute-done.2.refs_1_
  3.3 0.0 copy-start
  3.3 2.0 %copy-done = bf16[128,14336]{1,0:T(8,128)(2,1)S(1)} copy-done((bf16[128,14336]{1,0:T(8,128)(2,1)S(1)}, bf16[128,14336]{1,0:T(8,128)(2,1)}, u32[]{:S(2)}) %copy-start) | copy-done | bytes 3670040
  5.3 0.0 copy-start.2
  5.3 1.0 %copy-done.2 = bf16[3584,64]{0,1:T(8,128)(2,1)S(1)} copy-done((bf16[3584,64]{0,1:T(8,128)(2,1)S(1)}, bf16[3584,64]{0,1:T(8,128)(2,1)}, u32[]{:S(2)}) %copy-start.2) | copy-done | bytes 458776
  6.3 0.0 copy-start.6
  6.3 0.0 copy-start.7
  6.3 0.7 %shard_map.73._.refs_5_.refs_2_ = f32[64,128]{1,0:T(8,128)S(1)} custom-call(bf16[64,3584]{1,0:T(8,128)(2,1)S(1)} %bitcast.4, bf16[64,3584]{1,0:T(8,128)(2,1)S(1)} %collective-permute-done.2.refs_1_, bf16[128,14336]{1,0:T(8,128)(2,1)S(1)} %copy-done), custom_call_target="tpu_custom_call" | custom-call | tf_op jit(solution)/shard_map/pallas_call | solution.py:95
  7.1 0.0 copy-start.1
  7.1 0.5 %collective-permute-done.1.refs_2_ = bf16[64,1024]{1,0:T(8,128)(2,1)S(1)} collective-permute-done((bf16[64,1024]{1,0:T(8,128)(2,1)}, bf16[64,1024]{1,0:T(8,128)(2,1)S(1)}, u32[]{:S(2)}, u32[]{:S(2)}) %collective-permute-start.1) | collective-permute-done | bytes 131104 | tf_op jit(solution)/shard_map/ppermute | solution.py:31
  7.7 0.0 collective-permute-start.3
  7.7 0.0 copy-done.4
  7.7 0.0 copy-done.5
  7.7 0.0 copy-done.3
  7.7 0.6 %shard_map.74.refs_6_.refs_3_ = bf16[16,128]{1,0:T(8,128)(2,1)S(1)} custom-call(s32[1,128]{1,0:T(1,128)S(1)} %copy-done.3, s32[1,8]{1,0:T(1,128)S(1)} %copy-done.4, s32[1,8]{1,0:T(1,128)S(1)} %copy-done.5, f32[64,128]{1,0:T(8,128)S(1)} %shard_map.73._.refs_5_.refs_2_), custom_call_target="tpu_custom_call" | custom-call | tf_op jit(solution)/shard_map/pallas_call | solution.py:95
  8.2 0.0 collective-permute-done.refs_1_
  8.2 0.8 %collective-permute-done.3.refs_3_ = bf16[64,1024]{1,0:T(8,128)(2,1)S(1)} collective-permute-done((bf16[64,1024]{1,0:T(8,128)(2,1)S(1)}, bf16[64,1024]{1,0:T(8,128)(2,1)S(1)}, u32[]{:S(2)}, u32[]{:S(2)}) %collective-permute-start.3) | collective-permute-done | bytes 131104 | tf_op jit(solution)/shard_map/ppermute | solution.py:31
  9.0 0.0 copy-done.6
  9.0 0.0 copy-done.7
  9.0 0.5 %shard_map.75 = bf16[64,128]{1,0:T(8,128)(2,1)S(1)} custom-call(bf16[64,1024]{1,0:T(8,128)(2,1)S(1)} %bitcast.7, bf16[64,1024]{1,0:T(8,128)(2,1)S(1)} %collective-permute-done.refs_1_, bf16[64,1024]{1,0:T(8,128)(2,1)S(1)} %collective-permute-done.1.refs_2_, bf16[64,1024]{1,0:T(8,128)(2,1)S(1)} %collective-permute-done.3.refs_3_, ...), custom_call_target="tpu_custom_call" | custom-call | flops 1500000000 | bytes 1000000 | tf_op jit(solution)/shard_map/pallas_call | solution.py:95
  9.5 2.1 %collective-permute-start.4 = (bf16[64,128]{1,0:T(8,128)(2,1)S(1)}, bf16[64,128]{1,0:T(8,128)(2,1)S(1)}, u32[]{:S(2)}, u32[]{:S(2)}) collective-permute-start(bf16[64,128]{1,0:T(8,128)(2,1)S(1)} %shard_map.75), channel_id=1, source_target_pairs={{0,8},{4,12},{8,0},{12,4},{16,24},{20,28},{24,16},{28,20},{1,9},{5... | collective-permute-start | bytes 49160 | tf_op jit(solution)/shard_map/ppermute | solution.py:31
  11.6 2.6 %collective-permute-start.5 = (bf16[64,128]{1,0:T(8,128)(2,1)S(1)}, bf16[64,128]{1,0:T(8,128)(2,1)S(1)}, u32[]{:S(2)}, u32[]{:S(2)}) collective-permute-start(bf16[64,128]{1,0:T(8,128)(2,1)S(1)} %shard_map.75), channel_id=1, source_target_pairs={{0,16},{4,20},{8,24},{12,28},{16,0},{20,4},{24,8},{28,12},{1,17},{... | collective-permute-start | bytes 49160 | tf_op jit(solution)/shard_map/ppermute | solution.py:31
  14.2 0.0 collective-permute-start.6
  14.2 0.0 collective-permute-done.4
  14.2 2.0 %collective-permute-done.5 = bf16[64,128]{1,0:T(8,128)(2,1)S(1)} collective-permute-done((bf16[64,128]{1,0:T(8,128)(2,1)S(1)}, bf16[64,128]{1,0:T(8,128)(2,1)S(1)}, u32[]{:S(2)}, u32[]{:S(2)}) %collective-permute-start.5) | collective-permute-done | bytes 16416 | tf_op jit(solution)/shard_map/ppermute | solution.py:31
  16.2 3.5 %collective-permute-done.6 = bf16[64,128]{1,0:T(8,128)(2,1)S(1)} collective-permute-done((bf16[64,128]{1,0:T(8,128)(2,1)S(1)}, bf16[64,128]{1,0:T(8,128)(2,1)S(1)}, u32[]{:S(2)}, u32[]{:S(2)}) %collective-permute-start.6) | collective-permute-done | bytes 16416 | tf_op jit(solution)/shard_map/ppermute | solution.py:31
  19.7 0.0 collective-permute-done.11.refs_0_
  19.7 0.1 collective-permute-start.12
  19.8 0.0 copy-done.1
  19.8 0.4 %shard_map.77.refs_2_ = f32[64,128]{1,0:T(8,128)S(1)} custom-call(bf16[64,3584]{1,0:T(8,128)(2,1)S(1)} %collective-permute-done.11.refs_0_, bf16[128,14336]{1,0:T(8,128)(2,1)S(1)} %copy-done.1, f32[64,128]{1,0:T(8,128)S(1)} %shard_map.73._.refs_5_.refs_2_), custom_call_target="tpu_custom_call" | custom-call | tf_op jit(solution)/shard_map/pallas_call | solution.py:95
  20.3 1.6 %collective-permute-start.7 = (bf16[256,128]{1,0:T(8,128)(2,1)S(1)}, bf16[256,128]{1,0:T(8,128)(2,1)S(1)}, u32[]{:S(2)}, u32[]{:S(2)}) collective-permute-start(bf16[256,128]{1,0:T(8,128)(2,1)S(1)} %pad_maximum_fusion), channel_id=1, source_target_pairs={{0,4},{4,0},{8,12},{12,8},{16,20},{20,16},{24,28},{28,24},{1,5},{5... | collective-permute-start | bytes 196616 | tf_op jit(solution)/shard_map/ppermute | solution.py:31
  21.9 0.0 collective-permute-done.12.refs_0_
  21.9 1.1 %shard_map.78 = bf16[32,24,128]{2,1,0:T(8,128)(2,1)} custom-call(bf16[64,3584]{1,0:T(8,128)(2,1)S(1)} %collective-permute-done.12.refs_0_, bf16[128,14336]{1,0:T(8,128)(2,1)S(1)} %copy-done.1, f32[64,128]{1,0:T(8,128)S(1)} %shard_map.77.refs_2_, bf16[16,128]{1,0:T(8,128)(2,1)S(1)} %shard_map.74.refs_6_.refs_3_), custom_call_target="tpu_custom_call" | custom-call | tf_op jit(solution)/shard_map/pallas_call | solution.py:95
  23.0 3.3 %all-to-all-start = ((bf16[32,24,128]{2,1,0:T(8,128)(2,1)}), bf16[32,24,128]{2,1,0:T(8,128)(2,1)S(1)}, u32[]{:S(2)}, u32[]{:S(2)}) async-start(bf16[32,24,128]{2,1,0:T(8,128)(2,1)} %shard_map.78), calls=%async_computation | async-start | bytes 393216 | tf_op jit(solution)/shard_map/all_to_all | solution.py:222
  26.3 0.0 collective-permute-done.7
  26.3 1.8 %collective-permute-start.9 = (bf16[512,128]{1,0:T(8,128)(2,1)S(1)}, bf16[512,128]{1,0:T(8,128)(2,1)S(1)}, u32[]{:S(2)}, u32[]{:S(2)}) collective-permute-start(bf16[512,128]{1,0:T(8,128)(2,1)S(1)} %constant_dynamic-update-slice_fusion.refs_0_), channel_id=1, source_target_pairs={{0,2},{1,3},{2,0},{3,1},{4,6},{5,7},{6,4},{7,5},{8,10},{9,11},{10,... | collective-permute-start | bytes 393224 | tf_op jit(solution)/shard_map/ppermute | solution.py:31
  28.2 0.0 collective-permute-start.8
  28.2 5.6 %collective-permute-done.9.refs_2_ = bf16[512,128]{1,0:T(8,128)(2,1)S(1)} collective-permute-done((bf16[512,128]{1,0:T(8,128)(2,1)S(1)}, bf16[512,128]{1,0:T(8,128)(2,1)S(1)}, u32[]{:S(2)}, u32[]{:S(2)}) %collective-permute-start.9) | collective-permute-done | bytes 131104 | tf_op jit(solution)/shard_map/ppermute | solution.py:31
  33.8 0.0 collective-permute-start.10
  33.8 0.0 collective-permute-done.8.refs_1_
  33.8 1.3 %collective-permute-done.10.refs_3_ = bf16[512,128]{1,0:T(8,128)(2,1)S(1)} collective-permute-done((bf16[512,128]{1,0:T(8,128)(2,1)S(1)}, bf16[512,128]{1,0:T(8,128)(2,1)S(1)}, u32[]{:S(2)}, u32[]{:S(2)}) %collective-permute-start.10) | collective-permute-done | bytes 131104 | tf_op jit(solution)/shard_map/ppermute | solution.py:31
  35.1 0.2 shard_map.76.refs_4_
  35.3 0.0 all-to-all-done.refs_5_
  35.4 2.3 %shard_map.79 = f32[24,1024]{1,0:T(8,128)} custom-call(bf16[512,128]{1,0:T(8,128)(2,1)S(1)} %constant_dynamic-update-slice_fusion.refs_0_, bf16[512,128]{1,0:T(8,128)(2,1)S(1)} %collective-permute-done.8.refs_1_, bf16[512,128]{1,0:T(8,128)(2,1)S(1)} %collective-permute-done.9.refs_2_, bf16[512,128]{1,0:T(8,128)(2,1)S(1)} %collective-permute-done.10.refs_3_, ...), custom_call_target="tpu_custom_call" | custom-call | tf_op jit(solution)/shard_map/pallas_call | solution.py:95
  (6 shorter events, 0.0 us)
Async XLA Ops:
  0.0 7.7 %copy-start.4 = (s32[1,8]{1,0:T(1,128)S(1)}, s32[1,8]{1,0:T(1,128)}, u32[]{:S(2)}) copy-start(s32[1,8]{1,0:T(1,128)} %owner_dp.1) | copy-start | bytes 100
  0.0 7.7 %copy-start.5 = (s32[1,8]{1,0:T(1,128)S(1)}, s32[1,8]{1,0:T(1,128)}, u32[]{:S(2)}) copy-start(s32[1,8]{1,0:T(1,128)} %owner_slot.1) | copy-start | bytes 100
  0.0 7.7 %copy-start.3 = (s32[1,128]{1,0:T(1,128)S(1)}, s32[1,128]{1,0:T(1,128)}, u32[]{:S(2)}) copy-start(s32[1,128]{1,0:T(1,128)} %piece_of.1) | copy-start | bytes 1540
  0.0 3.3 %collective-permute-start.2 = (bf16[64,3584]{1,0:T(8,128)(2,1)}, bf16[64,3584]{1,0:T(8,128)(2,1)S(1)}, u32[]{:S(2)}, u32[]{:S(2)}) collective-permute-start(bf16[64,3584]{1,0:T(8,128)(2,1)} %bitcast.2), channel_id=1, source_target_pairs={{0,1},{1,0},{2,3},{3,2},{4,5},{5,4},{6,7},{7,6},{8,9},{9,8},{10,11... | collective-permute-start | bytes 1376264 | tf_op jit(solution)/shard_map/ppermute | solution.py:31
  0.5 7.1 %collective-permute-start.1 = (bf16[64,1024]{1,0:T(8,128)(2,1)}, bf16[64,1024]{1,0:T(8,128)(2,1)S(1)}, u32[]{:S(2)}, u32[]{:S(2)}) collective-permute-start(bf16[64,1024]{1,0:T(8,128)(2,1)} %bitcast.5), channel_id=1, source_target_pairs={{0,2},{1,3},{2,0},{3,1},{4,6},{5,7},{6,4},{7,5},{8,10},{9,11},{10,... | collective-permute-start | bytes 393224 | tf_op jit(solution)/shard_map/ppermute | solution.py:31
  3.1 16.6 %collective-permute-start.11 = (bf16[64,3584]{1,0:T(8,128)(2,1)}, bf16[64,3584]{1,0:T(8,128)(2,1)S(1)}, u32[]{:S(2)}, u32[]{:S(2)}) collective-permute-start(bf16[64,3584]{1,0:T(8,128)(2,1)} %bitcast.3), channel_id=1, source_target_pairs={{0,2},{1,3},{2,0},{3,1},{4,6},{5,7},{6,4},{7,5},{8,10},{9,11},{10,... | collective-permute-start | bytes 1376264 | tf_op jit(solution)/shard_map/ppermute | solution.py:31
  3.2 5.1 %collective-permute-start = (bf16[64,1024]{1,0:T(8,128)(2,1)}, bf16[64,1024]{1,0:T(8,128)(2,1)S(1)}, u32[]{:S(2)}, u32[]{:S(2)}) collective-permute-start(bf16[64,1024]{1,0:T(8,128)(2,1)} %bitcast.6), channel_id=1, source_target_pairs={{0,1},{1,0},{2,3},{3,2},{4,5},{5,4},{6,7},{7,6},{8,9},{9,8},{10,11... | collective-permute-start | bytes 393224 | tf_op jit(solution)/shard_map/ppermute | solution.py:31
  3.3 2.0 %copy-start = (bf16[128,14336]{1,0:T(8,128)(2,1)S(1)}, bf16[128,14336]{1,0:T(8,128)(2,1)}, u32[]{:S(2)}) copy-start(bf16[128,14336]{1,0:T(8,128)(2,1)} %refs_1_.3) | copy-start | bytes 11010052
  5.3 1.0 %copy-start.2 = (bf16[3584,64]{0,1:T(8,128)(2,1)S(1)}, bf16[3584,64]{0,1:T(8,128)(2,1)}, u32[]{:S(2)}) copy-start(bf16[3584,64]{0,1:T(8,128)(2,1)} %param.12) | copy-start | bytes 1376260
  6.3 2.7 %copy-start.6 = (bf16[128,4096]{1,0:T(8,128)(2,1)S(1)}, bf16[128,4096]{1,0:T(8,128)(2,1)}, u32[]{:S(2)}) copy-start(bf16[128,4096]{1,0:T(8,128)(2,1)} %refs_4_.1) | copy-start | bytes 3145732
  6.3 2.7 %copy-start.7 = (bf16[1024,64]{0,1:T(8,128)(2,1)S(1)}, bf16[1024,64]{0,1:T(8,128)(2,1)}, u32[]{:S(2)}) copy-start(bf16[1024,64]{0,1:T(8,128)(2,1)} %param.13) | copy-start | bytes 393220
  7.1 12.7 %copy-start.1 = (bf16[128,14336]{1,0:T(8,128)(2,1)S(1)}, bf16[128,14336]{1,0:T(8,128)(2,1)}, u32[]{:S(2)}) copy-start(bf16[128,14336]{1,0:T(8,128)(2,1)} %refs_1_.3) | copy-start | bytes 11010052
  7.7 1.3 %collective-permute-start.3 = (bf16[64,1024]{1,0:T(8,128)(2,1)S(1)}, bf16[64,1024]{1,0:T(8,128)(2,1)S(1)}, u32[]{:S(2)}, u32[]{:S(2)}) collective-permute-start(bf16[64,1024]{1,0:T(8,128)(2,1)S(1)} %collective-permute-done.1.refs_2_), channel_id=1, source_target_pairs={{0,1},{1,0},{2,3},{3,2},{4,5},{5,4},{6,7},{7,6},{8,9},{9,8},{10,11... | collective-permute-start | bytes 393224 | tf_op jit(solution)/shard_map/ppermute | solution.py:31
  9.5 4.7 %collective-permute-start.4 = (bf16[64,128]{1,0:T(8,128)(2,1)S(1)}, bf16[64,128]{1,0:T(8,128)(2,1)S(1)}, u32[]{:S(2)}, u32[]{:S(2)}) collective-permute-start(bf16[64,128]{1,0:T(8,128)(2,1)S(1)} %shard_map.75), channel_id=1, source_target_pairs={{0,8},{4,12},{8,0},{12,4},{16,24},{20,28},{24,16},{28,20},{1,9},{5... | collective-permute-start | bytes 49160 | tf_op jit(solution)/shard_map/ppermute | solution.py:31
  11.6 4.6 %collective-permute-start.5 = (bf16[64,128]{1,0:T(8,128)(2,1)S(1)}, bf16[64,128]{1,0:T(8,128)(2,1)S(1)}, u32[]{:S(2)}, u32[]{:S(2)}) collective-permute-start(bf16[64,128]{1,0:T(8,128)(2,1)S(1)} %shard_map.75), channel_id=1, source_target_pairs={{0,16},{4,20},{8,24},{12,28},{16,0},{20,4},{24,8},{28,12},{1,17},{... | collective-permute-start | bytes 49160 | tf_op jit(solution)/shard_map/ppermute | solution.py:31
  14.2 5.5 %collective-permute-start.6 = (bf16[64,128]{1,0:T(8,128)(2,1)S(1)}, bf16[64,128]{1,0:T(8,128)(2,1)S(1)}, u32[]{:S(2)}, u32[]{:S(2)}) collective-permute-start(bf16[64,128]{1,0:T(8,128)(2,1)S(1)} %shard_map.75), channel_id=1, source_target_pairs={{0,24},{4,28},{8,16},{12,20},{16,8},{20,12},{24,0},{28,4},{1,25},{... | collective-permute-start | bytes 49160 | tf_op jit(solution)/shard_map/ppermute | solution.py:31
  19.7 2.2 %collective-permute-start.12 = (bf16[64,3584]{1,0:T(8,128)(2,1)S(1)}, bf16[64,3584]{1,0:T(8,128)(2,1)S(1)}, u32[]{:S(2)}, u32[]{:S(2)}) collective-permute-start(bf16[64,3584]{1,0:T(8,128)(2,1)S(1)} %collective-permute-done.11.refs_0_), channel_id=1, source_target_pairs={{0,1},{1,0},{2,3},{3,2},{4,5},{5,4},{6,7},{7,6},{8,9},{9,8},{10,11... | collective-permute-start | bytes 1376264 | tf_op jit(solution)/shard_map/ppermute | solution.py:31
  20.3 6.0 %collective-permute-start.7 = (bf16[256,128]{1,0:T(8,128)(2,1)S(1)}, bf16[256,128]{1,0:T(8,128)(2,1)S(1)}, u32[]{:S(2)}, u32[]{:S(2)}) collective-permute-start(bf16[256,128]{1,0:T(8,128)(2,1)S(1)} %pad_maximum_fusion), channel_id=1, source_target_pairs={{0,4},{4,0},{8,12},{12,8},{16,20},{20,16},{24,28},{28,24},{1,5},{5... | collective-permute-start | bytes 196616 | tf_op jit(solution)/shard_map/ppermute | solution.py:31
  23.0 12.3 %all-to-all-start = ((bf16[32,24,128]{2,1,0:T(8,128)(2,1)}), bf16[32,24,128]{2,1,0:T(8,128)(2,1)S(1)}, u32[]{:S(2)}, u32[]{:S(2)}) async-start(bf16[32,24,128]{2,1,0:T(8,128)(2,1)} %shard_map.78), calls=%async_computation | async-start | bytes 393216 | tf_op jit(solution)/shard_map/all_to_all | solution.py:222
  26.3 7.5 %collective-permute-start.9 = (bf16[512,128]{1,0:T(8,128)(2,1)S(1)}, bf16[512,128]{1,0:T(8,128)(2,1)S(1)}, u32[]{:S(2)}, u32[]{:S(2)}) collective-permute-start(bf16[512,128]{1,0:T(8,128)(2,1)S(1)} %constant_dynamic-update-slice_fusion.refs_0_), channel_id=1, source_target_pairs={{0,2},{1,3},{2,0},{3,1},{4,6},{5,7},{6,4},{7,5},{8,10},{9,11},{10,... | collective-permute-start | bytes 393224 | tf_op jit(solution)/shard_map/ppermute | solution.py:31
  28.2 5.6 %collective-permute-start.8 = (bf16[512,128]{1,0:T(8,128)(2,1)S(1)}, bf16[512,128]{1,0:T(8,128)(2,1)S(1)}, u32[]{:S(2)}, u32[]{:S(2)}) collective-permute-start(bf16[512,128]{1,0:T(8,128)(2,1)S(1)} %constant_dynamic-update-slice_fusion.refs_0_), channel_id=1, source_target_pairs={{0,1},{1,0},{2,3},{3,2},{4,5},{5,4},{6,7},{7,6},{8,9},{9,8},{10,11... | collective-permute-start | bytes 393224 | tf_op jit(solution)/shard_map/ppermute | solution.py:31
  33.8 1.3 %collective-permute-start.10 = (bf16[512,128]{1,0:T(8,128)(2,1)S(1)}, bf16[512,128]{1,0:T(8,128)(2,1)S(1)}, u32[]{:S(2)}, u32[]{:S(2)}) collective-permute-start(bf16[512,128]{1,0:T(8,128)(2,1)S(1)} %collective-permute-done.9.refs_2_), channel_id=1, source_target_pairs={{0,1},{1,0},{2,3},{3,2},{4,5},{5,4},{6,7},{7,6},{8,9},{9,8},{10,11... | collective-permute-start | bytes 393224 | tf_op jit(solution)/shard_map/ppermute | solution.py:31

commit v6 on v5

--- a/solution.py
+++ b/solution.py
@@ -20,9 +20,6 @@
 ERRORS_COST = pl.CostEstimate(
     flops=1_500_000_000, bytes_accessed=1_000_000, transcendentals=0
 )
-PICKED_COST = pl.CostEstimate(
-    flops=600_000_000, bytes_accessed=1_000_000, transcendentals=0
-)
 ROOM = pltpu.CompilerParams(vmem_limit_bytes=16 * 1024 * 1024)
 
 
@@ -107,65 +104,47 @@
     refs[-1][...] = low_rank(refs[:count], which, refs[count]).astype(BF16)
 
 
-def picked_kernel(*refs):
-    out = refs[-1]
-    rows, count = out.shape[0], out.shape[1] // refs[0].shape[1]
-    width = len(refs[:-1]) * refs[0].shape[0] // count
-    column = lax.axis_index("dp") * rows + lax.broadcasted_iota(jnp.int32, (rows, width), 0)
-    at = lax.broadcasted_iota(jnp.int32, (rows, width), 1)
-    pick = (at == column % width).astype(F32).astype(BF16)
-    err = jnp.concatenate(
-        [ref[k : k + width, :] for ref in refs[:-1] for k in range(0, ref.shape[0], width)], axis=1
-    )
-    out[...] = jnp.dot(pick, err, preferred_element_type=F32)
-
-
 def gram_kernel(order, lead, group_examples, scale, *refs):
-    errors, picked, messages, out = refs[:-3], refs[-3], refs[-2], refs[-1]
+    errors, messages, out = refs[:-2], refs[-2], refs[-1]
     count_fsdp, count_dp = len(errors), len(order)
     rows_here, columns_here = out.shape
     width = errors[0].shape[0] // count_dp
     mine = columns_here // width
     d, f = lax.axis_index("dp"), lax.axis_index("fsdp")
-    wide, narrow = [], []
+    wide = []
     for g, e_ref in enumerate(errors):
         places = [(d ^ k) * count_fsdp + (f ^ g) for k in order]
         err = jnp.concatenate([e_ref[k * width : (k + 1) * width, :] for k in range(count_dp)], axis=1)
-        held = jnp.concatenate([messages[k] for k in places], axis=1)
-        here, shared = held[:mine, :], held[mine:, :]
-        key = shared.astype(F32)[lead : lead + 1, :]
-        tokens = key.shape[1]
-        example = lax.broadcasted_iota(jnp.int32, (group_examples, tokens), 0).astype(F32)
+        low = jnp.concatenate([messages[k] for k in places], axis=1)
+        key = low.astype(F32)[mine + lead : mine + lead + 1, :]
+        example = lax.broadcasted_iota(jnp.int32, (group_examples, key.shape[1]), 0).astype(F32)
         member = (example == key).astype(F32).astype(BF16)
-        spread_rows = [member * here[i : i + 1, :] for i in range(mine)]
-        spread_rows = jnp.concatenate(
-            [jnp.concatenate(spread_rows[i : i + 2], axis=1) for i in range(0, mine, 2)], axis=0
+        rows = [member * low[i : i + 1, :] for i in range(mine + lead + lead % 2)]
+        rows = jnp.concatenate(
+            [jnp.concatenate(rows[i : i + 2], axis=1) for i in range(0, len(rows), 2)], axis=0
         )
         blank = jnp.zeros_like(err)
         twice = jnp.concatenate(
             [jnp.concatenate([err, blank], axis=1), jnp.concatenate([blank, err], axis=1)], axis=0
         )
         wide.append(
-            lax.dot_general(spread_rows, twice, CONTRACT_LAST, preferred_element_type=F32).astype(BF16)
-        )
-        column = d * rows_here + lax.broadcasted_iota(jnp.int32, (rows_here, tokens), 0)
-        shared = shared.astype(F32)
-        chosen = shared[:1, :]
-        for i in range(1, lead):
-            chosen = jnp.where(column >= i * width, shared[i : i + 1, :], chosen)
-        product = chosen * picked[:, g * tokens : (g + 1) * tokens]
-        upper = product.astype(BF16)
-        lower = (product - upper.astype(F32)).astype(BF16)
-        part = lax.dot_general(upper, member, CONTRACT_LAST, preferred_element_type=F32)
-        part += lax.dot_general(lower, member, CONTRACT_LAST, preferred_element_type=F32)
-        narrow.append(part.astype(BF16))
-    left = jnp.concatenate(narrow, axis=1)
-    blocks = []
-    for i in range(mine // 2):
-        right = jnp.concatenate(
+            lax.dot_general(rows, twice, CONTRACT_LAST, preferred_element_type=F32).astype(BF16)
+        )
+
+    def pair(i):
+        return jnp.concatenate(
             [w[i * group_examples : (i + 1) * group_examples, :] for w in wide], axis=0
         )
-        blocks.append(jnp.dot(left, right, preferred_element_type=F32))
+
+    grid = (rows_here, 2 * width)
+    column = d * rows_here + lax.broadcasted_iota(jnp.int32, grid, 0)
+    at = lax.broadcasted_iota(jnp.int32, grid, 1)
+    left = 0.0
+    for i in range((lead + 1) // 2):
+        pick = (at + 2 * width * i == column).astype(F32).astype(BF16)
+        left += lax.dot_general(pick, pair(mine // 2 + i), CONTRACT_LAST, preferred_element_type=F32)
+    left = left.astype(BF16)
+    blocks = [jnp.dot(left, pair(i), preferred_element_type=F32) for i in range(mine // 2)]
     out[...] = jnp.concatenate(blocks, axis=1) * scale
 
 
@@ -221,16 +200,10 @@
     )
     messages = lax.all_to_all(messages, BOTH, split_axis=0, concat_axis=0, tiled=True)
     all_errors = spread(widen(errors, "dp", first), bits)
-    picked = call(
-        picked_kernel,
-        all_errors,
-        jax.ShapeDtypeStruct((rows_here, count_dp * count_fsdp * token_rows), F32),
-        cost=PICKED_COST,
-    )
     scale = 1.0 / math.sqrt(owned * count_dp * count_fsdp)
     return call(
         functools.partial(gram_kernel, order, lead, owned * count_dp, scale),
-        [*all_errors, picked, messages],
+        [*all_errors, messages],
         jax.ShapeDtypeStruct((rows_here, width * width // count_fsdp), F32),
     )
 

time: 37.9 us -> 38.1 us (level)
    pallas_call x7 -> x6, Pallas kernels: 5.84 us -> 5.83 us  [call(): pl.pallas_call(kernel, out_shape=outputs, in_specs=specs or [VMEM] * len(...]
where the time goes in v6:
time: 38.1 us; the launch traced here: 37.7 us
  starting transfers between devices  14.7 us (39%)
  waiting for transfers between devices  13.8 us (36%)
  Pallas kernels  5.83 us (15%)
  local copies, waits for them, and re-layouts  3.12 us (8%)
    ppermute x13, waiting for transfers between devices, swap(): return lax.ppermute(value, axis, [(i, i ^ bit) for i in range(count)])  13.8 us
    ppermute x13, starting transfers between devices, swap(): return lax.ppermute(value, axis, [(i, i ^ bit) for i in range(count)])  11.5 us
    pallas_call x6, Pallas kernels, call(): pl.pallas_call(kernel, out_shape=outputs, in_specs=specs or [VMEM] * len(...  5.83 us
    all_to_all x1, starting transfers between devices, by_tokens(): lax.all_to_all(messages, BOTH, split_axis=0, concat_axis=0, tiled=True)  3.27 us
    unnamed x20, local copies, waits for them, and re-layouts  3.11 us
  transfers between devices with their start and end apart: 14, of which 6 were waited for; matrix products, arithmetic and copies ran while one was open for 0% of the time, Pallas kernels for 9%

profile of v6, /device:TPU:0, one launch (start us, length us, event | category | flops | bytes accessed | tf_op | source)
XLA Modules:
  0.0 37.7 jit_solution(602300478865313467)
XLA Ops:
  0.0 0.0 copy-start.4
  0.0 0.0 copy-start.5
  0.0 0.0 copy-start.3
  0.0 0.5 %collective-permute-start.2 = (bf16[64,3584]{1,0:T(8,128)(2,1)}, bf16[64,3584]{1,0:T(8,128)(2,1)S(1)}, u32[]{:S(2)}, u32[]{:S(2)}) collective-permute-start(bf16[64,3584]{1,0:T(8,128)(2,1)} %bitcast.2), channel_id=1, source_target_pairs={{0,1},{1,0},{2,3},{3,2},{4,5},{5,4},{6,7},{7,6},{8,9},{9,8},{10,11... | collective-permute-start | bytes 1376264 | tf_op jit(solution)/shard_map/ppermute | solution.py:28
  0.5 2.6 %collective-permute-start.1 = (bf16[64,1024]{1,0:T(8,128)(2,1)}, bf16[64,1024]{1,0:T(8,128)(2,1)S(1)}, u32[]{:S(2)}, u32[]{:S(2)}) collective-permute-start(bf16[64,1024]{1,0:T(8,128)(2,1)} %bitcast.5), channel_id=1, source_target_pairs={{0,2},{1,3},{2,0},{3,1},{4,6},{5,7},{6,4},{7,5},{8,10},{9,11},{10,... | collective-permute-start | bytes 393224 | tf_op jit(solution)/shard_map/ppermute | solution.py:28
  3.1 0.1 collective-permute-start.11
  3.2 0.1 collective-permute-start
  3.3 0.0 collective-permute-done.2.refs_1_
  3.3 0.0 copy-start
  3.3 2.0 %copy-done = bf16[128,14336]{1,0:T(8,128)(2,1)S(1)} copy-done((bf16[128,14336]{1,0:T(8,128)(2,1)S(1)}, bf16[128,14336]{1,0:T(8,128)(2,1)}, u32[]{:S(2)}) %copy-start) | copy-done | bytes 3670040
  5.3 0.0 copy-start.2
  5.3 1.0 %copy-done.2 = bf16[3584,64]{0,1:T(8,128)(2,1)S(1)} copy-done((bf16[3584,64]{0,1:T(8,128)(2,1)S(1)}, bf16[3584,64]{0,1:T(8,128)(2,1)}, u32[]{:S(2)}) %copy-start.2) | copy-done | bytes 458776
  6.3 0.0 copy-start.6
  6.3 0.0 copy-start.7
  6.3 0.7 %shard_map.73._.refs_5_.refs_2_ = f32[64,128]{1,0:T(8,128)S(1)} custom-call(bf16[64,3584]{1,0:T(8,128)(2,1)S(1)} %bitcast.4, bf16[64,3584]{1,0:T(8,128)(2,1)S(1)} %collective-permute-done.2.refs_1_, bf16[128,14336]{1,0:T(8,128)(2,1)S(1)} %copy-done), custom_call_target="tpu_custom_call" | custom-call | tf_op jit(solution)/shard_map/pallas_call | solution.py:92
  7.1 0.0 copy-start.1
  7.1 0.5 %collective-permute-done.1.refs_2_ = bf16[64,1024]{1,0:T(8,128)(2,1)S(1)} collective-permute-done((bf16[64,1024]{1,0:T(8,128)(2,1)}, bf16[64,1024]{1,0:T(8,128)(2,1)S(1)}, u32[]{:S(2)}, u32[]{:S(2)}) %collective-permute-start.1) | collective-permute-done | bytes 131104 | tf_op jit(solution)/shard_map/ppermute | solution.py:28
  7.7 0.0 collective-permute-start.3
  7.7 0.0 copy-done.4
  7.7 0.0 copy-done.5
  7.7 0.0 copy-done.3
  7.7 0.6 %shard_map.74.refs_6_.refs_3_ = bf16[16,128]{1,0:T(8,128)(2,1)S(1)} custom-call(s32[1,128]{1,0:T(1,128)S(1)} %copy-done.3, s32[1,8]{1,0:T(1,128)S(1)} %copy-done.4, s32[1,8]{1,0:T(1,128)S(1)} %copy-done.5, f32[64,128]{1,0:T(8,128)S(1)} %shard_map.73._.refs_5_.refs_2_), custom_call_target="tpu_custom_call" | custom-call | tf_op jit(solution)/shard_map/pallas_call | solution.py:92
  8.2 0.0 collective-permute-done.refs_1_
  8.2 0.8 %collective-permute-done.3.refs_3_ = bf16[64,1024]{1,0:T(8,128)(2,1)S(1)} collective-permute-done((bf16[64,1024]{1,0:T(8,128)(2,1)S(1)}, bf16[64,1024]{1,0:T(8,128)(2,1)S(1)}, u32[]{:S(2)}, u32[]{:S(2)}) %collective-permute-start.3) | collective-permute-done | bytes 131104 | tf_op jit(solution)/shard_map/ppermute | solution.py:28
  9.0 0.0 copy-done.6
  9.0 0.0 copy-done.7
  9.0 0.5 %shard_map.75 = bf16[64,128]{1,0:T(8,128)(2,1)S(1)} custom-call(bf16[64,1024]{1,0:T(8,128)(2,1)S(1)} %bitcast.7, bf16[64,1024]{1,0:T(8,128)(2,1)S(1)} %collective-permute-done.refs_1_, bf16[64,1024]{1,0:T(8,128)(2,1)S(1)} %collective-permute-done.1.refs_2_, bf16[64,1024]{1,0:T(8,128)(2,1)S(1)} %collective-permute-done.3.refs_3_, ...), custom_call_target="tpu_custom_call" | custom-call | flops 1500000000 | bytes 1000000 | tf_op jit(solution)/shard_map/pallas_call | solution.py:92
  9.5 2.1 %collective-permute-start.4 = (bf16[64,128]{1,0:T(8,128)(2,1)S(1)}, bf16[64,128]{1,0:T(8,128)(2,1)S(1)}, u32[]{:S(2)}, u32[]{:S(2)}) collective-permute-start(bf16[64,128]{1,0:T(8,128)(2,1)S(1)} %shard_map.75), channel_id=1, source_target_pairs={{0,8},{4,12},{8,0},{12,4},{16,24},{20,28},{24,16},{28,20},{1,9},{5... | collective-permute-start | bytes 49160 | tf_op jit(solution)/shard_map/ppermute | solution.py:28
  11.6 2.6 %collective-permute-start.5 = (bf16[64,128]{1,0:T(8,128)(2,1)S(1)}, bf16[64,128]{1,0:T(8,128)(2,1)S(1)}, u32[]{:S(2)}, u32[]{:S(2)}) collective-permute-start(bf16[64,128]{1,0:T(8,128)(2,1)S(1)} %shard_map.75), channel_id=1, source_target_pairs={{0,16},{4,20},{8,24},{12,28},{16,0},{20,4},{24,8},{28,12},{1,17},{... | collective-permute-start | bytes 49160 | tf_op jit(solution)/shard_map/ppermute | solution.py:28
  14.2 0.0 collective-permute-start.6
  14.2 0.0 collective-permute-done.4
  14.2 2.0 %collective-permute-done.5 = bf16[64,128]{1,0:T(8,128)(2,1)S(1)} collective-permute-done((bf16[64,128]{1,0:T(8,128)(2,1)S(1)}, bf16[64,128]{1,0:T(8,128)(2,1)S(1)}, u32[]{:S(2)}, u32[]{:S(2)}) %collective-permute-start.5) | collective-permute-done | bytes 16416 | tf_op jit(solution)/shard_map/ppermute | solution.py:28
  16.2 3.5 %collective-permute-done.6 = bf16[64,128]{1,0:T(8,128)(2,1)S(1)} collective-permute-done((bf16[64,128]{1,0:T(8,128)(2,1)S(1)}, bf16[64,128]{1,0:T(8,128)(2,1)S(1)}, u32[]{:S(2)}, u32[]{:S(2)}) %collective-permute-start.6) | collective-permute-done | bytes 16416 | tf_op jit(solution)/shard_map/ppermute | solution.py:28
  19.7 0.0 collective-permute-done.11.refs_0_
  19.7 0.1 collective-permute-start.12
  19.8 0.0 copy-done.1
  19.8 0.4 %shard_map.76.refs_2_ = f32[64,128]{1,0:T(8,128)S(1)} custom-call(bf16[64,3584]{1,0:T(8,128)(2,1)S(1)} %collective-permute-done.11.refs_0_, bf16[128,14336]{1,0:T(8,128)(2,1)S(1)} %copy-done.1, f32[64,128]{1,0:T(8,128)S(1)} %shard_map.73._.refs_5_.refs_2_), custom_call_target="tpu_custom_call" | custom-call | tf_op jit(solution)/shard_map/pallas_call | solution.py:92
  20.3 1.6 %collective-permute-start.7 = (bf16[256,128]{1,0:T(8,128)(2,1)S(1)}, bf16[256,128]{1,0:T(8,128)(2,1)S(1)}, u32[]{:S(2)}, u32[]{:S(2)}) collective-permute-start(bf16[256,128]{1,0:T(8,128)(2,1)S(1)} %pad_maximum_fusion), channel_id=1, source_target_pairs={{0,4},{4,0},{8,12},{12,8},{16,20},{20,16},{24,28},{28,24},{1,5},{5... | collective-permute-start | bytes 196616 | tf_op jit(solution)/shard_map/ppermute | solution.py:28
  21.9 0.0 collective-permute-done.12.refs_0_
  21.9 1.1 %shard_map.77 = bf16[32,24,128]{2,1,0:T(8,128)(2,1)} custom-call(bf16[64,3584]{1,0:T(8,128)(2,1)S(1)} %collective-permute-done.12.refs_0_, bf16[128,14336]{1,0:T(8,128)(2,1)S(1)} %copy-done.1, f32[64,128]{1,0:T(8,128)S(1)} %shard_map.76.refs_2_, bf16[16,128]{1,0:T(8,128)(2,1)S(1)} %shard_map.74.refs_6_.refs_3_), custom_call_target="tpu_custom_call" | custom-call | tf_op jit(solution)/shard_map/pallas_call | solution.py:92
  23.0 3.3 %all-to-all-start = ((bf16[32,24,128]{2,1,0:T(8,128)(2,1)}), bf16[32,24,128]{2,1,0:T(8,128)(2,1)S(1)}, u32[]{:S(2)}, u32[]{:S(2)}) async-start(bf16[32,24,128]{2,1,0:T(8,128)(2,1)} %shard_map.77), calls=%async_computation | async-start | bytes 393216 | tf_op jit(solution)/shard_map/all_to_all | solution.py:201
  26.3 0.0 collective-permute-done.7
  26.3 1.8 %collective-permute-start.9 = (bf16[512,128]{1,0:T(8,128)(2,1)S(1)}, bf16[512,128]{1,0:T(8,128)(2,1)S(1)}, u32[]{:S(2)}, u32[]{:S(2)}) collective-permute-start(bf16[512,128]{1,0:T(8,128)(2,1)S(1)} %constant_dynamic-update-slice_fusion.refs_0_), channel_id=1, source_target_pairs={{0,2},{1,3},{2,0},{3,1},{4,6},{5,7},{6,4},{7,5},{8,10},{9,11},{10,... | collective-permute-start | bytes 393224 | tf_op jit(solution)/shard_map/ppermute | solution.py:28
  28.2 0.0 collective-permute-start.8
  28.2 5.6 %collective-permute-done.9.refs_2_ = bf16[512,128]{1,0:T(8,128)(2,1)S(1)} collective-permute-done((bf16[512,128]{1,0:T(8,128)(2,1)S(1)}, bf16[512,128]{1,0:T(8,128)(2,1)S(1)}, u32[]{:S(2)}, u32[]{:S(2)}) %collective-permute-start.9) | collective-permute-done | bytes 131104 | tf_op jit(solution)/shard_map/ppermute | solution.py:28
  33.8 0.0 collective-permute-start.10
  33.8 0.0 collective-permute-done.8.refs_1_
  33.8 1.3 %collective-permute-done.10.refs_3_ = bf16[512,128]{1,0:T(8,128)(2,1)S(1)} collective-permute-done((bf16[512,128]{1,0:T(8,128)(2,1)S(1)}, bf16[512,128]{1,0:T(8,128)(2,1)S(1)}, u32[]{:S(2)}, u32[]{:S(2)}) %collective-permute-start.10) | collective-permute-done | bytes 131104 | tf_op jit(solution)/shard_map/ppermute | solution.py:28
  35.1 0.0 all-to-all-done.refs_4_
  35.2 2.5 %shard_map.78 = f32[24,1024]{1,0:T(8,128)} custom-call(bf16[512,128]{1,0:T(8,128)(2,1)S(1)} %constant_dynamic-update-slice_fusion.refs_0_, bf16[512,128]{1,0:T(8,128)(2,1)S(1)} %collective-permute-done.8.refs_1_, bf16[512,128]{1,0:T(8,128)(2,1)S(1)} %collective-permute-done.9.refs_2_, bf16[512,128]{1,0:T(8,128)(2,1)S(1)} %collective-permute-done.10.refs_3_, ...), custom_call_target="tpu_custom_call" | custom-call | tf_op jit(solution)/shard_map/pallas_call | solution.py:92
  (6 shorter events, 0.0 us)
Async XLA Ops:
  0.0 7.7 %copy-start.4 = (s32[1,8]{1,0:T(1,128)S(1)}, s32[1,8]{1,0:T(1,128)}, u32[]{:S(2)}) copy-start(s32[1,8]{1,0:T(1,128)} %owner_dp.1) | copy-start | bytes 100
  0.0 7.7 %copy-start.5 = (s32[1,8]{1,0:T(1,128)S(1)}, s32[1,8]{1,0:T(1,128)}, u32[]{:S(2)}) copy-start(s32[1,8]{1,0:T(1,128)} %owner_slot.1) | copy-start | bytes 100
  0.0 7.7 %copy-start.3 = (s32[1,128]{1,0:T(1,128)S(1)}, s32[1,128]{1,0:T(1,128)}, u32[]{:S(2)}) copy-start(s32[1,128]{1,0:T(1,128)} %piece_of.1) | copy-start | bytes 1540
  0.0 3.3 %collective-permute-start.2 = (bf16[64,3584]{1,0:T(8,128)(2,1)}, bf16[64,3584]{1,0:T(8,128)(2,1)S(1)}, u32[]{:S(2)}, u32[]{:S(2)}) collective-permute-start(bf16[64,3584]{1,0:T(8,128)(2,1)} %bitcast.2), channel_id=1, source_target_pairs={{0,1},{1,0},{2,3},{3,2},{4,5},{5,4},{6,7},{7,6},{8,9},{9,8},{10,11... | collective-permute-start | bytes 1376264 | tf_op jit(solution)/shard_map/ppermute | solution.py:28
  0.5 7.1 %collective-permute-start.1 = (bf16[64,1024]{1,0:T(8,128)(2,1)}, bf16[64,1024]{1,0:T(8,128)(2,1)S(1)}, u32[]{:S(2)}, u32[]{:S(2)}) collective-permute-start(bf16[64,1024]{1,0:T(8,128)(2,1)} %bitcast.5), channel_id=1, source_target_pairs={{0,2},{1,3},{2,0},{3,1},{4,6},{5,7},{6,4},{7,5},{8,10},{9,11},{10,... | collective-permute-start | bytes 393224 | tf_op jit(solution)/shard_map/ppermute | solution.py:28
  3.1 16.6 %collective-permute-start.11 = (bf16[64,3584]{1,0:T(8,128)(2,1)}, bf16[64,3584]{1,0:T(8,128)(2,1)S(1)}, u32[]{:S(2)}, u32[]{:S(2)}) collective-permute-start(bf16[64,3584]{1,0:T(8,128)(2,1)} %bitcast.3), channel_id=1, source_target_pairs={{0,2},{1,3},{2,0},{3,1},{4,6},{5,7},{6,4},{7,5},{8,10},{9,11},{10,... | collective-permute-start | bytes 1376264 | tf_op jit(solution)/shard_map/ppermute | solution.py:28
  3.2 5.1 %collective-permute-start = (bf16[64,1024]{1,0:T(8,128)(2,1)}, bf16[64,1024]{1,0:T(8,128)(2,1)S(1)}, u32[]{:S(2)}, u32[]{:S(2)}) collective-permute-start(bf16[64,1024]{1,0:T(8,128)(2,1)} %bitcast.6), channel_id=1, source_target_pairs={{0,1},{1,0},{2,3},{3,2},{4,5},{5,4},{6,7},{7,6},{8,9},{9,8},{10,11... | collective-permute-start | bytes 393224 | tf_op jit(solution)/shard_map/ppermute | solution.py:28
  3.3 2.0 %copy-start = (bf16[128,14336]{1,0:T(8,128)(2,1)S(1)}, bf16[128,14336]{1,0:T(8,128)(2,1)}, u32[]{:S(2)}) copy-start(bf16[128,14336]{1,0:T(8,128)(2,1)} %refs_1_.3) | copy-start | bytes 11010052
  5.3 1.0 %copy-start.2 = (bf16[3584,64]{0,1:T(8,128)(2,1)S(1)}, bf16[3584,64]{0,1:T(8,128)(2,1)}, u32[]{:S(2)}) copy-start(bf16[3584,64]{0,1:T(8,128)(2,1)} %param.12) | copy-start | bytes 1376260
  6.3 2.7 %copy-start.6 = (bf16[128,4096]{1,0:T(8,128)(2,1)S(1)}, bf16[128,4096]{1,0:T(8,128)(2,1)}, u32[]{:S(2)}) copy-start(bf16[128,4096]{1,0:T(8,128)(2,1)} %refs_4_.1) | copy-start | bytes 3145732
  6.3 2.7 %copy-start.7 = (bf16[1024,64]{0,1:T(8,128)(2,1)S(1)}, bf16[1024,64]{0,1:T(8,128)(2,1)}, u32[]{:S(2)}) copy-start(bf16[1024,64]{0,1:T(8,128)(2,1)} %param.13) | copy-start | bytes 393220
  7.1 12.7 %copy-start.1 = (bf16[128,14336]{1,0:T(8,128)(2,1)S(1)}, bf16[128,14336]{1,0:T(8,128)(2,1)}, u32[]{:S(2)}) copy-start(bf16[128,14336]{1,0:T(8,128)(2,1)} %refs_1_.3) | copy-start | bytes 11010052
  7.7 1.3 %collective-permute-start.3 = (bf16[64,1024]{1,0:T(8,128)(2,1)S(1)}, bf16[64,1024]{1,0:T(8,128)(2,1)S(1)}, u32[]{:S(2)}, u32[]{:S(2)}) collective-permute-start(bf16[64,1024]{1,0:T(8,128)(2,1)S(1)} %collective-permute-done.1.refs_2_), channel_id=1, source_target_pairs={{0,1},{1,0},{2,3},{3,2},{4,5},{5,4},{6,7},{7,6},{8,9},{9,8},{10,11... | collective-permute-start | bytes 393224 | tf_op jit(solution)/shard_map/ppermute | solution.py:28
  9.5 4.7 %collective-permute-start.4 = (bf16[64,128]{1,0:T(8,128)(2,1)S(1)}, bf16[64,128]{1,0:T(8,128)(2,1)S(1)}, u32[]{:S(2)}, u32[]{:S(2)}) collective-permute-start(bf16[64,128]{1,0:T(8,128)(2,1)S(1)} %shard_map.75), channel_id=1, source_target_pairs={{0,8},{4,12},{8,0},{12,4},{16,24},{20,28},{24,16},{28,20},{1,9},{5... | collective-permute-start | bytes 49160 | tf_op jit(solution)/shard_map/ppermute | solution.py:28
  11.6 4.6 %collective-permute-start.5 = (bf16[64,128]{1,0:T(8,128)(2,1)S(1)}, bf16[64,128]{1,0:T(8,128)(2,1)S(1)}, u32[]{:S(2)}, u32[]{:S(2)}) collective-permute-start(bf16[64,128]{1,0:T(8,128)(2,1)S(1)} %shard_map.75), channel_id=1, source_target_pairs={{0,16},{4,20},{8,24},{12,28},{16,0},{20,4},{24,8},{28,12},{1,17},{... | collective-permute-start | bytes 49160 | tf_op jit(solution)/shard_map/ppermute | solution.py:28
  14.2 5.5 %collective-permute-start.6 = (bf16[64,128]{1,0:T(8,128)(2,1)S(1)}, bf16[64,128]{1,0:T(8,128)(2,1)S(1)}, u32[]{:S(2)}, u32[]{:S(2)}) collective-permute-start(bf16[64,128]{1,0:T(8,128)(2,1)S(1)} %shard_map.75), channel_id=1, source_target_pairs={{0,24},{4,28},{8,16},{12,20},{16,8},{20,12},{24,0},{28,4},{1,25},{... | collective-permute-start | bytes 49160 | tf_op jit(solution)/shard_map/ppermute | solution.py:28
  19.7 2.1 %collective-permute-start.12 = (bf16[64,3584]{1,0:T(8,128)(2,1)S(1)}, bf16[64,3584]{1,0:T(8,128)(2,1)S(1)}, u32[]{:S(2)}, u32[]{:S(2)}) collective-permute-start(bf16[64,3584]{1,0:T(8,128)(2,1)S(1)} %collective-permute-done.11.refs_0_), channel_id=1, source_target_pairs={{0,1},{1,0},{2,3},{3,2},{4,5},{5,4},{6,7},{7,6},{8,9},{9,8},{10,11... | collective-permute-start | bytes 1376264 | tf_op jit(solution)/shard_map/ppermute | solution.py:28
  20.3 6.0 %collective-permute-start.7 = (bf16[256,128]{1,0:T(8,128)(2,1)S(1)}, bf16[256,128]{1,0:T(8,128)(2,1)S(1)}, u32[]{:S(2)}, u32[]{:S(2)}) collective-permute-start(bf16[256,128]{1,0:T(8,128)(2,1)S(1)} %pad_maximum_fusion), channel_id=1, source_target_pairs={{0,4},{4,0},{8,12},{12,8},{16,20},{20,16},{24,28},{28,24},{1,5},{5... | collective-permute-start | bytes 196616 | tf_op jit(solution)/shard_map/ppermute | solution.py:28
  23.0 12.2 %all-to-all-start = ((bf16[32,24,128]{2,1,0:T(8,128)(2,1)}), bf16[32,24,128]{2,1,0:T(8,128)(2,1)S(1)}, u32[]{:S(2)}, u32[]{:S(2)}) async-start(bf16[32,24,128]{2,1,0:T(8,128)(2,1)} %shard_map.77), calls=%async_computation | async-start | bytes 393216 | tf_op jit(solution)/shard_map/all_to_all | solution.py:201
  26.3 7.4 %collective-permute-start.9 = (bf16[512,128]{1,0:T(8,128)(2,1)S(1)}, bf16[512,128]{1,0:T(8,128)(2,1)S(1)}, u32[]{:S(2)}, u32[]{:S(2)}) collective-permute-start(bf16[512,128]{1,0:T(8,128)(2,1)S(1)} %constant_dynamic-update-slice_fusion.refs_0_), channel_id=1, source_target_pairs={{0,2},{1,3},{2,0},{3,1},{4,6},{5,7},{6,4},{7,5},{8,10},{9,11},{10,... | collective-permute-start | bytes 393224 | tf_op jit(solution)/shard_map/ppermute | solution.py:28
  28.2 5.6 %collective-permute-start.8 = (bf16[512,128]{1,0:T(8,128)(2,1)S(1)}, bf16[512,128]{1,0:T(8,128)(2,1)S(1)}, u32[]{:S(2)}, u32[]{:S(2)}) collective-permute-start(bf16[512,128]{1,0:T(8,128)(2,1)S(1)} %constant_dynamic-update-slice_fusion.refs_0_), channel_id=1, source_target_pairs={{0,1},{1,0},{2,3},{3,2},{4,5},{5,4},{6,7},{7,6},{8,9},{9,8},{10,11... | collective-permute-start | bytes 393224 | tf_op jit(solution)/shard_map/ppermute | solution.py:28
  33.8 1.3 %collective-permute-start.10 = (bf16[512,128]{1,0:T(8,128)(2,1)S(1)}, bf16[512,128]{1,0:T(8,128)(2,1)S(1)}, u32[]{:S(2)}, u32[]{:S(2)}) collective-permute-start(bf16[512,128]{1,0:T(8,128)(2,1)S(1)} %collective-permute-done.9.refs_2_), channel_id=1, source_target_pairs={{0,1},{1,0},{2,3},{3,2},{4,5},{5,4},{6,7},{7,6},{8,9},{9,8},{10,11... | collective-permute-start | bytes 393224 | tf_op jit(solution)/shard_map/ppermute | solution.py:28

commit v7 on v6

--- a/solution.py
+++ b/solution.py
@@ -12,7 +12,6 @@
 GR = 192
 BF16 = jnp.bfloat16
 F32 = jnp.float32
-BOTH = ("dp", "fsdp")
 CONTRACT_LAST = (((1,), (1,)), ((), ()))
 VMEM = pl.BlockSpec(memory_space=pltpu.VMEM)
 SMEM = pl.BlockSpec(memory_space=pltpu.SMEM)
@@ -82,9 +81,9 @@
     tokens, total, keys, out = refs[count:]
     rows = (low_rank(refs[:count], which, tokens) + total[...]).astype(BF16)
     shared = jnp.concatenate([rows[:lead, :], keys[: out.shape[1] - mine - lead, :]], axis=0)
-    parts = rows.shape[0] // mine
+    each = out.shape[0] * mine // rows.shape[0]
     for k in range(out.shape[0]):
-        f = k % parts
+        f = k // each
         out[k] = jnp.concatenate([rows[f * mine : (f + 1) * mine, :], shared], axis=0)
 
 
@@ -113,7 +112,7 @@
     d, f = lax.axis_index("dp"), lax.axis_index("fsdp")
     wide = []
     for g, e_ref in enumerate(errors):
-        places = [(d ^ k) * count_fsdp + (f ^ g) for k in order]
+        places = [(f ^ g) * count_dp + (d ^ k) for k in order]
         err = jnp.concatenate([e_ref[k * width : (k + 1) * width, :] for k in range(count_dp)], axis=1)
         low = jnp.concatenate([messages[k] for k in places], axis=1)
         key = low.astype(F32)[mine + lead : mine + lead + 1, :]
@@ -198,7 +197,7 @@
         [far_in[-1], hidden_in, inputs, keys],
         jax.ShapeDtypeStruct((count_dp * count_fsdp, mine + tile, token_rows), BF16),
     )
-    messages = lax.all_to_all(messages, BOTH, split_axis=0, concat_axis=0, tiled=True)
+    messages = lax.all_to_all(messages, ("fsdp", "dp"), split_axis=0, concat_axis=0, tiled=True)
     all_errors = spread(widen(errors, "dp", first), bits)
     scale = 1.0 / math.sqrt(owned * count_dp * count_fsdp)
     return call(

time: 38.1 us -> 37.8 us (level)
  no operation moved by 1% of the time
where the time goes in v7:
time: 37.8 us; the launch traced here: 37.6 us
  starting transfers between devices  14.7 us (39%)
  waiting for transfers between devices  13.8 us (37%)
  Pallas kernels  5.83 us (15%)
  local copies, waits for them, and re-layouts  3.12 us (8%)
    ppermute x13, waiting for transfers between devices, swap(): return lax.ppermute(value, axis, [(i, i ^ bit) for i in range(count)])  13.8 us
    ppermute x13, starting transfers between devices, swap(): return lax.ppermute(value, axis, [(i, i ^ bit) for i in range(count)])  11.5 us
    pallas_call x6, Pallas kernels, call(): pl.pallas_call(kernel, out_shape=outputs, in_specs=specs or [VMEM] * len(...  5.83 us
    all_to_all x1, starting transfers between devices, by_tokens(): lax.all_to_all(messages, ('fsdp', 'dp'), split_axis=0, concat_axis=0, til...  3.27 us
    unnamed x20, local copies, waits for them, and re-layouts  3.11 us
  transfers between devices with their start and end apart: 14, of which 6 were waited for; matrix products, arithmetic and copies ran while one was open for 0% of the time, Pallas kernels for 9%

profile of v7, /device:TPU:0, one launch (start us, length us, event | category | flops | bytes accessed | tf_op | source)
XLA Modules:
  0.0 37.6 jit_solution(10847944371095805005)
XLA Ops:
  0.0 0.0 copy-start.4
  0.0 0.0 copy-start.5
  0.0 0.0 copy-start.3
  0.0 0.5 %collective-permute-start.2 = (bf16[64,3584]{1,0:T(8,128)(2,1)}, bf16[64,3584]{1,0:T(8,128)(2,1)S(1)}, u32[]{:S(2)}, u32[]{:S(2)}) collective-permute-start(bf16[64,3584]{1,0:T(8,128)(2,1)} %bitcast.2), channel_id=1, source_target_pairs={{0,1},{1,0},{2,3},{3,2},{4,5},{5,4},{6,7},{7,6},{8,9},{9,8},{10,11... | collective-permute-start | bytes 1376264 | tf_op jit(solution)/shard_map/ppermute | solution.py:27
  0.5 2.6 %collective-permute-start.1 = (bf16[64,1024]{1,0:T(8,128)(2,1)}, bf16[64,1024]{1,0:T(8,128)(2,1)S(1)}, u32[]{:S(2)}, u32[]{:S(2)}) collective-permute-start(bf16[64,1024]{1,0:T(8,128)(2,1)} %bitcast.5), channel_id=1, source_target_pairs={{0,2},{1,3},{2,0},{3,1},{4,6},{5,7},{6,4},{7,5},{8,10},{9,11},{10,... | collective-permute-start | bytes 393224 | tf_op jit(solution)/shard_map/ppermute | solution.py:27
  3.1 0.1 collective-permute-start.11
  3.2 0.1 collective-permute-start
  3.3 0.0 collective-permute-done.2.refs_1_
  3.3 0.0 copy-start
  3.3 2.0 %copy-done = bf16[128,14336]{1,0:T(8,128)(2,1)S(1)} copy-done((bf16[128,14336]{1,0:T(8,128)(2,1)S(1)}, bf16[128,14336]{1,0:T(8,128)(2,1)}, u32[]{:S(2)}) %copy-start) | copy-done | bytes 3670040
  5.3 0.0 copy-start.2
  5.3 1.0 %copy-done.2 = bf16[3584,64]{0,1:T(8,128)(2,1)S(1)} copy-done((bf16[3584,64]{0,1:T(8,128)(2,1)S(1)}, bf16[3584,64]{0,1:T(8,128)(2,1)}, u32[]{:S(2)}) %copy-start.2) | copy-done | bytes 458776
  6.3 0.0 copy-start.6
  6.3 0.0 copy-start.7
  6.3 0.7 %shard_map.73._.refs_5_.refs_2_ = f32[64,128]{1,0:T(8,128)S(1)} custom-call(bf16[64,3584]{1,0:T(8,128)(2,1)S(1)} %bitcast.4, bf16[64,3584]{1,0:T(8,128)(2,1)S(1)} %collective-permute-done.2.refs_1_, bf16[128,14336]{1,0:T(8,128)(2,1)S(1)} %copy-done), custom_call_target="tpu_custom_call" | custom-call | tf_op jit(solution)/shard_map/pallas_call | solution.py:91
  7.1 0.0 copy-start.1
  7.1 0.5 %collective-permute-done.1.refs_2_ = bf16[64,1024]{1,0:T(8,128)(2,1)S(1)} collective-permute-done((bf16[64,1024]{1,0:T(8,128)(2,1)}, bf16[64,1024]{1,0:T(8,128)(2,1)S(1)}, u32[]{:S(2)}, u32[]{:S(2)}) %collective-permute-start.1) | collective-permute-done | bytes 131104 | tf_op jit(solution)/shard_map/ppermute | solution.py:27
  7.7 0.0 collective-permute-start.3
  7.7 0.0 copy-done.4
  7.7 0.0 copy-done.5
  7.7 0.0 copy-done.3
  7.7 0.6 %shard_map.74.refs_6_.refs_3_ = bf16[16,128]{1,0:T(8,128)(2,1)S(1)} custom-call(s32[1,128]{1,0:T(1,128)S(1)} %copy-done.3, s32[1,8]{1,0:T(1,128)S(1)} %copy-done.4, s32[1,8]{1,0:T(1,128)S(1)} %copy-done.5, f32[64,128]{1,0:T(8,128)S(1)} %shard_map.73._.refs_5_.refs_2_), custom_call_target="tpu_custom_call" | custom-call | tf_op jit(solution)/shard_map/pallas_call | solution.py:91
  8.2 0.0 collective-permute-done.refs_1_
  8.2 0.8 %collective-permute-done.3.refs_3_ = bf16[64,1024]{1,0:T(8,128)(2,1)S(1)} collective-permute-done((bf16[64,1024]{1,0:T(8,128)(2,1)S(1)}, bf16[64,1024]{1,0:T(8,128)(2,1)S(1)}, u32[]{:S(2)}, u32[]{:S(2)}) %collective-permute-start.3) | collective-permute-done | bytes 131104 | tf_op jit(solution)/shard_map/ppermute | solution.py:27
  9.0 0.0 copy-done.6
  9.0 0.0 copy-done.7
  9.0 0.5 %shard_map.75 = bf16[64,128]{1,0:T(8,128)(2,1)S(1)} custom-call(bf16[64,1024]{1,0:T(8,128)(2,1)S(1)} %bitcast.7, bf16[64,1024]{1,0:T(8,128)(2,1)S(1)} %collective-permute-done.refs_1_, bf16[64,1024]{1,0:T(8,128)(2,1)S(1)} %collective-permute-done.1.refs_2_, bf16[64,1024]{1,0:T(8,128)(2,1)S(1)} %collective-permute-done.3.refs_3_, ...), custom_call_target="tpu_custom_call" | custom-call | flops 1500000000 | bytes 1000000 | tf_op jit(solution)/shard_map/pallas_call | solution.py:91
  9.5 2.1 %collective-permute-start.4 = (bf16[64,128]{1,0:T(8,128)(2,1)S(1)}, bf16[64,128]{1,0:T(8,128)(2,1)S(1)}, u32[]{:S(2)}, u32[]{:S(2)}) collective-permute-start(bf16[64,128]{1,0:T(8,128)(2,1)S(1)} %shard_map.75), channel_id=1, source_target_pairs={{0,8},{4,12},{8,0},{12,4},{16,24},{20,28},{24,16},{28,20},{1,9},{5... | collective-permute-start | bytes 49160 | tf_op jit(solution)/shard_map/ppermute | solution.py:27
  11.6 2.6 %collective-permute-start.5 = (bf16[64,128]{1,0:T(8,128)(2,1)S(1)}, bf16[64,128]{1,0:T(8,128)(2,1)S(1)}, u32[]{:S(2)}, u32[]{:S(2)}) collective-permute-start(bf16[64,128]{1,0:T(8,128)(2,1)S(1)} %shard_map.75), channel_id=1, source_target_pairs={{0,16},{4,20},{8,24},{12,28},{16,0},{20,4},{24,8},{28,12},{1,17},{... | collective-permute-start | bytes 49160 | tf_op jit(solution)/shard_map/ppermute | solution.py:27
  14.2 0.0 collective-permute-start.6
  14.2 0.0 collective-permute-done.4
  14.2 2.0 %collective-permute-done.5 = bf16[64,128]{1,0:T(8,128)(2,1)S(1)} collective-permute-done((bf16[64,128]{1,0:T(8,128)(2,1)S(1)}, bf16[64,128]{1,0:T(8,128)(2,1)S(1)}, u32[]{:S(2)}, u32[]{:S(2)}) %collective-permute-start.5) | collective-permute-done | bytes 16416 | tf_op jit(solution)/shard_map/ppermute | solution.py:27
  16.2 3.5 %collective-permute-done.6 = bf16[64,128]{1,0:T(8,128)(2,1)S(1)} collective-permute-done((bf16[64,128]{1,0:T(8,128)(2,1)S(1)}, bf16[64,128]{1,0:T(8,128)(2,1)S(1)}, u32[]{:S(2)}, u32[]{:S(2)}) %collective-permute-start.6) | collective-permute-done | bytes 16416 | tf_op jit(solution)/shard_map/ppermute | solution.py:27
  19.7 0.0 collective-permute-done.11.refs_0_
  19.7 0.1 collective-permute-start.12
  19.8 0.0 copy-done.1
  19.8 0.4 %shard_map.76.refs_2_ = f32[64,128]{1,0:T(8,128)S(1)} custom-call(bf16[64,3584]{1,0:T(8,128)(2,1)S(1)} %collective-permute-done.11.refs_0_, bf16[128,14336]{1,0:T(8,128)(2,1)S(1)} %copy-done.1, f32[64,128]{1,0:T(8,128)S(1)} %shard_map.73._.refs_5_.refs_2_), custom_call_target="tpu_custom_call" | custom-call | tf_op jit(solution)/shard_map/pallas_call | solution.py:91
  20.3 1.6 %collective-permute-start.7 = (bf16[256,128]{1,0:T(8,128)(2,1)S(1)}, bf16[256,128]{1,0:T(8,128)(2,1)S(1)}, u32[]{:S(2)}, u32[]{:S(2)}) collective-permute-start(bf16[256,128]{1,0:T(8,128)(2,1)S(1)} %pad_maximum_fusion), channel_id=1, source_target_pairs={{0,4},{4,0},{8,12},{12,8},{16,20},{20,16},{24,28},{28,24},{1,5},{5... | collective-permute-start | bytes 196616 | tf_op jit(solution)/shard_map/ppermute | solution.py:27
  21.9 0.0 collective-permute-done.12.refs_0_
  21.9 1.1 %shard_map.77 = bf16[32,24,128]{2,1,0:T(8,128)(2,1)} custom-call(bf16[64,3584]{1,0:T(8,128)(2,1)S(1)} %collective-permute-done.12.refs_0_, bf16[128,14336]{1,0:T(8,128)(2,1)S(1)} %copy-done.1, f32[64,128]{1,0:T(8,128)S(1)} %shard_map.76.refs_2_, bf16[16,128]{1,0:T(8,128)(2,1)S(1)} %shard_map.74.refs_6_.refs_3_), custom_call_target="tpu_custom_call" | custom-call | tf_op jit(solution)/shard_map/pallas_call | solution.py:91
  23.0 3.3 %all-to-all-start = ((bf16[32,24,128]{2,1,0:T(8,128)(2,1)}), bf16[32,24,128]{2,1,0:T(8,128)(2,1)S(1)}, u32[]{:S(2)}, u32[]{:S(2)}) async-start(bf16[32,24,128]{2,1,0:T(8,128)(2,1)} %shard_map.77), calls=%async_computation | async-start | bytes 393216 | tf_op jit(solution)/shard_map/all_to_all | solution.py:200
  26.3 0.0 collective-permute-done.7
  26.3 1.8 %collective-permute-start.9 = (bf16[512,128]{1,0:T(8,128)(2,1)S(1)}, bf16[512,128]{1,0:T(8,128)(2,1)S(1)}, u32[]{:S(2)}, u32[]{:S(2)}) collective-permute-start(bf16[512,128]{1,0:T(8,128)(2,1)S(1)} %constant_dynamic-update-slice_fusion.refs_0_), channel_id=1, source_target_pairs={{0,2},{1,3},{2,0},{3,1},{4,6},{5,7},{6,4},{7,5},{8,10},{9,11},{10,... | collective-permute-start | bytes 393224 | tf_op jit(solution)/shard_map/ppermute | solution.py:27
  28.2 0.0 collective-permute-start.8
  28.2 5.6 %collective-permute-done.9.refs_2_ = bf16[512,128]{1,0:T(8,128)(2,1)S(1)} collective-permute-done((bf16[512,128]{1,0:T(8,128)(2,1)S(1)}, bf16[512,128]{1,0:T(8,128)(2,1)S(1)}, u32[]{:S(2)}, u32[]{:S(2)}) %collective-permute-start.9) | collective-permute-done | bytes 131104 | tf_op jit(solution)/shard_map/ppermute | solution.py:27
  33.7 0.0 collective-permute-start.10
  33.7 0.0 collective-permute-done.8.refs_1_
  33.8 1.3 %collective-permute-done.10.refs_3_ = bf16[512,128]{1,0:T(8,128)(2,1)S(1)} collective-permute-done((bf16[512,128]{1,0:T(8,128)(2,1)S(1)}, bf16[512,128]{1,0:T(8,128)(2,1)S(1)}, u32[]{:S(2)}, u32[]{:S(2)}) %collective-permute-start.10) | collective-permute-done | bytes 131104 | tf_op jit(solution)/shard_map/ppermute | solution.py:27
  35.1 0.0 all-to-all-done.refs_4_
  35.1 2.5 %shard_map.78 = f32[24,1024]{1,0:T(8,128)} custom-call(bf16[512,128]{1,0:T(8,128)(2,1)S(1)} %constant_dynamic-update-slice_fusion.refs_0_, bf16[512,128]{1,0:T(8,128)(2,1)S(1)} %collective-permute-done.8.refs_1_, bf16[512,128]{1,0:T(8,128)(2,1)S(1)} %collective-permute-done.9.refs_2_, bf16[512,128]{1,0:T(8,128)(2,1)S(1)} %collective-permute-done.10.refs_3_, ...), custom_call_target="tpu_custom_call" | custom-call | tf_op jit(solution)/shard_map/pallas_call | solution.py:91
  (6 shorter events, 0.0 us)
Async XLA Ops:
  0.0 7.7 %copy-start.4 = (s32[1,8]{1,0:T(1,128)S(1)}, s32[1,8]{1,0:T(1,128)}, u32[]{:S(2)}) copy-start(s32[1,8]{1,0:T(1,128)} %owner_dp.1) | copy-start | bytes 100
  0.0 7.7 %copy-start.5 = (s32[1,8]{1,0:T(1,128)S(1)}, s32[1,8]{1,0:T(1,128)}, u32[]{:S(2)}) copy-start(s32[1,8]{1,0:T(1,128)} %owner_slot.1) | copy-start | bytes 100
  0.0 7.7 %copy-start.3 = (s32[1,128]{1,0:T(1,128)S(1)}, s32[1,128]{1,0:T(1,128)}, u32[]{:S(2)}) copy-start(s32[1,128]{1,0:T(1,128)} %piece_of.1) | copy-start | bytes 1540
  0.0 3.3 %collective-permute-start.2 = (bf16[64,3584]{1,0:T(8,128)(2,1)}, bf16[64,3584]{1,0:T(8,128)(2,1)S(1)}, u32[]{:S(2)}, u32[]{:S(2)}) collective-permute-start(bf16[64,3584]{1,0:T(8,128)(2,1)} %bitcast.2), channel_id=1, source_target_pairs={{0,1},{1,0},{2,3},{3,2},{4,5},{5,4},{6,7},{7,6},{8,9},{9,8},{10,11... | collective-permute-start | bytes 1376264 | tf_op jit(solution)/shard_map/ppermute | solution.py:27
  0.5 7.1 %collective-permute-start.1 = (bf16[64,1024]{1,0:T(8,128)(2,1)}, bf16[64,1024]{1,0:T(8,128)(2,1)S(1)}, u32[]{:S(2)}, u32[]{:S(2)}) collective-permute-start(bf16[64,1024]{1,0:T(8,128)(2,1)} %bitcast.5), channel_id=1, source_target_pairs={{0,2},{1,3},{2,0},{3,1},{4,6},{5,7},{6,4},{7,5},{8,10},{9,11},{10,... | collective-permute-start | bytes 393224 | tf_op jit(solution)/shard_map/ppermute | solution.py:27
  3.1 16.6 %collective-permute-start.11 = (bf16[64,3584]{1,0:T(8,128)(2,1)}, bf16[64,3584]{1,0:T(8,128)(2,1)S(1)}, u32[]{:S(2)}, u32[]{:S(2)}) collective-permute-start(bf16[64,3584]{1,0:T(8,128)(2,1)} %bitcast.3), channel_id=1, source_target_pairs={{0,2},{1,3},{2,0},{3,1},{4,6},{5,7},{6,4},{7,5},{8,10},{9,11},{10,... | collective-permute-start | bytes 1376264 | tf_op jit(solution)/shard_map/ppermute | solution.py:27
  3.2 5.1 %collective-permute-start = (bf16[64,1024]{1,0:T(8,128)(2,1)}, bf16[64,1024]{1,0:T(8,128)(2,1)S(1)}, u32[]{:S(2)}, u32[]{:S(2)}) collective-permute-start(bf16[64,1024]{1,0:T(8,128)(2,1)} %bitcast.6), channel_id=1, source_target_pairs={{0,1},{1,0},{2,3},{3,2},{4,5},{5,4},{6,7},{7,6},{8,9},{9,8},{10,11... | collective-permute-start | bytes 393224 | tf_op jit(solution)/shard_map/ppermute | solution.py:27
  3.3 2.0 %copy-start = (bf16[128,14336]{1,0:T(8,128)(2,1)S(1)}, bf16[128,14336]{1,0:T(8,128)(2,1)}, u32[]{:S(2)}) copy-start(bf16[128,14336]{1,0:T(8,128)(2,1)} %refs_1_.3) | copy-start | bytes 11010052
  5.3 1.0 %copy-start.2 = (bf16[3584,64]{0,1:T(8,128)(2,1)S(1)}, bf16[3584,64]{0,1:T(8,128)(2,1)}, u32[]{:S(2)}) copy-start(bf16[3584,64]{0,1:T(8,128)(2,1)} %param.12) | copy-start | bytes 1376260
  6.3 2.7 %copy-start.6 = (bf16[128,4096]{1,0:T(8,128)(2,1)S(1)}, bf16[128,4096]{1,0:T(8,128)(2,1)}, u32[]{:S(2)}) copy-start(bf16[128,4096]{1,0:T(8,128)(2,1)} %refs_4_.1) | copy-start | bytes 3145732
  6.3 2.7 %copy-start.7 = (bf16[1024,64]{0,1:T(8,128)(2,1)S(1)}, bf16[1024,64]{0,1:T(8,128)(2,1)}, u32[]{:S(2)}) copy-start(bf16[1024,64]{0,1:T(8,128)(2,1)} %param.13) | copy-start | bytes 393220
  7.1 12.7 %copy-start.1 = (bf16[128,14336]{1,0:T(8,128)(2,1)S(1)}, bf16[128,14336]{1,0:T(8,128)(2,1)}, u32[]{:S(2)}) copy-start(bf16[128,14336]{1,0:T(8,128)(2,1)} %refs_1_.3) | copy-start | bytes 11010052
  7.7 1.3 %collective-permute-start.3 = (bf16[64,1024]{1,0:T(8,128)(2,1)S(1)}, bf16[64,1024]{1,0:T(8,128)(2,1)S(1)}, u32[]{:S(2)}, u32[]{:S(2)}) collective-permute-start(bf16[64,1024]{1,0:T(8,128)(2,1)S(1)} %collective-permute-done.1.refs_2_), channel_id=1, source_target_pairs={{0,1},{1,0},{2,3},{3,2},{4,5},{5,4},{6,7},{7,6},{8,9},{9,8},{10,11... | collective-permute-start | bytes 393224 | tf_op jit(solution)/shard_map/ppermute | solution.py:27
  9.5 4.7 %collective-permute-start.4 = (bf16[64,128]{1,0:T(8,128)(2,1)S(1)}, bf16[64,128]{1,0:T(8,128)(2,1)S(1)}, u32[]{:S(2)}, u32[]{:S(2)}) collective-permute-start(bf16[64,128]{1,0:T(8,128)(2,1)S(1)} %shard_map.75), channel_id=1, source_target_pairs={{0,8},{4,12},{8,0},{12,4},{16,24},{20,28},{24,16},{28,20},{1,9},{5... | collective-permute-start | bytes 49160 | tf_op jit(solution)/shard_map/ppermute | solution.py:27
  11.6 4.6 %collective-permute-start.5 = (bf16[64,128]{1,0:T(8,128)(2,1)S(1)}, bf16[64,128]{1,0:T(8,128)(2,1)S(1)}, u32[]{:S(2)}, u32[]{:S(2)}) collective-permute-start(bf16[64,128]{1,0:T(8,128)(2,1)S(1)} %shard_map.75), channel_id=1, source_target_pairs={{0,16},{4,20},{8,24},{12,28},{16,0},{20,4},{24,8},{28,12},{1,17},{... | collective-permute-start | bytes 49160 | tf_op jit(solution)/shard_map/ppermute | solution.py:27
  14.2 5.5 %collective-permute-start.6 = (bf16[64,128]{1,0:T(8,128)(2,1)S(1)}, bf16[64,128]{1,0:T(8,128)(2,1)S(1)}, u32[]{:S(2)}, u32[]{:S(2)}) collective-permute-start(bf16[64,128]{1,0:T(8,128)(2,1)S(1)} %shard_map.75), channel_id=1, source_target_pairs={{0,24},{4,28},{8,16},{12,20},{16,8},{20,12},{24,0},{28,4},{1,25},{... | collective-permute-start | bytes 49160 | tf_op jit(solution)/shard_map/ppermute | solution.py:27
  19.7 2.1 %collective-permute-start.12 = (bf16[64,3584]{1,0:T(8,128)(2,1)S(1)}, bf16[64,3584]{1,0:T(8,128)(2,1)S(1)}, u32[]{:S(2)}, u32[]{:S(2)}) collective-permute-start(bf16[64,3584]{1,0:T(8,128)(2,1)S(1)} %collective-permute-done.11.refs_0_), channel_id=1, source_target_pairs={{0,1},{1,0},{2,3},{3,2},{4,5},{5,4},{6,7},{7,6},{8,9},{9,8},{10,11... | collective-permute-start | bytes 1376264 | tf_op jit(solution)/shard_map/ppermute | solution.py:27
  20.3 6.0 %collective-permute-start.7 = (bf16[256,128]{1,0:T(8,128)(2,1)S(1)}, bf16[256,128]{1,0:T(8,128)(2,1)S(1)}, u32[]{:S(2)}, u32[]{:S(2)}) collective-permute-start(bf16[256,128]{1,0:T(8,128)(2,1)S(1)} %pad_maximum_fusion), channel_id=1, source_target_pairs={{0,4},{4,0},{8,12},{12,8},{16,20},{20,16},{24,28},{28,24},{1,5},{5... | collective-permute-start | bytes 196616 | tf_op jit(solution)/shard_map/ppermute | solution.py:27
  23.0 12.1 %all-to-all-start = ((bf16[32,24,128]{2,1,0:T(8,128)(2,1)}), bf16[32,24,128]{2,1,0:T(8,128)(2,1)S(1)}, u32[]{:S(2)}, u32[]{:S(2)}) async-start(bf16[32,24,128]{2,1,0:T(8,128)(2,1)} %shard_map.77), calls=%async_computation | async-start | bytes 393216 | tf_op jit(solution)/shard_map/all_to_all | solution.py:200
  26.3 7.4 %collective-permute-start.9 = (bf16[512,128]{1,0:T(8,128)(2,1)S(1)}, bf16[512,128]{1,0:T(8,128)(2,1)S(1)}, u32[]{:S(2)}, u32[]{:S(2)}) collective-permute-start(bf16[512,128]{1,0:T(8,128)(2,1)S(1)} %constant_dynamic-update-slice_fusion.refs_0_), channel_id=1, source_target_pairs={{0,2},{1,3},{2,0},{3,1},{4,6},{5,7},{6,4},{7,5},{8,10},{9,11},{10,... | collective-permute-start | bytes 393224 | tf_op jit(solution)/shard_map/ppermute | solution.py:27
  28.2 5.6 %collective-permute-start.8 = (bf16[512,128]{1,0:T(8,128)(2,1)S(1)}, bf16[512,128]{1,0:T(8,128)(2,1)S(1)}, u32[]{:S(2)}, u32[]{:S(2)}) collective-permute-start(bf16[512,128]{1,0:T(8,128)(2,1)S(1)} %constant_dynamic-update-slice_fusion.refs_0_), channel_id=1, source_target_pairs={{0,1},{1,0},{2,3},{3,2},{4,5},{5,4},{6,7},{7,6},{8,9},{9,8},{10,11... | collective-permute-start | bytes 393224 | tf_op jit(solution)/shard_map/ppermute | solution.py:27
  33.7 1.3 %collective-permute-start.10 = (bf16[512,128]{1,0:T(8,128)(2,1)S(1)}, bf16[512,128]{1,0:T(8,128)(2,1)S(1)}, u32[]{:S(2)}, u32[]{:S(2)}) collective-permute-start(bf16[512,128]{1,0:T(8,128)(2,1)S(1)} %collective-permute-done.9.refs_2_), channel_id=1, source_target_pairs={{0,1},{1,0},{2,3},{3,2},{4,5},{5,4},{6,7},{7,6},{8,9},{9,8},{10,11... | collective-permute-start | bytes 393224 | tf_op jit(solution)/shard_map/ppermute | solution.py:27

commit v8 on v7

--- a/solution.py
+++ b/solution.py
@@ -60,12 +60,6 @@
 
 def near_kernel(which, *refs):
     refs[-1][...] = low_rank(refs[: len(which)], which, refs[-2])
-
-
-def project_kernel(which, *refs):
-    count = len(which)
-    tokens, total, out = refs[count:]
-    out[...] = low_rank(refs[:count], which, tokens) + total[...]
 
 
 def keys_kernel(owned, piece_of, owner_dp, owner_slot, _, out):
@@ -188,13 +182,9 @@
     half = order[: len(order) // 2]
     errors = jnp.concatenate([errors] + [swap(errors, "dp", k) for k in half[1:]], axis=0)
     far_in = spread(after(far_in, errors), low)
-    for k in range(top - 1):
-        inputs = call(
-            functools.partial(project_kernel, [top + k]), [far_in[k], hidden_in, inputs], square
-        )
     messages = call(
-        functools.partial(message_kernel, [2 * top - 1], mine, lead),
-        [far_in[-1], hidden_in, inputs, keys],
+        functools.partial(message_kernel, list(range(top, 2 * top)), mine, lead),
+        [*far_in, hidden_in, inputs, keys],
         jax.ShapeDtypeStruct((count_dp * count_fsdp, mine + tile, token_rows), BF16),
     )
     messages = lax.all_to_all(messages, ("fsdp", "dp"), split_axis=0, concat_axis=0, tiled=True)

time: 37.8 us -> 38.1 us (level)
    pallas_call x6 -> x5, Pallas kernels: 5.83 us -> 5.72 us  [call(): pl.pallas_call(kernel, out_shape=outputs, in_specs=specs or [VMEM] * len(...]
  transfers between devices with their start and end apart: 14 -> 14, of which waited for: 6 -> 7; matrix products, arithmetic and copies ran while one was open for 0% -> 0% of each run, Pallas kernels for 9% -> 9%
where the time goes in v8:
time: 38.1 us; the launch traced here: 37.9 us
  starting transfers between devices  15 us (39%)
  waiting for transfers between devices  13.9 us (36%)
  Pallas kernels  5.72 us (15%)
  local copies, waits for them, and re-layouts  3.12 us (8%)
    ppermute x13, waiting for transfers between devices, swap(): return lax.ppermute(value, axis, [(i, i ^ bit) for i in range(count)])  13.9 us
    ppermute x13, starting transfers between devices, swap(): return lax.ppermute(value, axis, [(i, i ^ bit) for i in range(count)])  11.5 us
    pallas_call x5, Pallas kernels, call(): pl.pallas_call(kernel, out_shape=outputs, in_specs=specs or [VMEM] * len(...  5.72 us
    all_to_all x1, starting transfers between devices, by_tokens(): lax.all_to_all(messages, ('fsdp', 'dp'), split_axis=0, concat_axis=0, til...  3.54 us
    unnamed x20, local copies, waits for them, and re-layouts  3.11 us
  transfers between devices with their start and end apart: 14, of which 7 were waited for; matrix products, arithmetic and copies ran while one was open for 0% of the time, Pallas kernels for 9%

profile of v8, /device:TPU:0, one launch (start us, length us, event | category | flops | bytes accessed | tf_op | source)
XLA Modules:
  0.0 37.9 jit_solution(3497089200108953961)
XLA Ops:
  0.0 0.0 copy-start.4
  0.0 0.0 copy-start.5
  0.0 0.0 copy-start.3
  0.0 0.5 %collective-permute-start.2 = (bf16[64,3584]{1,0:T(8,128)(2,1)}, bf16[64,3584]{1,0:T(8,128)(2,1)S(1)}, u32[]{:S(2)}, u32[]{:S(2)}) collective-permute-start(bf16[64,3584]{1,0:T(8,128)(2,1)} %bitcast.2), channel_id=1, source_target_pairs={{0,1},{1,0},{2,3},{3,2},{4,5},{5,4},{6,7},{7,6},{8,9},{9,8},{10,11... | collective-permute-start | bytes 1376264 | tf_op jit(solution)/shard_map/ppermute | solution.py:27
  0.5 2.6 %collective-permute-start.1 = (bf16[64,1024]{1,0:T(8,128)(2,1)}, bf16[64,1024]{1,0:T(8,128)(2,1)S(1)}, u32[]{:S(2)}, u32[]{:S(2)}) collective-permute-start(bf16[64,1024]{1,0:T(8,128)(2,1)} %bitcast.5), channel_id=1, source_target_pairs={{0,2},{1,3},{2,0},{3,1},{4,6},{5,7},{6,4},{7,5},{8,10},{9,11},{10,... | collective-permute-start | bytes 393224 | tf_op jit(solution)/shard_map/ppermute | solution.py:27
  3.1 0.1 collective-permute-start.11
  3.2 0.1 collective-permute-start
  3.3 0.0 collective-permute-done.2.refs_1_
  3.3 0.0 copy-start
  3.3 2.0 %copy-done = bf16[128,14336]{1,0:T(8,128)(2,1)S(1)} copy-done((bf16[128,14336]{1,0:T(8,128)(2,1)S(1)}, bf16[128,14336]{1,0:T(8,128)(2,1)}, u32[]{:S(2)}) %copy-start) | copy-done | bytes 3670040
  5.3 0.0 copy-start.2
  5.3 1.0 %copy-done.2 = bf16[3584,64]{0,1:T(8,128)(2,1)S(1)} copy-done((bf16[3584,64]{0,1:T(8,128)(2,1)S(1)}, bf16[3584,64]{0,1:T(8,128)(2,1)}, u32[]{:S(2)}) %copy-start.2) | copy-done | bytes 458776
  6.3 0.0 copy-start.6
  6.3 0.0 copy-start.7
  6.3 0.7 %shard_map.73._.refs_5_.refs_3_ = f32[64,128]{1,0:T(8,128)S(1)} custom-call(bf16[64,3584]{1,0:T(8,128)(2,1)S(1)} %bitcast.4, bf16[64,3584]{1,0:T(8,128)(2,1)S(1)} %collective-permute-done.2.refs_1_, bf16[128,14336]{1,0:T(8,128)(2,1)S(1)} %copy-done), custom_call_target="tpu_custom_call" | custom-call | tf_op jit(solution)/shard_map/pallas_call | solution.py:85
  7.1 0.0 copy-start.1
  7.1 0.5 %collective-permute-done.1.refs_2_ = bf16[64,1024]{1,0:T(8,128)(2,1)S(1)} collective-permute-done((bf16[64,1024]{1,0:T(8,128)(2,1)}, bf16[64,1024]{1,0:T(8,128)(2,1)S(1)}, u32[]{:S(2)}, u32[]{:S(2)}) %collective-permute-start.1) | collective-permute-done | bytes 131104 | tf_op jit(solution)/shard_map/ppermute | solution.py:27
  7.7 0.0 collective-permute-start.3
  7.7 0.0 copy-done.4
  7.7 0.0 copy-done.5
  7.7 0.0 copy-done.3
  7.7 0.6 %shard_map.74.refs_6_.refs_4_ = bf16[16,128]{1,0:T(8,128)(2,1)S(1)} custom-call(s32[1,128]{1,0:T(1,128)S(1)} %copy-done.3, s32[1,8]{1,0:T(1,128)S(1)} %copy-done.4, s32[1,8]{1,0:T(1,128)S(1)} %copy-done.5, f32[64,128]{1,0:T(8,128)S(1)} %shard_map.73._.refs_5_.refs_3_), custom_call_target="tpu_custom_call" | custom-call | tf_op jit(solution)/shard_map/pallas_call | solution.py:85
  8.2 0.0 collective-permute-done.refs_1_
  8.2 0.8 %collective-permute-done.3.refs_3_ = bf16[64,1024]{1,0:T(8,128)(2,1)S(1)} collective-permute-done((bf16[64,1024]{1,0:T(8,128)(2,1)S(1)}, bf16[64,1024]{1,0:T(8,128)(2,1)S(1)}, u32[]{:S(2)}, u32[]{:S(2)}) %collective-permute-start.3) | collective-permute-done | bytes 131104 | tf_op jit(solution)/shard_map/ppermute | solution.py:27
  9.0 0.0 copy-done.6
  9.0 0.0 copy-done.7
  9.0 0.5 %shard_map.75 = bf16[64,128]{1,0:T(8,128)(2,1)S(1)} custom-call(bf16[64,1024]{1,0:T(8,128)(2,1)S(1)} %bitcast.7, bf16[64,1024]{1,0:T(8,128)(2,1)S(1)} %collective-permute-done.refs_1_, bf16[64,1024]{1,0:T(8,128)(2,1)S(1)} %collective-permute-done.1.refs_2_, bf16[64,1024]{1,0:T(8,128)(2,1)S(1)} %collective-permute-done.3.refs_3_, ...), custom_call_target="tpu_custom_call" | custom-call | flops 1500000000 | bytes 1000000 | tf_op jit(solution)/shard_map/pallas_call | solution.py:85
  9.5 2.1 %collective-permute-start.4 = (bf16[64,128]{1,0:T(8,128)(2,1)S(1)}, bf16[64,128]{1,0:T(8,128)(2,1)S(1)}, u32[]{:S(2)}, u32[]{:S(2)}) collective-permute-start(bf16[64,128]{1,0:T(8,128)(2,1)S(1)} %shard_map.75), channel_id=1, source_target_pairs={{0,8},{4,12},{8,0},{12,4},{16,24},{20,28},{24,16},{28,20},{1,9},{5... | collective-permute-start | bytes 49160 | tf_op jit(solution)/shard_map/ppermute | solution.py:27
  11.6 2.6 %collective-permute-start.5 = (bf16[64,128]{1,0:T(8,128)(2,1)S(1)}, bf16[64,128]{1,0:T(8,128)(2,1)S(1)}, u32[]{:S(2)}, u32[]{:S(2)}) collective-permute-start(bf16[64,128]{1,0:T(8,128)(2,1)S(1)} %shard_map.75), channel_id=1, source_target_pairs={{0,16},{4,20},{8,24},{12,28},{16,0},{20,4},{24,8},{28,12},{1,17},{... | collective-permute-start | bytes 49160 | tf_op jit(solution)/shard_map/ppermute | solution.py:27
  14.2 0.0 collective-permute-start.6
  14.2 0.0 collective-permute-done.4
  14.2 2.0 %collective-permute-done.5 = bf16[64,128]{1,0:T(8,128)(2,1)S(1)} collective-permute-done((bf16[64,128]{1,0:T(8,128)(2,1)S(1)}, bf16[64,128]{1,0:T(8,128)(2,1)S(1)}, u32[]{:S(2)}, u32[]{:S(2)}) %collective-permute-start.5) | collective-permute-done | bytes 16416 | tf_op jit(solution)/shard_map/ppermute | solution.py:27
  16.2 3.5 %collective-permute-done.6 = bf16[64,128]{1,0:T(8,128)(2,1)S(1)} collective-permute-done((bf16[64,128]{1,0:T(8,128)(2,1)S(1)}, bf16[64,128]{1,0:T(8,128)(2,1)S(1)}, u32[]{:S(2)}, u32[]{:S(2)}) %collective-permute-start.6) | collective-permute-done | bytes 16416 | tf_op jit(solution)/shard_map/ppermute | solution.py:27
  19.7 0.0 collective-permute-done.11.refs_0_
  19.7 0.1 collective-permute-start.12
  19.8 1.6 %collective-permute-start.7 = (bf16[256,128]{1,0:T(8,128)(2,1)S(1)}, bf16[256,128]{1,0:T(8,128)(2,1)S(1)}, u32[]{:S(2)}, u32[]{:S(2)}) collective-permute-start(bf16[256,128]{1,0:T(8,128)(2,1)S(1)} %pad_maximum_fusion), channel_id=1, source_target_pairs={{0,4},{4,0},{8,12},{12,8},{16,20},{20,16},{24,28},{28,24},{1,5},{5... | collective-permute-start | bytes 196616 | tf_op jit(solution)/shard_map/ppermute | solution.py:27
  21.4 0.2 collective-permute-done.12.refs_1_
  21.6 0.0 copy-done.1
  21.6 1.4 %shard_map.76 = bf16[32,24,128]{2,1,0:T(8,128)(2,1)} custom-call(bf16[64,3584]{1,0:T(8,128)(2,1)S(1)} %collective-permute-done.11.refs_0_, bf16[64,3584]{1,0:T(8,128)(2,1)S(1)} %collective-permute-done.12.refs_1_, bf16[128,14336]{1,0:T(8,128)(2,1)S(1)} %copy-done.1, f32[64,128]{1,0:T(8,128)S(1)} %shard_map.73._.refs_5_.refs_3_, ...), custom_call_target="tpu_custom_call" | custom-call | tf_op jit(solution)/shard_map/pallas_call | solution.py:85
  23.1 3.5 %all-to-all-start = ((bf16[32,24,128]{2,1,0:T(8,128)(2,1)}), bf16[32,24,128]{2,1,0:T(8,128)(2,1)S(1)}, u32[]{:S(2)}, u32[]{:S(2)}) async-start(bf16[32,24,128]{2,1,0:T(8,128)(2,1)} %shard_map.76), calls=%async_computation | async-start | bytes 393216 | tf_op jit(solution)/shard_map/all_to_all | solution.py:190
  26.6 0.0 collective-permute-done.7
  26.7 1.8 %collective-permute-start.9 = (bf16[512,128]{1,0:T(8,128)(2,1)S(1)}, bf16[512,128]{1,0:T(8,128)(2,1)S(1)}, u32[]{:S(2)}, u32[]{:S(2)}) collective-permute-start(bf16[512,128]{1,0:T(8,128)(2,1)S(1)} %constant_dynamic-update-slice_fusion.refs_0_), channel_id=1, source_target_pairs={{0,2},{1,3},{2,0},{3,1},{4,6},{5,7},{6,4},{7,5},{8,10},{9,11},{10,... | collective-permute-start | bytes 393224 | tf_op jit(solution)/shard_map/ppermute | solution.py:27
  28.5 0.0 collective-permute-start.8
  28.5 5.6 %collective-permute-done.9.refs_2_ = bf16[512,128]{1,0:T(8,128)(2,1)S(1)} collective-permute-done((bf16[512,128]{1,0:T(8,128)(2,1)S(1)}, bf16[512,128]{1,0:T(8,128)(2,1)S(1)}, u32[]{:S(2)}, u32[]{:S(2)}) %collective-permute-start.9) | collective-permute-done | bytes 131104 | tf_op jit(solution)/shard_map/ppermute | solution.py:27
  34.1 0.0 collective-permute-start.10
  34.1 0.0 collective-permute-done.8.refs_1_
  34.1 1.3 %collective-permute-done.10.refs_3_ = bf16[512,128]{1,0:T(8,128)(2,1)S(1)} collective-permute-done((bf16[512,128]{1,0:T(8,128)(2,1)S(1)}, bf16[512,128]{1,0:T(8,128)(2,1)S(1)}, u32[]{:S(2)}, u32[]{:S(2)}) %collective-permute-start.10) | collective-permute-done | bytes 131104 | tf_op jit(solution)/shard_map/ppermute | solution.py:27
  35.4 0.0 all-to-all-done.refs_4_
  35.4 2.5 %shard_map.77 = f32[24,1024]{1,0:T(8,128)} custom-call(bf16[512,128]{1,0:T(8,128)(2,1)S(1)} %constant_dynamic-update-slice_fusion.refs_0_, bf16[512,128]{1,0:T(8,128)(2,1)S(1)} %collective-permute-done.8.refs_1_, bf16[512,128]{1,0:T(8,128)(2,1)S(1)} %collective-permute-done.9.refs_2_, bf16[512,128]{1,0:T(8,128)(2,1)S(1)} %collective-permute-done.10.refs_3_, ...), custom_call_target="tpu_custom_call" | custom-call | tf_op jit(solution)/shard_map/pallas_call | solution.py:85
  (6 shorter events, 0.0 us)
Async XLA Ops:
  0.0 7.7 %copy-start.4 = (s32[1,8]{1,0:T(1,128)S(1)}, s32[1,8]{1,0:T(1,128)}, u32[]{:S(2)}) copy-start(s32[1,8]{1,0:T(1,128)} %owner_dp.1) | copy-start | bytes 100
  0.0 7.7 %copy-start.5 = (s32[1,8]{1,0:T(1,128)S(1)}, s32[1,8]{1,0:T(1,128)}, u32[]{:S(2)}) copy-start(s32[1,8]{1,0:T(1,128)} %owner_slot.1) | copy-start | bytes 100
  0.0 7.7 %copy-start.3 = (s32[1,128]{1,0:T(1,128)S(1)}, s32[1,128]{1,0:T(1,128)}, u32[]{:S(2)}) copy-start(s32[1,128]{1,0:T(1,128)} %piece_of.1) | copy-start | bytes 1540
  0.0 3.3 %collective-permute-start.2 = (bf16[64,3584]{1,0:T(8,128)(2,1)}, bf16[64,3584]{1,0:T(8,128)(2,1)S(1)}, u32[]{:S(2)}, u32[]{:S(2)}) collective-permute-start(bf16[64,3584]{1,0:T(8,128)(2,1)} %bitcast.2), channel_id=1, source_target_pairs={{0,1},{1,0},{2,3},{3,2},{4,5},{5,4},{6,7},{7,6},{8,9},{9,8},{10,11... | collective-permute-start | bytes 1376264 | tf_op jit(solution)/shard_map/ppermute | solution.py:27
  0.5 7.1 %collective-permute-start.1 = (bf16[64,1024]{1,0:T(8,128)(2,1)}, bf16[64,1024]{1,0:T(8,128)(2,1)S(1)}, u32[]{:S(2)}, u32[]{:S(2)}) collective-permute-start(bf16[64,1024]{1,0:T(8,128)(2,1)} %bitcast.5), channel_id=1, source_target_pairs={{0,2},{1,3},{2,0},{3,1},{4,6},{5,7},{6,4},{7,5},{8,10},{9,11},{10,... | collective-permute-start | bytes 393224 | tf_op jit(solution)/shard_map/ppermute | solution.py:27
  3.1 16.6 %collective-permute-start.11 = (bf16[64,3584]{1,0:T(8,128)(2,1)}, bf16[64,3584]{1,0:T(8,128)(2,1)S(1)}, u32[]{:S(2)}, u32[]{:S(2)}) collective-permute-start(bf16[64,3584]{1,0:T(8,128)(2,1)} %bitcast.3), channel_id=1, source_target_pairs={{0,2},{1,3},{2,0},{3,1},{4,6},{5,7},{6,4},{7,5},{8,10},{9,11},{10,... | collective-permute-start | bytes 1376264 | tf_op jit(solution)/shard_map/ppermute | solution.py:27
  3.2 5.1 %collective-permute-start = (bf16[64,1024]{1,0:T(8,128)(2,1)}, bf16[64,1024]{1,0:T(8,128)(2,1)S(1)}, u32[]{:S(2)}, u32[]{:S(2)}) collective-permute-start(bf16[64,1024]{1,0:T(8,128)(2,1)} %bitcast.6), channel_id=1, source_target_pairs={{0,1},{1,0},{2,3},{3,2},{4,5},{5,4},{6,7},{7,6},{8,9},{9,8},{10,11... | collective-permute-start | bytes 393224 | tf_op jit(solution)/shard_map/ppermute | solution.py:27
  3.3 2.0 %copy-start = (bf16[128,14336]{1,0:T(8,128)(2,1)S(1)}, bf16[128,14336]{1,0:T(8,128)(2,1)}, u32[]{:S(2)}) copy-start(bf16[128,14336]{1,0:T(8,128)(2,1)} %refs_2_.3) | copy-start | bytes 11010052
  5.3 1.0 %copy-start.2 = (bf16[3584,64]{0,1:T(8,128)(2,1)S(1)}, bf16[3584,64]{0,1:T(8,128)(2,1)}, u32[]{:S(2)}) copy-start(bf16[3584,64]{0,1:T(8,128)(2,1)} %param.12) | copy-start | bytes 1376260
  6.3 2.7 %copy-start.6 = (bf16[128,4096]{1,0:T(8,128)(2,1)S(1)}, bf16[128,4096]{1,0:T(8,128)(2,1)}, u32[]{:S(2)}) copy-start(bf16[128,4096]{1,0:T(8,128)(2,1)} %refs_4_.1) | copy-start | bytes 3145732
  6.3 2.7 %copy-start.7 = (bf16[1024,64]{0,1:T(8,128)(2,1)S(1)}, bf16[1024,64]{0,1:T(8,128)(2,1)}, u32[]{:S(2)}) copy-start(bf16[1024,64]{0,1:T(8,128)(2,1)} %param.13) | copy-start | bytes 393220
  7.1 14.5 %copy-start.1 = (bf16[128,14336]{1,0:T(8,128)(2,1)S(1)}, bf16[128,14336]{1,0:T(8,128)(2,1)}, u32[]{:S(2)}) copy-start(bf16[128,14336]{1,0:T(8,128)(2,1)} %refs_2_.3) | copy-start | bytes 11010052
  7.7 1.3 %collective-permute-start.3 = (bf16[64,1024]{1,0:T(8,128)(2,1)S(1)}, bf16[64,1024]{1,0:T(8,128)(2,1)S(1)}, u32[]{:S(2)}, u32[]{:S(2)}) collective-permute-start(bf16[64,1024]{1,0:T(8,128)(2,1)S(1)} %collective-permute-done.1.refs_2_), channel_id=1, source_target_pairs={{0,1},{1,0},{2,3},{3,2},{4,5},{5,4},{6,7},{7,6},{8,9},{9,8},{10,11... | collective-permute-start | bytes 393224 | tf_op jit(solution)/shard_map/ppermute | solution.py:27
  9.5 4.7 %collective-permute-start.4 = (bf16[64,128]{1,0:T(8,128)(2,1)S(1)}, bf16[64,128]{1,0:T(8,128)(2,1)S(1)}, u32[]{:S(2)}, u32[]{:S(2)}) collective-permute-start(bf16[64,128]{1,0:T(8,128)(2,1)S(1)} %shard_map.75), channel_id=1, source_target_pairs={{0,8},{4,12},{8,0},{12,4},{16,24},{20,28},{24,16},{28,20},{1,9},{5... | collective-permute-start | bytes 49160 | tf_op jit(solution)/shard_map/ppermute | solution.py:27
  11.6 4.6 %collective-permute-start.5 = (bf16[64,128]{1,0:T(8,128)(2,1)S(1)}, bf16[64,128]{1,0:T(8,128)(2,1)S(1)}, u32[]{:S(2)}, u32[]{:S(2)}) collective-permute-start(bf16[64,128]{1,0:T(8,128)(2,1)S(1)} %shard_map.75), channel_id=1, source_target_pairs={{0,16},{4,20},{8,24},{12,28},{16,0},{20,4},{24,8},{28,12},{1,17},{... | collective-permute-start | bytes 49160 | tf_op jit(solution)/shard_map/ppermute | solution.py:27
  14.2 5.5 %collective-permute-start.6 = (bf16[64,128]{1,0:T(8,128)(2,1)S(1)}, bf16[64,128]{1,0:T(8,128)(2,1)S(1)}, u32[]{:S(2)}, u32[]{:S(2)}) collective-permute-start(bf16[64,128]{1,0:T(8,128)(2,1)S(1)} %shard_map.75), channel_id=1, source_target_pairs={{0,24},{4,28},{8,16},{12,20},{16,8},{20,12},{24,0},{28,4},{1,25},{... | collective-permute-start | bytes 49160 | tf_op jit(solution)/shard_map/ppermute | solution.py:27
  19.7 1.9 %collective-permute-start.12 = (bf16[64,3584]{1,0:T(8,128)(2,1)S(1)}, bf16[64,3584]{1,0:T(8,128)(2,1)S(1)}, u32[]{:S(2)}, u32[]{:S(2)}) collective-permute-start(bf16[64,3584]{1,0:T(8,128)(2,1)S(1)} %collective-permute-done.11.refs_0_), channel_id=1, source_target_pairs={{0,1},{1,0},{2,3},{3,2},{4,5},{5,4},{6,7},{7,6},{8,9},{9,8},{10,11... | collective-permute-start | bytes 1376264 | tf_op jit(solution)/shard_map/ppermute | solution.py:27
  19.8 6.8 %collective-permute-start.7 = (bf16[256,128]{1,0:T(8,128)(2,1)S(1)}, bf16[256,128]{1,0:T(8,128)(2,1)S(1)}, u32[]{:S(2)}, u32[]{:S(2)}) collective-permute-start(bf16[256,128]{1,0:T(8,128)(2,1)S(1)} %pad_maximum_fusion), channel_id=1, source_target_pairs={{0,4},{4,0},{8,12},{12,8},{16,20},{20,16},{24,28},{28,24},{1,5},{5... | collective-permute-start | bytes 196616 | tf_op jit(solution)/shard_map/ppermute | solution.py:27
  23.1 12.4 %all-to-all-start = ((bf16[32,24,128]{2,1,0:T(8,128)(2,1)}), bf16[32,24,128]{2,1,0:T(8,128)(2,1)S(1)}, u32[]{:S(2)}, u32[]{:S(2)}) async-start(bf16[32,24,128]{2,1,0:T(8,128)(2,1)} %shard_map.76), calls=%async_computation | async-start | bytes 393216 | tf_op jit(solution)/shard_map/all_to_all | solution.py:190
  26.7 7.4 %collective-permute-start.9 = (bf16[512,128]{1,0:T(8,128)(2,1)S(1)}, bf16[512,128]{1,0:T(8,128)(2,1)S(1)}, u32[]{:S(2)}, u32[]{:S(2)}) collective-permute-start(bf16[512,128]{1,0:T(8,128)(2,1)S(1)} %constant_dynamic-update-slice_fusion.refs_0_), channel_id=1, source_target_pairs={{0,2},{1,3},{2,0},{3,1},{4,6},{5,7},{6,4},{7,5},{8,10},{9,11},{10,... | collective-permute-start | bytes 393224 | tf_op jit(solution)/shard_map/ppermute | solution.py:27
  28.5 5.6 %collective-permute-start.8 = (bf16[512,128]{1,0:T(8,128)(2,1)S(1)}, bf16[512,128]{1,0:T(8,128)(2,1)S(1)}, u32[]{:S(2)}, u32[]{:S(2)}) collective-permute-start(bf16[512,128]{1,0:T(8,128)(2,1)S(1)} %constant_dynamic-update-slice_fusion.refs_0_), channel_id=1, source_target_pairs={{0,1},{1,0},{2,3},{3,2},{4,5},{5,4},{6,7},{7,6},{8,9},{9,8},{10,11... | collective-permute-start | bytes 393224 | tf_op jit(solution)/shard_map/ppermute | solution.py:27
  34.1 1.3 %collective-permute-start.10 = (bf16[512,128]{1,0:T(8,128)(2,1)S(1)}, bf16[512,128]{1,0:T(8,128)(2,1)S(1)}, u32[]{:S(2)}, u32[]{:S(2)}) collective-permute-start(bf16[512,128]{1,0:T(8,128)(2,1)S(1)} %collective-permute-done.9.refs_2_), channel_id=1, source_target_pairs={{0,1},{1,0},{2,3},{3,2},{4,5},{5,4},{6,7},{7,6},{8,9},{9,8},{10,11... | collective-permute-start | bytes 393224 | tf_op jit(solution)/shard_map/ppermute | solution.py:27
